TPU v7x, 32 devices: a whole 2x2x4 slice. The times are simulated.
32 devices in a mesh: dp: 4 (over y, core), expert: 8 (over z, x).
Axes of the slice: x: 2, y: 2, z: 4, core: 2. Of those that a mesh axis runs over, the one named last changes fastest.
Arguments:
- tokens: bfloat16 [4096, 2560], P(('dp', 'expert')), may hold values from -6 to 6
- cotangent: bfloat16 [4096, 2560], P(('dp', 'expert')), may hold values from -6 to 6
- routes: int32 [4096, 1], P(('dp', 'expert')), may hold values from 0 to 7; in each aligned block of 128 rows (0 to 127, 128 to 255, ...) at most 24 rows name the same one
- gates: float32 [4096, 1], P(('dp', 'expert')), may hold values from 0.25 to 1
- hot_index: int32 [512], P(('dp', 'expert')), may hold values from 0 to 127, as said below
- hot_gate: float32 [512], P(('dp', 'expert')), may hold values from 0.25 to 1
- w_gate_up: bfloat16 [8, 2560, 1536], P('expert', 'dp'), may hold values from -0.125 to 0.125
- w_down: bfloat16 [8, 768, 2560], P('expert', 'dp'), may hold values from -0.21875 to 0.21875
- w_hot_gu: bfloat16 [2, 768, 2560], P(None, 'dp', 'expert'), may hold values from -0.125 to 0.125
- w_hot_dn: bfloat16 [768, 2560], P('dp', 'expert'), may hold values from -0.21875 to 0.21875
Outputs:
- layer_out: bfloat16 [4096, 2560], P(('dp', 'expert'))
- input_grad: bfloat16 [4096, 2560], P(('dp', 'expert'))
- grad_gate_up: bfloat16 [8, 2560, 1536], P('expert', 'dp')
- grad_down: bfloat16 [8, 768, 2560], P('expert', 'dp')
- grad_hot_gu: bfloat16 [2, 768, 2560], P(None, 'dp', 'expert')
- grad_hot_dn: bfloat16 [768, 2560], P('dp', 'expert')
Inputs may be any that keep to these rules, and one draw needn't show every extreme that they name: `routes`: each token names 1 different routed experts; the tokens of one device name any one routed expert at most 24 times, some expert exactly 24 times. `hot_index`: the 16 entries of one device name different tokens of that device, by their index within the device.
All inputs are finite; a program needn't handle non-finite values.
Results may differ from a plain program's by a relative error of at most 0.018.
Values may be sent and summed in bfloat16 or wider, within the bound.
No kernel may reach another device: no remote copies, remote signals or barrier semaphores. Data moves between devices by JAX's collectives and lax.ppermute only.
A program may use at most 128 MiB of HBM per device.

v0:
```python
import jax
import jax.numpy as jnp
from jax import lax
from jax.experimental import pallas as pl
from jax.experimental.pallas import tpu as pltpu
from jax.sharding import PartitionSpec as P

BF = jnp.bfloat16
F32 = jnp.float32
NN = (((1,), (0,)), ((), ()))
NT = (((1,), (1,)), ((), ()))
TN = (((0,), (0,)), ((), ()))
ROOM = 56 * 1024 * 1024
LIGHT = pl.CostEstimate(flops=1, bytes_accessed=1, transcendentals=0)
SMEM = pl.BlockSpec(memory_space=pltpu.SMEM)
ANYWHERE = pl.BlockSpec(memory_space=pl.ANY)
INSIDE = pl.BlockSpec(memory_space=pltpu.VMEM)
PIECES = 8


def mm(a, b, dims=NN):
    return lax.dot_general(a, b, dims, preferred_element_type=F32)


def after(value, *earlier):
    return lax.optimization_barrier((value,) + earlier)[0]


def params():
    return pltpu.CompilerParams(vmem_limit_bytes=ROOM)


LIGHT = pl.CostEstimate(flops=1, bytes_accessed=1, transcendentals=0)


def struct(*shape, dtype=BF):
    return jax.ShapeDtypeStruct(shape, dtype)


def whole(array):
    return pl.BlockSpec(array.shape, lambda *_: (0,) * len(array.shape))


def stack_rows(refs, scratch):
    rows = refs[0].shape[0]
    for i, ref in enumerate(refs):
        scratch[i * rows : (i + 1) * rows, :] = ref[...]


def fetch(order_ref, blocks, w_ref, sems):
    deep = blocks[0].shape[0]
    copies = []
    for j, block in enumerate(blocks):
        place = pl.multiple_of(order_ref[j] * deep, deep)
        copies.append(pltpu.make_async_copy(block, w_ref.at[pl.ds(place, deep)], sems.at[j]))
        copies[-1].start()
    return copies


def down_scratch(blocks):
    deep, width = blocks[0].shape
    return [pltpu.VMEM((len(blocks) * deep, width), BF), pltpu.SemaphoreType.DMA((len(blocks),))]


def fetch_each(blocks, w_ref, sems):
    copies = []
    for j, block in enumerate(blocks):
        copies.append(pltpu.make_async_copy(block, w_ref.at[j], sems.at[j]))
        copies[-1].start()
    return copies


def each_scratch(blocks):
    return [
        pltpu.VMEM((len(blocks),) + blocks[0].shape, BF),
        pltpu.SemaphoreType.DMA((len(blocks),)),
    ]


def expert(order, received, w_gu, w_down):
    rows = received.shape[0]
    depth, width = w_gu[0].shape
    deep, wide = w_down[0].shape
    half = width // 2
    m = len(w_gu)
    step = 512 if wide % 512 == 0 else wide

    def body(order_ref, in_ref, *refs):
        gu_in, dn_in, rest = refs[:m], refs[m : 2 * m], refs[2 * m :]
        back_ref, hid_ref, d_ref, acc, gu_ref, gu_sems, dn_ref, dn_sems = rest
        gu_copies = fetch_each(gu_in, gu_ref, gu_sems)
        dn_copies = fetch(order_ref, dn_in, dn_ref, dn_sems)
        for j, copy in enumerate(gu_copies):
            copy.wait()
            found = mm(in_ref[:, wide + j * depth : wide + (j + 1) * depth], gu_ref[j])
            if j == 0:
                acc[...] = found
            else:
                acc[...] += found
        g = acc[:, :half]
        u = acc[:, half:]
        s = jax.nn.sigmoid(g)
        hid_ref[...] = (g * s * u).astype(BF)
        for copy in dn_copies:
            copy.wait()
        d_hidden = mm(in_ref[:, :wide], dn_ref[...], NT)
        d_ref[:, :half] = (d_hidden * u * s * (1.0 + g * (1.0 - s))).astype(BF)
        d_ref[:, half:] = (d_hidden * g * s).astype(BF)
        for j in range(m):
            at = wide + j * depth
            back_ref[:, at : at + depth] = mm(d_ref[...], gu_ref[j], NT).astype(BF)
        for c in range(0, wide, step):
            back_ref[:, c : c + step] = mm(hid_ref[...], dn_ref[:, c : c + step]).astype(BF)

    return pl.pallas_call(
        body,
        in_specs=[SMEM, INSIDE] + [ANYWHERE] * (2 * m),
        out_specs=[INSIDE] * 3,
        out_shape=[struct(rows, 2 * wide), struct(rows, half), struct(rows, width)],
        scratch_shapes=[pltpu.VMEM((rows, width), F32)]
        + each_scratch(w_gu)
        + down_scratch(w_down),
        compiler_params=params(),
        cost_estimate=LIGHT,
        name="expert",
    )(order, received, *w_gu, *w_down)


def gate_up_grads(xs, ds, k, wide, scale, received):
    n, rows, width = len(xs), xs[0].shape[0], ds[0].shape[1]
    step = 512 if width % 512 == 0 else width
    extra = [] if received is None else [received]
    if wide % 128 != 0:
        xs, k = [x[:, k * wide : (k + 1) * wide] for x in xs], 0

    def body(*refs):
        x_refs, d_refs, rest = refs[:n], refs[n : 2 * n], refs[2 * n :]
        out_ref, x_scr, d_scr = rest[-3:]

        @pl.when(pl.program_id(0) == 0)
        def _():
            stack_rows(x_refs, x_scr)

        stack_rows(d_refs, d_scr)
        found = mm(x_scr[...], d_scr[...], TN) * scale
        if extra:
            found = found + rest[0][...].astype(F32)
        out_ref[...] = found.astype(BF)

    shape = struct(wide, width)
    column = lambda i: (0, i)
    return pl.pallas_call(
        body,
        grid=(width // step,),
        in_specs=[pl.BlockSpec((rows, wide), lambda i: (0, k))] * n
        + [pl.BlockSpec((rows, step), column)] * n
        + [pl.BlockSpec((wide, step), column)] * len(extra),
        out_specs=pl.BlockSpec((wide, step), column),
        out_shape=shape,
        scratch_shapes=[pltpu.VMEM((n * rows, wide), BF), pltpu.VMEM((n * rows, step), BF)],
        compiler_params=params(),
        cost_estimate=LIGHT,
        name="gate_up_grads",
    )(*xs, *ds, *extra)


def down_grads(order, hidden, rows_s, wide, count, scale):
    rows, half = hidden.shape
    deep = half // count
    step = 512 if wide % 512 == 0 else wide

    def body(order_ref, h_ref, s_ref, *refs):
        outs, scratch = refs[:count], refs[count]
        scratch[...] = mm(h_ref[...], s_ref[...], TN) * scale
        for j in range(count):
            place = pl.multiple_of(order_ref[j] * deep, deep)
            outs[j][...] = scratch[pl.ds(place, deep), :].astype(BF)

    shapes = [struct(deep, wide)] * count
    return pl.pallas_call(
        body,
        grid=(wide // step,),
        in_specs=[SMEM, whole(hidden), pl.BlockSpec((rows, step), lambda i: (0, i))],
        out_specs=[pl.BlockSpec((deep, step), lambda i: (0, i))] * count,
        out_shape=shapes,
        scratch_shapes=[pltpu.VMEM((half, step), F32)],
        compiler_params=params(),
        cost_estimate=LIGHT,
        name="down_grads",
    )(order, hidden, rows_s)


def popular_partials(select, packed, weights, hid):
    parts, count = select.shape[:2]
    narrow = packed.shape[1] // (2 * parts)
    columns = sum(w.shape[0] for w in weights)

    def body(sel_ref, in_ref, *refs):
        w_refs, (x_ref, s_ref, p_ref) = refs[: len(weights)], refs[len(weights) :]
        x = None
        s = None
        for q in range(parts):
            rows = mm(sel_ref[q], in_ref[...])
            one = rows[:, q * narrow : (q + 1) * narrow]
            two = rows[:, (parts + q) * narrow : (parts + q + 1) * narrow]
            x = one if x is None else x + one
            s = two if s is None else s + two
        x = x.astype(BF)
        s = s.astype(BF)
        x_ref[...] = x
        s_ref[...] = s
        at = 0
        for w_ref in w_refs:
            for top in range(0, w_ref.shape[0], 3 * hid):
                p_ref[:, at : at + 2 * hid] = mm(x, w_ref[top : top + 2 * hid, :], NT).astype(BF)
                p_ref[:, at + 2 * hid : at + 3 * hid] = mm(
                    s, w_ref[top + 2 * hid : top + 3 * hid, :], NT
                ).astype(BF)
                at += 3 * hid

    return pl.pallas_call(
        body,
        in_specs=[INSIDE] * (2 + len(weights)),
        out_specs=[INSIDE] * 3,
        out_shape=[
            struct(count, narrow),
            struct(count, narrow),
            struct(count, columns),
        ],
        compiler_params=params(),
        cost_estimate=LIGHT,
        name="popular_partials",
    )(select, packed, *weights)


def popular_middle(own, others, hid):
    rows, columns = own.shape

    def body(own_ref, *refs):
        parts, out_ref = refs[:-1], refs[-1]
        act = own_ref[...].astype(F32)
        for part in parts:
            act = act + part[...].astype(F32)
        for at in range(0, columns, 3 * hid):
            g = act[:, at : at + hid]
            u = act[:, at + hid : at + 2 * hid]
            dh = act[:, at + 2 * hid : at + 3 * hid]
            s = jax.nn.sigmoid(g)
            out_ref[:, at : at + hid] = (dh * u * s * (1.0 + g * (1.0 - s))).astype(BF)
            out_ref[:, at + hid : at + 2 * hid] = (dh * g * s).astype(BF)
            out_ref[:, at + 2 * hid : at + 3 * hid] = (g * s * u).astype(BF)

    return pl.pallas_call(
        body,
        in_specs=[INSIDE] * (1 + len(others)),
        out_specs=INSIDE,
        out_shape=struct(rows, columns),
        compiler_params=params(),
        cost_estimate=LIGHT,
        name="popular_middle",
    )(own, *others)


def popular_back(select, lines, x, s, weights, hid, scale):
    parts, count, spots = select.shape
    narrow = x.shape[1]
    m = len(weights)
    n = len(lines)
    columns = lines[0].shape[1]

    def body(sel_ref, x_ref, s_ref, *refs):
        ins, w_refs, back_ref = refs[:n], refs[n : n + m], refs[n + m]
        grads, mid_ref = refs[n + m + 1 : -1], refs[-1]
        stack_rows(ins, mid_ref)
        grad = None
        out = None
        at = 0
        for w_ref, g_ref in zip(w_refs, grads):
            for top in range(0, w_ref.shape[0], 3 * hid):
                d_gate = mid_ref[:, at : at + hid]
                d_up = mid_ref[:, at + hid : at + 2 * hid]
                hidden = mid_ref[:, at + 2 * hid : at + 3 * hid]
                sides = ((d_gate, x_ref), (d_up, x_ref), (hidden, s_ref))
                for i, (left, right) in enumerate(sides):
                    here = slice(top + i * hid, top + (i + 1) * hid)
                    product = mm(left, w_ref[here, :])
                    if i == 2:
                        out = product if out is None else out + product
                    else:
                        grad = product if grad is None else grad + product
                    g_ref[here, :] = (mm(left, right[...], TN) * scale).astype(BF)
                at += 3 * hid
        grad = grad.astype(BF)
        out = out.astype(BF)
        for q in range(parts):
            back_ref[:, q * narrow : (q + 1) * narrow] = mm(sel_ref[q], grad, TN).astype(BF)
            back_ref[:, (parts + q) * narrow : (parts + q + 1) * narrow] = mm(
                sel_ref[q], out, TN
            ).astype(BF)

    return pl.pallas_call(
        body,
        in_specs=[INSIDE] * (3 + n + m),
        out_specs=[INSIDE] * (1 + m),
        out_shape=[struct(spots, 2 * parts * narrow)]
        + [struct(w.shape[0], narrow) for w in weights],
        scratch_shapes=[pltpu.VMEM((count, columns), BF)],
        compiler_params=params(),
        cost_estimate=LIGHT,
        name="popular_back",
    )(select, x, s, *lines, *weights)


def slot_positions(route_block, count):
    flat = route_block.reshape(-1)
    onehot = (flat[:, None] == jnp.arange(count, dtype=jnp.int32)[None, :]).astype(jnp.int32)
    before = jnp.cumsum(onehot, axis=0) - onehot
    return (flat, jnp.sum(before * onehot, axis=1))


def exchange(blocks):
    return lax.all_to_all(blocks, "expert", split_axis=0, concat_axis=0, tiled=True)


def local(
    tokens, cotangent, routes, gates, hot_index, hot_gate, w_gate_up, w_down, w_hot_gu, w_hot_dn
):
    owners = lax.axis_size("expert")
    groups = lax.axis_size("dp")
    cores = 2 if groups % 2 == 0 else 1
    chips = groups // cores
    tok_dev, width_d = tokens.shape
    topk = routes.shape[1]
    slots = max(2, 3 * tok_dev * topk // (2 * owners))
    entries = tok_dev * topk
    rows = owners * slots
    inverse = 1.0 / (4 * groups)
    me = lax.axis_index("dp")
    chip, core = me // cores, me % cores

    def shift(value, r):
        pairs = [
            (i, ((i // cores + r) % chips) * cores + i % cores) for i in range(groups)
        ]
        return lax.ppermute(value, "dp", pairs)

    def swap(value):
        pairs = [(i, (i // cores) * cores + (i + 1) % cores) for i in range(groups)]
        return lax.ppermute(value, "dp", pairs)

    order = jnp.stack(
        [
            ((chip - r) % chips) * cores + (core + k) % cores
            for k in range(cores)
            for r in range(chips)
        ]
    ).astype(jnp.int32)

    across = 1
    while 2 * (2 * across) ** 2 <= owners:
        across *= 2
    depths = owners // across
    spot = lax.axis_index("expert")

    def hop(value, j):
        return lax.ppermute(value, "expert", [(i, i ^ j) for i in range(owners)])

    wide = width_d // groups
    hid = w_hot_dn.shape[0]
    narrow = width_d // owners
    hot_w = jnp.concatenate([w_hot_gu, w_hot_dn[None]], axis=0).reshape(3 * hid, narrow)
    hot_near = [hot_w] + [shift(hot_w, r) for r in range(1, chips)]
    down_own = after(w_down[0], hot_near[-1])
    gu_near = [w_gate_up[0]] + [shift(w_gate_up[0], r) for r in range(1, chips)]
    down_near = [w_down[0]] + [shift(down_own, r) for r in range(1, chips)]
    gu_far = [swap(w_gate_up[0])] if cores == 2 else []
    down_far = [swap(w_down[0])] if cores == 2 else []

    flat, pos = slot_positions(routes, owners)
    dest = flat * slots + pos
    slot_ids = jnp.arange(rows, dtype=jnp.int32)[:, None]
    pick = (slot_ids == dest[None, :]).astype(BF)

    def as_rows(value, width):
        value = value.reshape(owners, -1)
        spare = -value.shape[1] % width
        return jnp.pad(value, ((0, 0), (0, spare))).reshape(owners, -1, width)

    hot_dev = hot_index.shape[0]
    few = 2 * hot_dev // PIECES
    hot_pick = (
        hot_index[:, None] == jnp.arange(tok_dev, dtype=jnp.int32)[None, :]
    ).astype(BF)
    hot_x = mm(hot_pick, tokens).astype(BF)
    hot_s = (hot_gate[:, None] * mm(hot_pick, cotangent)).astype(BF)
    hot_send = jnp.concatenate([hot_x, hot_s], axis=0).reshape(PIECES, few, owners, narrow)
    hot_send = hot_send.transpose(2, 1, 0, 3).reshape(owners * few, PIECES * narrow)
    packed_id = jnp.arange(owners * few, dtype=jnp.int32)
    turn = ((packed_id ^ (spot * few))[:, None] == packed_id[None, :]).astype(BF)
    row = jnp.arange(owners * hot_dev, dtype=jnp.int32)
    step = row // hot_dev
    source = spot ^ ((step % depths) * across + step // depths)
    piece = (row % hot_dev) // few

    def selection(index):
        hit = (index * few + row % few)[:, None] == packed_id[None, :]
        return jnp.stack([hit & (piece == q)[:, None] for q in range(PIECES // 2)]).astype(BF)

    scaled = (gates[:, :, None] * cotangent[:, None, :].astype(F32)).astype(BF)
    tok_rel = jnp.concatenate(
        [
            lax.dynamic_slice_in_dim(tokens, order[j] * wide, wide, 1)
            for j in range(groups)
        ],
        axis=1,
    )
    tok_rel = jnp.repeat(tok_rel, topk, axis=0) if topk > 1 else tok_rel
    both = jnp.concatenate([scaled.reshape(entries, width_d), tok_rel], axis=1)
    both = mm(pick, both).astype(BF).reshape(owners, slots, 2 * width_d)
    load = 2 * hot_dev * narrow
    extra = -(-load // (slots * 512)) * 512
    hot_send = jnp.pad(hot_send.reshape(owners, load), ((0, 0), (0, slots * extra - load)))
    send = jnp.concatenate([both, hot_send.reshape(owners, slots, extra)], axis=2)
    received = exchange(send)
    hot_recv = received[:, :, 2 * width_d :].reshape(owners, slots * extra)[:, :load]
    hot_recv = hot_recv.reshape(owners * few, PIECES * narrow)
    received = received.reshape(rows, 2 * width_d + extra)

    hot_near = jnp.concatenate(list(after(tuple(hot_near), send, *gu_far, *down_far)), axis=0)
    hot_ws = [hot_near] + ([swap(hot_near)] if cores == 2 else [])
    hot_x, hot_s, partial = popular_partials(selection(source), hot_recv, hot_ws, hid)
    share = depths * hot_dev
    level_in = [hop(partial[j * share : (j + 1) * share], j) for j in range(1, across)]
    if cores == 2:
        gu_far = gu_far + [swap(block) for block in gu_near[1:]]
        down_far = down_far + [swap(block) for block in down_near[1:]]
    level = partial[:share].astype(F32)
    for value in level_in:
        level = level + value.astype(F32)
    level = level.astype(BF)
    level = [level[j * hot_dev : (j + 1) * hot_dev] for j in range(depths)]
    depth_in = [hop(level[j], j * across) for j in range(1, depths)]
    hot_own = popular_middle(level[0], depth_in, hid)
    line = [hot_own] + [hop(hot_own, j * across) for j in range(1, depths)]
    work = after(received, hot_own)
    back, hidden, d_act = expert(order, work, gu_near + gu_far, down_near + down_far)

    def columns_of(r):
        return jnp.concatenate(
            [
                received[:, width_d + (k * chips + r) * wide : width_d + (k * chips + r + 1) * wide]
                for k in range(cores)
            ],
            axis=1,
        )

    xs = [columns_of(0)] + [shift(columns_of(r), -r) for r in range(1, chips)]
    ds = [d_act] + [shift(d_act, -r) for r in range(1, chips)]
    back = after(back, xs[-1], *line[1:])
    back = exchange(back.reshape(owners, slots, 2 * width_d)).reshape(rows, 2 * width_d)

    line = jnp.concatenate(list(after(tuple(line), d_act)))
    lines = [line] + [hop(line, j) for j in range(1, across)]
    lines = list(after(tuple(lines), ds[-1]))
    hot_back, *hot_grads = popular_back(
        selection(step), lines, hot_x, hot_s, hot_ws, hid, inverse
    )

    dn_parts = down_grads(order, hidden, received, width_d, groups, inverse)
    dn_sum = list(dn_parts[:chips])
    if cores == 2:
        dn_in = [swap(part) for part in dn_parts[chips:]]
        dn_sum = [
            (one.astype(F32) + two.astype(F32)).astype(BF) for one, two in zip(dn_sum, dn_in)
        ]
    dn_total = dn_sum[0].astype(F32)
    dn_recv = [shift(dn_sum[r], -r) for r in range(1, chips)]
    for value in dn_recv:
        dn_total = dn_total + value.astype(F32)
    grad_dn = dn_total.astype(BF)

    hot_back = hot_back.reshape(across, depths, few, PIECES * narrow)
    hot_back = [hot_back[0]] + [hop(hot_back[j], j) for j in range(1, across)]
    hot_back = jnp.stack(hot_back, axis=1)
    hot_back = [hot_back[0]] + [hop(hot_back[j], j * across) for j in range(1, depths)]
    hot_back = jnp.concatenate(hot_back).reshape(owners * few, PIECES * narrow)
    hot_back = mm(turn, hot_back).astype(BF)

    xs_late = list(after(tuple(xs), d_act))
    gu_in = None
    if cores == 2:
        gu_in = swap(gate_up_grads(xs_late, ds, 1, wide, inverse, None))

    hot_sum = hot_grads[0]
    if cores == 2:
        hot_sum = (hot_sum.astype(F32) + swap(hot_grads[1]).astype(F32)).astype(BF)
    hot_sum = hot_sum.reshape(chips, 3 * hid, narrow)
    hot_total = hot_sum[0].astype(F32)
    hot_far = [shift(hot_sum[r], -r) for r in range(1, chips)]
    for value in hot_far:
        hot_total = hot_total + value.astype(F32)
    grad_hot = hot_total.astype(BF).reshape(3, hid, narrow)
    xs_last = list(after(tuple(xs_late), *hot_far, *dn_recv))
    grad_gu = gate_up_grads(xs_last, ds, 0, wide, inverse, gu_in)

    hot_back = hot_back.reshape(owners, few, PIECES, narrow)
    hot_back = hot_back.transpose(2, 1, 0, 3).reshape(2, hot_dev, width_d)
    landed = mm(pick, back, TN)
    picked = landed[:, :width_d]
    layer_out = (
        (gates.reshape(entries)[:, None] * picked).reshape(tok_dev, topk, width_d).sum(axis=1)
    )
    token_gate = jnp.sum(jnp.where(hot_pick > 0, hot_gate[:, None], 0.0), axis=0)
    layer_out = layer_out + token_gate[:, None] * mm(hot_pick, hot_back[1], TN)
    returned = landed[:, width_d:]
    returned = returned.reshape(tok_dev, topk, width_d).sum(axis=1)
    blocks = jnp.stack([returned[:, j * wide : (j + 1) * wide] for j in range(groups)])
    input_grad = jnp.concatenate(
        [
            lax.dynamic_index_in_dim(
                blocks,
                ((q - core) % cores) * chips + (chip - p) % chips,
                0,
                keepdims=False,
            )
            for p in range(chips)
            for q in range(cores)
        ],
        axis=1,
    )
    input_grad = input_grad + mm(hot_pick, hot_back[0], TN)
    return (
        layer_out.astype(BF),
        input_grad.astype(BF),
        grad_gu[None],
        grad_dn[None],
        grad_hot[:2],
        grad_hot[2],
    )


def solution(mesh):
    tok = P(("dp", "expert"), None)
    flat = P(("dp", "expert"))
    rows = P("expert", "dp", None)
    hot = (P(None, "dp", "expert"), P("dp", "expert"))
    return jax.shard_map(
        local,
        mesh=mesh,
        in_specs=(tok, tok, tok, tok, flat, flat, rows, rows) + hot,
        out_specs=(tok, tok, rows, rows) + hot,
        check_vma=False,
    )
```

profile of v0, /device:TPU:0, one launch (start us, length us, event | category | flops | bytes accessed | tf_op | source)
XLA Modules:
  0.0 258.9 jit_solution(10968094453481131844)
XLA Ops:
  0.8 0.8 fusion.7
  1.8 0.8 select_reduce_fusion
  2.6 0.7 multiply_add_fusion.2
  3.3 1.3 fusion.5
  5.8 0.7 convolution_convert_fusion
  6.5 1.5 pad_maximum_fusion
  8.0 7.4 %all-to-all-start = ((bf16[8,24,5632]{2,1,0:T(8,128)(2,1)}), bf16[8,24,5632]{2,1,0:T(8,128)(2,1)S(1)}, u32[]{:S(2)}, u32[]{:S(2)}) async-start(bf16[8,24,5632]{2,1,0:T(8,128)(2,1)} %pad_maximum_fusion), calls=%async_computation | async-start | bytes 4325376 | tf_op jit(solution)/shard_map/all_to_all | solution.py:322
  15.9 1.5 collective-permute-start.8
  17.4 1.0 pad_maximum_fusion.4
  19.0 51.4 %collective-permute-done = bf16[576,320]{1,0:T(8,128)(2,1)S(1)} collective-permute-done((bf16[576,320]{1,0:T(8,128)(2,1)S(1)}, bf16[576,320]{1,0:T(8,128)(2,1)S(1)}, u32[]{:S(2)}, u32[]{:S(2)}) %collective-permute-start) | collective-permute-done | bytes 368672 | tf_op jit(solution)/shard_map/ppermute | solution.py:345
  70.4 1.3 copy-done.7
  72.1 1.5 copy.53
  73.5 1.6 collective-permute-start.10
  75.2 0.8 copy.54.sel_ref
  76.2 2.2 copy.55.refs_1_.refs_3_
  78.5 1.1 reshape.563.in_ref
  79.6 3.7 %popular_partials.1 = (bf16[128,320]{1,0:T(8,128)(2,1)}, bf16[128,320]{1,0:T(8,128)(2,1)}, bf16[128,2304]{1,0:T(8,128)(2,1)}) custom-call(bf16[4,128,32]{2,1,0:T(8,128)(2,1)} %copy.54.sel_ref, bf16[32,2560]{1,0:T(8,128)(2,1)} %reshape.563.in_ref, bf16[1152,320]{1,0:T(8,128)(2,1)} %copy-done.1, bf16[1152,320]{1,0:T(8,128)(2,1)} %copy.55.refs_1_.refs_3_), custom_call_target="tpu_custom_call" | custom-call | flops 1 | bytes 1 | tf_op jit(solution)/shard_map/popular_partials/pallas_call | solution.py:221
  83.3 1.0 slice.105
  84.3 2.1 collective-permute-start.4
  86.4 0.8 copy.56.sel_ref
  87.1 11.0 %collective-permute-done.10.refs_5_ = bf16[192,2560]{1,0:T(8,128)(2,1)} collective-permute-done((bf16[192,2560]{1,0:T(8,128)(2,1)}, bf16[192,2560]{1,0:T(8,128)(2,1)}, u32[]{:S(2)}, u32[]{:S(2)}) %collective-permute-start.10) | collective-permute-done | bytes 983072 | tf_op jit(solution)/shard_map/ppermute | solution.py:345
  98.1 1.0 add_convert_fusion.5
  99.1 0.7 fusion.34
  99.8 2.0 collective-permute-start.5
  101.8 2.4 collective-permute-start.6
  104.7 6.1 %collective-permute-done.6.refs_1_ = bf16[16,2304]{1,0:T(8,128)(2,1)S(1)} collective-permute-done((bf16[16,2304]{1,0:T(8,128)(2,1)S(1)}, bf16[16,2304]{1,0:T(8,128)(2,1)S(1)}, u32[]{:S(2)}, u32[]{:S(2)}) %collective-permute-start.6) | collective-permute-done | bytes 73760 | tf_op jit(solution)/shard_map/ppermute | solution.py:366
  111.4 1.7 popular_middle.1
  113.2 1.6 collective-permute-start.13
  114.8 1.5 collective-permute-start.14
  116.3 1.3 collective-permute-start.15
  118.2 1.0 copy-done.13
  119.2 12.6 %expert.1 = (bf16[192,5120]{1,0:T(8,128)(2,1)}, bf16[192,768]{1,0:T(8,128)(2,1)}, bf16[192,1536]{1,0:T(8,128)(2,1)}) custom-call(s32[4]{0:T(128)} %pad_add_fusion.order_ref, bf16[192,5632]{1,0:T(8,128)(2,1)} %bitcast.73, bf16[640,1536]{1,0:T(8,128)(2,1)} %bitcast.80, bf16[640,1536]{1,0:T(8,128)(2,1)} %collective-permute-done.8.refs_1_, ...), custom_call_target="tpu_custom_call" | custom-call | flops 1 | bytes 1 | tf_op jit(solution)/shard_map/expert/pallas_call | solution.py:115
  131.8 1.6 collective-permute-start.17
  133.5 1.5 collective-permute-start.16
  135.0 1.4 fusion.33
  137.0 5.7 %down_grads.1 = (bf16[192,2560]{1,0:T(8,128)(2,1)}, bf16[192,2560]{1,0:T(8,128)(2,1)}, bf16[192,2560]{1,0:T(8,128)(2,1)}, bf16[192,2560]{1,0:T(8,128)(2,1)}) custom-call(s32[4]{0:T(128)} %pad_add_fusion.order_ref, bf16[192,768]{1,0:T(8,128)(2,1)} %get-tuple-element.55.h_ref, bf16[192,5632]{1,0:T(8,128)(2,1)} %bitcast.75), custom_call_target="tpu_custom_call" | custom-call | flops 1 | bytes 1 | tf_op jit(solution)/shard_map/down_grads/pallas_call | solution.py:180
  142.8 5.6 %collective-permute-done.17.refs_3_ = bf16[192,1536]{1,0:T(8,128)(2,1)S(1)} collective-permute-done((bf16[192,1536]{1,0:T(8,128)(2,1)}, bf16[192,1536]{1,0:T(8,128)(2,1)S(1)}, u32[]{:S(2)}, u32[]{:S(2)}) %collective-permute-start.17) | collective-permute-done | bytes 589856 | tf_op jit(solution)/shard_map/ppermute | solution.py:345
  148.3 4.0 %popular_back.1 = (bf16[32,2560]{1,0:T(8,128)(2,1)}, bf16[1152,320]{1,0:T(8,128)(2,1)}, bf16[1152,320]{1,0:T(8,128)(2,1)}) custom-call(bf16[4,128,32]{2,1,0:T(8,128)(2,1)} %copy.56.sel_ref, bf16[128,320]{1,0:T(8,128)(2,1)} %get-tuple-element.41.x_ref, bf16[128,320]{1,0:T(8,128)(2,1)} %get-tuple-element.42.s_ref, bf16[64,2304]{1,0:T(8,128)(2,1)} %copy-done.14, ...), custom_call_target="tpu_custom_call" | custom-call | flops 1 | bytes 1 | tf_op jit(solution)/shard_map/popular_back/pallas_call | solution.py:301
  152.4 0.9 fusion.36
  153.3 1.5 collective-permute-start.18
  154.9 1.5 collective-permute-done.12.refs_1_
  156.4 0.8 copy-done.8
  157.2 4.4 %all-to-all-start.1 = ((bf16[8,24,5120]{2,1,0:T(8,128)(2,1)}), bf16[8,24,5120]{2,1,0:T(8,128)(2,1)S(1)}, u32[]{:S(2)}, u32[]{:S(2)}) async-start(bf16[8,24,5120]{2,1,0:T(8,128)(2,1)} %bitcast.81), calls=%async_computation.1 | async-start | bytes 3932160 | tf_op jit(solution)/shard_map/all_to_all | solution.py:322
  161.8 2.1 collective-permute-start.19
  163.9 2.4 collective-permute-start.20
  166.3 0.8 pad_maximum_fusion.3.refs_0_
  167.2 4.5 %gate_up_grads.2 = bf16[640,1536]{1,0:T(8,128)(2,1)} custom-call(bf16[192,1280]{1,0:T(8,128)(2,1)} %pad_maximum_fusion.3.refs_0_, bf16[192,1280]{1,0:T(8,128)(2,1)} %copy-done.8, bf16[192,1536]{1,0:T(8,128)(2,1)} %get-tuple-element.43.refs_2_, bf16[192,1536]{1,0:T(8,128)(2,1)} %copy-done.6), custom_call_target="tpu_custom_call" | custom-call | flops 1 | bytes 1 | tf_op jit(solution)/shard_map/gate_up_grads/pallas_call | solution.py:152
  171.7 2.3 copy.62
  173.9 18.9 %collective-permute-done.19 = bf16[2,4,2560]{2,1,0:T(4,128)(2,1)S(1)} collective-permute-done((bf16[2,4,2560]{2,1,0:T(4,128)(2,1)S(1)}, bf16[2,4,2560]{2,1,0:T(4,128)(2,1)S(1)}, u32[]{:S(2)}, u32[]{:S(2)}) %collective-permute-start.19) | collective-permute-done | bytes 40992 | tf_op jit(solution)/shard_map/ppermute | solution.py:366
  192.8 15.0 %collective-permute-done.20 = bf16[2,4,2560]{2,1,0:T(4,128)(2,1)S(1)} collective-permute-done((bf16[2,4,2560]{2,1,0:T(4,128)(2,1)S(1)}, bf16[2,4,2560]{2,1,0:T(4,128)(2,1)S(1)}, u32[]{:S(2)}, u32[]{:S(2)}) %collective-permute-start.20) | collective-permute-done | bytes 40992 | tf_op jit(solution)/shard_map/ppermute | solution.py:366
  208.0 2.4 add_convert_fusion.2
  210.4 1.5 collective-permute-start.25
  211.9 1.7 copy.63
  213.6 1.4 add_convert_fusion.3
  215.1 0.9 copy-done.2
  216.0 0.8 slice.155
  218.1 26.3 %collective-permute-done.23 = bf16[576,320]{1,0:T(8,128)(2,1)} collective-permute-done((bf16[576,320]{1,0:T(8,128)(2,1)}, bf16[576,320]{1,0:T(8,128)(2,1)}, u32[]{:S(2)}, u32[]{:S(2)}) %collective-permute-start.23) | collective-permute-done | bytes 368672 | tf_op jit(solution)/shard_map/ppermute | solution.py:345
  244.3 1.1 add_convert_fusion.4
  245.5 0.7 slice.157
  246.2 0.7 slice.158
  246.9 2.9 %fusion.4 = bf16[1,192,2560]{2,1,0:T(8,128)(2,1)} fusion(bf16[192,2560]{1,0:T(8,128)(2,1)} %collective-permute-done.25, bf16[192,2560]{1,0:T(8,128)(2,1)} %collective-permute-done.27, bf16[192,2560]{1,0:T(8,128)(2,1)S(1)} %copy-done.10), kind=kLoop, calls=%fused_computation.18 | loop fusion | flops 3932160 | bytes 3932160 | tf_op jit(solution)/shard_map/broadcast_in_dim | solution.py:536
  249.8 5.1 %gate_up_grads.3 = bf16[640,1536]{1,0:T(8,128)(2,1)} custom-call(bf16[192,1280]{1,0:T(8,128)(2,1)} %pad_maximum_fusion.3.refs_0_, bf16[192,1280]{1,0:T(8,128)(2,1)} %copy-done.8, bf16[192,1536]{1,0:T(8,128)(2,1)} %get-tuple-element.43.refs_2_, bf16[192,1536]{1,0:T(8,128)(2,1)} %copy-done.6, bf16[640,1536]{1,0:T(8,128)(2,1)} %collective-permute-done.26.refs_4_), custom_call_target="tpu_custom_call" | custom-call | flops 1 | bytes 1 | tf_op jit(solution)/shard_map/gate_up_grads/pallas_call | solution.py:152
  256.1 1.3 fusion.2
  257.6 1.3 fusion.1
  (127 shorter events, 8.8 us)
Async XLA Ops:
  0.6 4.2 %copy-start.5 = (bf16[128,2560]{1,0:T(8,128)(2,1)S(1)}, bf16[128,2560]{1,0:T(8,128)(2,1)}, u32[]{:S(2)}) copy-start(bf16[128,2560]{1,0:T(8,128)(2,1)} %param.11) | copy-start | bytes 1966084
  0.6 3.9 %copy-start.4 = (bf16[128,2560]{1,0:T(8,128)(2,1)S(1)}, bf16[128,2560]{1,0:T(8,128)(2,1)}, u32[]{:S(2)}) copy-start(bf16[128,2560]{1,0:T(8,128)(2,1)} %param.10) | copy-start | bytes 1966084
  0.7 3.9 %copy-start.21 = (s32[16]{0:T(128)S(1)}, s32[16]{0:T(128)}, u32[]{:S(2)}) copy-start(s32[16]{0:T(128)} %param.14) | copy-start | bytes 196
  0.7 4.1 %copy-start.23 = (f32[16]{0:T(128)S(1)}, f32[16]{0:T(128)}, u32[]{:S(2)}) copy-start(f32[16]{0:T(128)} %param.15) | copy-start | bytes 196
  8.0 7.4 %copy-start.11 = (bf16[1,192,2560]{2,1,0:T(8,128)(2,1)S(1)}, bf16[1,192,2560]{2,1,0:T(8,128)(2,1)}, u32[]{:S(2)}) copy-start(bf16[1,192,2560]{2,1,0:T(8,128)(2,1)} %param.17) | copy-start | bytes 2949124
  8.0 9.4 %copy-start.15 = (bf16[2,192,320]{2,1,0:T(8,128)(2,1)S(1)}, bf16[2,192,320]{2,1,0:T(8,128)(2,1)}, u32[]{:S(2)}) copy-start(bf16[2,192,320]{2,1,0:T(8,128)(2,1)} %param.18) | copy-start | bytes 737284
  8.0 70.4 %all-to-all-start = ((bf16[8,24,5632]{2,1,0:T(8,128)(2,1)}), bf16[8,24,5632]{2,1,0:T(8,128)(2,1)S(1)}, u32[]{:S(2)}, u32[]{:S(2)}) async-start(bf16[8,24,5632]{2,1,0:T(8,128)(2,1)} %pad_maximum_fusion), calls=%async_computation | async-start | bytes 4325376 | tf_op jit(solution)/shard_map/all_to_all | solution.py:322
  15.4 55.0 %collective-permute-start.1 = (bf16[640,1536]{1,0:T(8,128)(2,1)}, bf16[640,1536]{1,0:T(8,128)(2,1)S(1)}, u32[]{:S(2)}, u32[]{:S(2)}) collective-permute-start(bf16[640,1536]{1,0:T(8,128)(2,1)} %bitcast.78), channel_id=1, source_target_pairs={{0,8},{8,0},{16,24},{24,16},{1,9},{9,1},{17,25},{25,17},{2,10},{10... | collective-permute-start | bytes 5898248 | tf_op jit(solution)/shard_map/ppermute | solution.py:349
  15.4 55.0 %collective-permute-start.2 = (bf16[192,2560]{1,0:T(8,128)(2,1)S(1)}, bf16[192,2560]{1,0:T(8,128)(2,1)S(1)}, u32[]{:S(2)}, u32[]{:S(2)}) collective-permute-start(bf16[192,2560]{1,0:T(8,128)(2,1)S(1)} %bitcast.87), channel_id=1, source_target_pairs={{0,8},{8,0},{16,24},{24,16},{1,9},{9,1},{17,25},{25,17},{2,10},{10... | collective-permute-start | bytes 2949128 | tf_op jit(solution)/shard_map/ppermute | solution.py:349
  15.9 60.1 %collective-permute-start.8 = (bf16[640,1536]{1,0:T(8,128)(2,1)}, bf16[640,1536]{1,0:T(8,128)(2,1)}, u32[]{:S(2)}, u32[]{:S(2)}) collective-permute-start(bf16[640,1536]{1,0:T(8,128)(2,1)} %bitcast.79), channel_id=1, source_target_pairs={{0,16},{8,24},{16,0},{24,8},{1,17},{9,25},{17,1},{25,9},{2,18},{10... | collective-permute-start | bytes 5898248 | tf_op jit(solution)/shard_map/ppermute | solution.py:345
  18.4 52.0 %collective-permute-start = (bf16[576,320]{1,0:T(8,128)(2,1)S(1)}, bf16[576,320]{1,0:T(8,128)(2,1)S(1)}, u32[]{:S(2)}, u32[]{:S(2)}) collective-permute-start(bf16[576,320]{1,0:T(8,128)(2,1)S(1)} %bitcast.83), channel_id=1, source_target_pairs={{0,16},{8,24},{16,0},{24,8},{1,17},{9,25},{17,1},{25,9},{2,18},{10... | collective-permute-start | bytes 1105928 | tf_op jit(solution)/shard_map/ppermute | solution.py:345
  70.4 1.6 copy-start.12
  70.4 1.3 copy-start.7
  72.1 6.3 %copy-start.1 = (bf16[1152,320]{1,0:T(8,128)(2,1)}, bf16[1152,320]{1,0:T(8,128)(2,1)S(1)}, u32[]{:S(2)}) copy-start(bf16[1152,320]{1,0:T(8,128)(2,1)S(1)} %constant_dynamic-update-slice_fusion.refs_0_.refs_2_) | copy-start | bytes 2211844
  73.5 2.7 %collective-permute-start.3 = (bf16[1152,320]{0,1:T(8,128)(2,1)}, bf16[1152,320]{0,1:T(8,128)(2,1)}, u32[]{:S(2)}, u32[]{:S(2)}) collective-permute-start(bf16[1152,320]{0,1:T(8,128)(2,1)} %copy.53), channel_id=1, source_target_pairs={{0,8},{8,0},{16,24},{24,16},{1,9},{9,1},{17,25},{25,17},{2,10},{10... | collective-permute-start | bytes 2211848 | tf_op jit(solution)/shard_map/ppermute | solution.py:349
  73.5 24.5 %collective-permute-start.10 = (bf16[192,2560]{1,0:T(8,128)(2,1)}, bf16[192,2560]{1,0:T(8,128)(2,1)}, u32[]{:S(2)}, u32[]{:S(2)}) collective-permute-start(bf16[192,2560]{1,0:T(8,128)(2,1)} %bitcast.85), channel_id=1, source_target_pairs={{0,16},{8,24},{16,0},{24,8},{1,17},{9,25},{17,1},{25,9},{2,18},{10... | collective-permute-start | bytes 2949128 | tf_op jit(solution)/shard_map/ppermute | solution.py:345
  76.0 42.2 %collective-permute-start.9 = (bf16[640,1536]{1,0:T(8,128)(2,1)}, bf16[640,1536]{1,0:T(8,128)(2,1)}, u32[]{:S(2)}, u32[]{:S(2)}) collective-permute-start(bf16[640,1536]{1,0:T(8,128)(2,1)} %collective-permute-done.8.refs_1_), channel_id=1, source_target_pairs={{0,8},{8,0},{16,24},{24,16},{1,9},{9,1},{17,25},{25,17},{2,10},{10... | collective-permute-start | bytes 5898248 | tf_op jit(solution)/shard_map/ppermute | solution.py:349
  78.4 4.9 %copy-start = (bf16[8,24,5632]{2,1,0:T(8,128)(2,1)}, bf16[8,24,5632]{2,1,0:T(8,128)(2,1)S(1)}, u32[]{:S(2)}) copy-start(bf16[8,24,5632]{2,1,0:T(8,128)(2,1)S(1)} %all-to-all-done) | copy-start | bytes 6488068
  84.3 13.8 %collective-permute-start.4 = (bf16[64,2304]{1,0:T(8,128)(2,1)S(1)}, bf16[64,2304]{1,0:T(8,128)(2,1)S(1)}, u32[]{:S(2)}, u32[]{:S(2)}) collective-permute-start(bf16[64,2304]{1,0:T(8,128)(2,1)S(1)} %slice.105), channel_id=1, source_target_pairs={{0,1},{1,0},{2,3},{3,2},{4,5},{5,4},{6,7},{7,6},{8,9},{9,8},{10,11... | collective-permute-start | bytes 884744 | tf_op jit(solution)/shard_map/ppermute | solution.py:366
  98.1 20.1 %collective-permute-start.11 = (bf16[192,2560]{1,0:T(8,128)(2,1)}, bf16[192,2560]{1,0:T(8,128)(2,1)S(1)}, u32[]{:S(2)}, u32[]{:S(2)}) collective-permute-start(bf16[192,2560]{1,0:T(8,128)(2,1)} %collective-permute-done.10.refs_5_), channel_id=1, source_target_pairs={{0,8},{8,0},{16,24},{24,16},{1,9},{9,1},{17,25},{25,17},{2,10},{10... | collective-permute-start | bytes 2949128 | tf_op jit(solution)/shard_map/ppermute | solution.py:349
  99.8 4.9 %collective-permute-start.5 = (bf16[16,2304]{1,0:T(8,128)(2,1)S(1)}, bf16[16,2304]{1,0:T(8,128)(2,1)S(1)}, u32[]{:S(2)}, u32[]{:S(2)}) collective-permute-start(bf16[16,2304]{1,0:T(8,128)(2,1)S(1)} %get-tuple-element.76), channel_id=1, source_target_pairs={{0,2},{1,3},{2,0},{3,1},{4,6},{5,7},{6,4},{7,5},{8,10},{9,11},{10,... | collective-permute-start | bytes 221192 | tf_op jit(solution)/shard_map/ppermute | solution.py:366
  101.8 9.0 %collective-permute-start.6 = (bf16[16,2304]{1,0:T(8,128)(2,1)S(1)}, bf16[16,2304]{1,0:T(8,128)(2,1)S(1)}, u32[]{:S(2)}, u32[]{:S(2)}) collective-permute-start(bf16[16,2304]{1,0:T(8,128)(2,1)S(1)} %get-tuple-element.75), channel_id=1, source_target_pairs={{0,4},{1,5},{2,6},{3,7},{4,0},{5,1},{6,2},{7,3},{8,12},{9,13},{10,... | collective-permute-start | bytes 221192 | tf_op jit(solution)/shard_map/ppermute | solution.py:366
  104.2 6.6 %collective-permute-start.7 = (bf16[16,2304]{1,0:T(8,128)(2,1)S(1)}, bf16[16,2304]{1,0:T(8,128)(2,1)S(1)}, u32[]{:S(2)}, u32[]{:S(2)}) collective-permute-start(bf16[16,2304]{1,0:T(8,128)(2,1)S(1)} %get-tuple-element.74), channel_id=1, source_target_pairs={{0,6},{1,7},{2,4},{3,5},{4,2},{5,3},{6,0},{7,1},{8,14},{9,15},{10,... | collective-permute-start | bytes 221192 | tf_op jit(solution)/shard_map/ppermute | solution.py:366
  104.7 6.1 %copy-start.18 = (bf16[16,2304]{1,0:T(8,128)(2,1)}, bf16[16,2304]{1,0:T(8,128)(2,1)S(1)}, u32[]{:S(2)}) copy-start(bf16[16,2304]{1,0:T(8,128)(2,1)S(1)} %collective-permute-done.5.refs_0_) | copy-start | bytes 221188
  110.8 0.6 copy-start.19
  110.8 0.6 copy-start.20
  113.2 20.2 %collective-permute-start.13 = (bf16[16,2304]{1,0:T(8,128)(2,1)}, bf16[16,2304]{1,0:T(8,128)(2,1)S(1)}, u32[]{:S(2)}, u32[]{:S(2)}) collective-permute-start(bf16[16,2304]{1,0:T(8,128)(2,1)} %popular_middle.1), channel_id=1, source_target_pairs={{0,2},{1,3},{2,0},{3,1},{4,6},{5,7},{6,4},{7,5},{8,10},{9,11},{10,... | collective-permute-start | bytes 221192 | tf_op jit(solution)/shard_map/ppermute | solution.py:366
  114.8 18.6 %collective-permute-start.14 = (bf16[16,2304]{1,0:T(8,128)(2,1)}, bf16[16,2304]{1,0:T(8,128)(2,1)S(1)}, u32[]{:S(2)}, u32[]{:S(2)}) collective-permute-start(bf16[16,2304]{1,0:T(8,128)(2,1)} %popular_middle.1), channel_id=1, source_target_pairs={{0,4},{1,5},{2,6},{3,7},{4,0},{5,1},{6,2},{7,3},{8,12},{9,13},{10,... | collective-permute-start | bytes 221192 | tf_op jit(solution)/shard_map/ppermute | solution.py:366
  116.3 17.1 %collective-permute-start.15 = (bf16[16,2304]{1,0:T(8,128)(2,1)}, bf16[16,2304]{1,0:T(8,128)(2,1)S(1)}, u32[]{:S(2)}, u32[]{:S(2)}) collective-permute-start(bf16[16,2304]{1,0:T(8,128)(2,1)} %popular_middle.1), channel_id=1, source_target_pairs={{0,6},{1,7},{2,4},{3,5},{4,2},{5,3},{6,0},{7,1},{8,14},{9,15},{10,... | collective-permute-start | bytes 221192 | tf_op jit(solution)/shard_map/ppermute | solution.py:366
  118.2 15.2 %copy-start.16 = (bf16[16,2304]{1,0:T(8,128)(2,1)S(1)}, bf16[16,2304]{1,0:T(8,128)(2,1)}, u32[]{:S(2)}) copy-start(bf16[16,2304]{1,0:T(8,128)(2,1)} %popular_middle.1) | copy-start | bytes 221188
  118.2 1.0 copy-start.13
  131.8 16.5 %collective-permute-start.17 = (bf16[192,1536]{1,0:T(8,128)(2,1)}, bf16[192,1536]{1,0:T(8,128)(2,1)S(1)}, u32[]{:S(2)}, u32[]{:S(2)}) collective-permute-start(bf16[192,1536]{1,0:T(8,128)(2,1)} %get-tuple-element.43.refs_2_), channel_id=1, source_target_pairs={{0,16},{8,24},{16,0},{24,8},{1,17},{9,25},{17,1},{25,9},{2,18},{10... | collective-permute-start | bytes 1769480 | tf_op jit(solution)/shard_map/ppermute | solution.py:345
  133.5 3.0 %copy-start.14 = (bf16[64,2304]{1,0:T(8,128)(2,1)}, bf16[64,2304]{1,0:T(8,128)(2,1)S(1)}, u32[]{:S(2)}) copy-start(bf16[64,2304]{1,0:T(8,128)(2,1)S(1)} %constant_dynamic-update-slice_fusion.2.refs_0_) | copy-start | bytes 884740
  133.5 9.3 %collective-permute-start.16 = (bf16[64,2304]{1,0:T(8,128)(2,1)S(1)}, bf16[64,2304]{1,0:T(8,128)(2,1)S(1)}, u32[]{:S(2)}, u32[]{:S(2)}) collective-permute-start(bf16[64,2304]{1,0:T(8,128)(2,1)S(1)} %constant_dynamic-update-slice_fusion.2.refs_0_), channel_id=1, source_target_pairs={{0,1},{1,0},{2,3},{3,2},{4,5},{5,4},{6,7},{7,6},{8,9},{9,8},{10,11... | collective-permute-start | bytes 884744 | tf_op jit(solution)/shard_map/ppermute | solution.py:366
  136.5 20.0 %collective-permute-start.12 = (bf16[192,1280]{1,0:T(8,128)(2,1)S(1)}, bf16[192,1280]{1,0:T(8,128)(2,1)S(1)}, u32[]{:S(2)}, u32[]{:S(2)}) collective-permute-start(bf16[192,1280]{1,0:T(8,128)(2,1)S(1)} %pad_maximum_fusion.2), channel_id=1, source_target_pairs={{0,16},{8,24},{16,0},{24,8},{1,17},{9,25},{17,1},{25,9},{2,18},{10... | collective-permute-start | bytes 1474568 | tf_op jit(solution)/shard_map/ppermute | solution.py:345
  142.8 65.2 %collective-permute-start.24 = (bf16[192,2560]{1,0:T(8,128)(2,1)}, bf16[192,2560]{1,0:T(8,128)(2,1)}, u32[]{:S(2)}, u32[]{:S(2)}) collective-permute-start(bf16[192,2560]{1,0:T(8,128)(2,1)} %get-tuple-element.57), channel_id=1, source_target_pairs={{0,8},{8,0},{16,24},{24,16},{1,9},{9,1},{17,25},{25,17},{2,10},{10... | collective-permute-start | bytes 2949128 | tf_op jit(solution)/shard_map/ppermute | solution.py:349
  142.8 5.6 %copy-start.17 = (bf16[64,2304]{1,0:T(8,128)(2,1)}, bf16[64,2304]{1,0:T(8,128)(2,1)S(1)}, u32[]{:S(2)}) copy-start(bf16[64,2304]{1,0:T(8,128)(2,1)S(1)} %collective-permute-done.16.refs_1_) | copy-start | bytes 884740
  148.3 4.0 %copy-start.6 = (bf16[192,1536]{1,0:T(8,128)(2,1)}, bf16[192,1536]{1,0:T(8,128)(2,1)S(1)}, u32[]{:S(2)}) copy-start(bf16[192,1536]{1,0:T(8,128)(2,1)S(1)} %collective-permute-done.17.refs_3_) | copy-start | bytes 1769476
  153.3 8.3 %collective-permute-start.18 = (bf16[4,4,2560]{2,1,0:T(4,128)(2,1)S(1)}, bf16[4,4,2560]{2,1,0:T(4,128)(2,1)S(1)}, u32[]{:S(2)}, u32[]{:S(2)}) collective-permute-start(bf16[4,4,2560]{2,1,0:T(4,128)(2,1)S(1)} %squeeze.49), channel_id=1, source_target_pairs={{0,1},{1,0},{2,3},{3,2},{4,5},{5,4},{6,7},{7,6},{8,9},{9,8},{10,11... | collective-permute-start | bytes 245768 | tf_op jit(solution)/shard_map/ppermute | solution.py:366
  156.4 0.8 copy-start.8
  157.2 97.7 %all-to-all-start.1 = ((bf16[8,24,5120]{2,1,0:T(8,128)(2,1)}), bf16[8,24,5120]{2,1,0:T(8,128)(2,1)S(1)}, u32[]{:S(2)}, u32[]{:S(2)}) async-start(bf16[8,24,5120]{2,1,0:T(8,128)(2,1)} %bitcast.81), calls=%async_computation.1 | async-start | bytes 3932160 | tf_op jit(solution)/shard_map/all_to_all | solution.py:322
  161.8 31.0 %collective-permute-start.19 = (bf16[2,4,2560]{2,1,0:T(4,128)(2,1)S(1)}, bf16[2,4,2560]{2,1,0:T(4,128)(2,1)S(1)}, u32[]{:S(2)}, u32[]{:S(2)}) collective-permute-start(bf16[2,4,2560]{2,1,0:T(4,128)(2,1)S(1)} %get-tuple-element.81), channel_id=1, source_target_pairs={{0,2},{1,3},{2,0},{3,1},{4,6},{5,7},{6,4},{7,5},{8,10},{9,11},{10,... | collective-permute-start | bytes 122888 | tf_op jit(solution)/shard_map/ppermute | solution.py:366
  163.9 43.9 %collective-permute-start.20 = (bf16[2,4,2560]{2,1,0:T(4,128)(2,1)S(1)}, bf16[2,4,2560]{2,1,0:T(4,128)(2,1)S(1)}, u32[]{:S(2)}, u32[]{:S(2)}) collective-permute-start(bf16[2,4,2560]{2,1,0:T(4,128)(2,1)S(1)} %get-tuple-element.83), channel_id=1, source_target_pairs={{0,4},{1,5},{2,6},{3,7},{4,0},{5,1},{6,2},{7,3},{8,12},{9,13},{10,... | collective-permute-start | bytes 122888 | tf_op jit(solution)/shard_map/ppermute | solution.py:366
  166.2 41.6 %collective-permute-start.21 = (bf16[2,4,2560]{2,1,0:T(4,128)(2,1)S(1)}, bf16[2,4,2560]{2,1,0:T(4,128)(2,1)S(1)}, u32[]{:S(2)}, u32[]{:S(2)}) collective-permute-start(bf16[2,4,2560]{2,1,0:T(4,128)(2,1)S(1)} %get-tuple-element.82), channel_id=1, source_target_pairs={{0,6},{1,7},{2,4},{3,5},{4,2},{5,3},{6,0},{7,1},{8,14},{9,15},{10,... | collective-permute-start | bytes 122888 | tf_op jit(solution)/shard_map/ppermute | solution.py:366
  167.1 79.8 %collective-permute-start.27 = (bf16[192,2560]{1,0:T(8,128)(2,1)}, bf16[192,2560]{1,0:T(8,128)(2,1)}, u32[]{:S(2)}, u32[]{:S(2)}) collective-permute-start(bf16[192,2560]{1,0:T(8,128)(2,1)} %get-tuple-element.61), channel_id=1, source_target_pairs={{0,8},{8,0},{16,24},{24,16},{1,9},{9,1},{17,25},{25,17},{2,10},{10... | collective-permute-start | bytes 2949128 | tf_op jit(solution)/shard_map/ppermute | solution.py:349
  171.6 36.3 %copy-start.9 = (bf16[192,2560]{1,0:T(8,128)(2,1)S(1)}, bf16[192,2560]{1,0:T(8,128)(2,1)}, u32[]{:S(2)}) copy-start(bf16[192,2560]{1,0:T(8,128)(2,1)} %get-tuple-element.56) | copy-start | bytes 2949124
  192.8 19.1 %collective-permute-start.22 = (bf16[1152,320]{0,1:T(8,128)(2,1)}, bf16[1152,320]{0,1:T(8,128)(2,1)}, u32[]{:S(2)}, u32[]{:S(2)}) collective-permute-start(bf16[1152,320]{0,1:T(8,128)(2,1)} %copy.62), channel_id=1, source_target_pairs={{0,8},{8,0},{16,24},{24,16},{1,9},{9,1},{17,25},{25,17},{2,10},{10... | collective-permute-start | bytes 2211848 | tf_op jit(solution)/shard_map/ppermute | solution.py:349
  207.8 42.0 %collective-permute-start.26 = (bf16[640,1536]{1,0:T(8,128)(2,1)}, bf16[640,1536]{1,0:T(8,128)(2,1)}, u32[]{:S(2)}, u32[]{:S(2)}) collective-permute-start(bf16[640,1536]{1,0:T(8,128)(2,1)} %gate_up_grads.2), channel_id=1, source_target_pairs={{0,8},{8,0},{16,24},{24,16},{1,9},{9,1},{17,25},{25,17},{2,10},{10... | collective-permute-start | bytes 5898248 | tf_op jit(solution)/shard_map/ppermute | solution.py:349
  210.4 36.5 %collective-permute-start.25 = (bf16[192,2560]{1,0:T(8,128)(2,1)}, bf16[192,2560]{1,0:T(8,128)(2,1)}, u32[]{:S(2)}, u32[]{:S(2)}) collective-permute-start(bf16[192,2560]{1,0:T(8,128)(2,1)} %add_convert_fusion.2), channel_id=1, source_target_pairs={{0,16},{8,24},{16,0},{24,8},{1,17},{9,25},{17,1},{25,9},{2,18},{10... | collective-permute-start | bytes 2949128 | tf_op jit(solution)/shard_map/ppermute | solution.py:345
  215.0 0.9 copy-start.2
  216.8 27.5 %copy-start.3 = (bf16[1152,320]{1,0:T(8,128)(2,1)S(1)}, bf16[1152,320]{1,0:T(8,128)(2,1)}, u32[]{:S(2)}) copy-start(bf16[1152,320]{1,0:T(8,128)(2,1)} %copy-done.2) | copy-start | bytes 2211844
  216.8 27.5 %collective-permute-start.23 = (bf16[576,320]{1,0:T(8,128)(2,1)}, bf16[576,320]{1,0:T(8,128)(2,1)}, u32[]{:S(2)}, u32[]{:S(2)}) collective-permute-start(bf16[576,320]{1,0:T(8,128)(2,1)} %slice.155), channel_id=1, source_target_pairs={{0,16},{8,24},{16,0},{24,8},{1,17},{9,25},{17,1},{25,9},{2,18},{10... | collective-permute-start | bytes 1105928 | tf_op jit(solution)/shard_map/ppermute | solution.py:345
  218.1 28.8 %copy-start.10 = (bf16[192,2560]{1,0:T(8,128)(2,1)S(1)}, bf16[192,2560]{1,0:T(8,128)(2,1)}, u32[]{:S(2)}) copy-start(bf16[192,2560]{1,0:T(8,128)(2,1)} %get-tuple-element.60) | copy-start | bytes 2949124
  255.5 0.7 copy-start.22
where the time goes:
time: 260 us; the launch traced here: 259 us
  waiting for transfers between devices  136 us (52%)
  starting transfers between devices  38.8 us (15%)
  Pallas kernels  37.4 us (14%)
  local copies, waits for them, and re-layouts  23.6 us (9%)
  other arithmetic  17.1 us (7%)
  matrix products  4.51 us (2%)
    ppermute x7, waiting for transfers between devices, shift(): return lax.ppermute(value, 'dp', pairs)  95.7 us
    ppermute x12, waiting for transfers between devices, hop(): return lax.ppermute(value, 'expert', [(i, i ^ j) for i in range(owners)])  40.4 us
    ppermute x12, starting transfers between devices, hop(): return lax.ppermute(value, 'expert', [(i, i ^ j) for i in range(owners)])  18.4 us
    pallas_call x1, Pallas kernels, expert(): pl.pallas_call(body, in_specs=[SMEM, INSIDE] + [ANYWHERE] * (2 * m), out_...  12.6 us
    all_to_all x2, starting transfers between devices, exchange(): lax.all_to_all(blocks, 'expert', split_axis=0, concat_axis=0, tiled=True)  11.8 us
    pallas_call x2, Pallas kernels, gate_up_grads(): pl.pallas_call(body, grid=(width // step,), in_specs=[pl.BlockSpec((rows,...  9.61 us
    ppermute x7, starting transfers between devices, shift(): return lax.ppermute(value, 'dp', pairs)  7.86 us
    unnamed x57, local copies, waits for them, and re-layouts  5.74 us
  transfers between devices with their start and end apart: 30, of which 9 were waited for; matrix products, arithmetic and copies ran while one was open for 11% of the time, Pallas kernels for 14%

commit v1 on v0

--- a/solution.py
+++ b/solution.py
@@ -77,22 +77,22 @@
     ]
 
 
-def expert(order, received, w_gu, w_down):
-    rows = received.shape[0]
+def expert(order, rows_s, rows_x, w_gu, w_down):
+    rows = rows_s.shape[0]
     depth, width = w_gu[0].shape
     deep, wide = w_down[0].shape
     half = width // 2
     m = len(w_gu)
     step = 512 if wide % 512 == 0 else wide
 
-    def body(order_ref, in_ref, *refs):
+    def body(order_ref, s_ref, x_ref, *refs):
         gu_in, dn_in, rest = refs[:m], refs[m : 2 * m], refs[2 * m :]
         back_ref, hid_ref, d_ref, acc, gu_ref, gu_sems, dn_ref, dn_sems = rest
         gu_copies = fetch_each(gu_in, gu_ref, gu_sems)
         dn_copies = fetch(order_ref, dn_in, dn_ref, dn_sems)
         for j, copy in enumerate(gu_copies):
             copy.wait()
-            found = mm(in_ref[:, wide + j * depth : wide + (j + 1) * depth], gu_ref[j])
+            found = mm(x_ref[:, j * depth : (j + 1) * depth], gu_ref[j])
             if j == 0:
                 acc[...] = found
             else:
@@ -103,7 +103,7 @@
         hid_ref[...] = (g * s * u).astype(BF)
         for copy in dn_copies:
             copy.wait()
-        d_hidden = mm(in_ref[:, :wide], dn_ref[...], NT)
+        d_hidden = mm(s_ref[...], dn_ref[...], NT)
         d_ref[:, :half] = (d_hidden * u * s * (1.0 + g * (1.0 - s))).astype(BF)
         d_ref[:, half:] = (d_hidden * g * s).astype(BF)
         for j in range(m):
@@ -114,7 +114,7 @@
 
     return pl.pallas_call(
         body,
-        in_specs=[SMEM, INSIDE] + [ANYWHERE] * (2 * m),
+        in_specs=[SMEM, INSIDE, INSIDE] + [ANYWHERE] * (2 * m),
         out_specs=[INSIDE] * 3,
         out_shape=[struct(rows, 2 * wide), struct(rows, half), struct(rows, width)],
         scratch_shapes=[pltpu.VMEM((rows, width), F32)]
@@ -123,7 +123,7 @@
         compiler_params=params(),
         cost_estimate=LIGHT,
         name="expert",
-    )(order, received, *w_gu, *w_down)
+    )(order, rows_s, rows_x, *w_gu, *w_down)
 
 
 def gate_up_grads(xs, ds, k, wide, scale, received):
@@ -371,7 +371,8 @@
     hot_w = jnp.concatenate([w_hot_gu, w_hot_dn[None]], axis=0).reshape(3 * hid, narrow)
     hot_near = [hot_w] + [shift(hot_w, r) for r in range(1, chips)]
     down_own = after(w_down[0], hot_near[-1])
-    gu_near = [w_gate_up[0]] + [shift(w_gate_up[0], r) for r in range(1, chips)]
+    gu_own = after(w_gate_up[0], hot_near[-1])
+    gu_near = [w_gate_up[0]] + [shift(gu_own, r) for r in range(1, chips)]
     down_near = [w_down[0]] + [shift(down_own, r) for r in range(1, chips)]
     gu_far = [swap(w_gate_up[0])] if cores == 2 else []
     down_far = [swap(w_down[0])] if cores == 2 else []
@@ -399,14 +400,22 @@
     turn = ((packed_id ^ (spot * few))[:, None] == packed_id[None, :]).astype(BF)
     row = jnp.arange(owners * hot_dev, dtype=jnp.int32)
     step = row // hot_dev
-    source = spot ^ ((step % depths) * across + step // depths)
     piece = (row % hot_dev) // few
 
     def selection(index):
         hit = (index * few + row % few)[:, None] == packed_id[None, :]
         return jnp.stack([hit & (piece == q)[:, None] for q in range(PIECES // 2)]).astype(BF)
 
+    hot_send = mm(turn, hot_send).astype(BF).reshape(depths, across, few, PIECES * narrow)
+    near = [hot_send[0]] + [hop(hot_send[j], j * across) for j in range(1, depths)]
+    near = jnp.stack(near, axis=1)
+    hot_recv = jnp.concatenate([near[0]] + [hop(near[j], j) for j in range(1, across)])
+    hot_recv = hot_recv.reshape(owners * few, PIECES * narrow)
+
     scaled = (gates[:, :, None] * cotangent[:, None, :].astype(F32)).astype(BF)
+    send_s = mm(pick, scaled.reshape(entries, width_d)).astype(BF)
+    rows_s = exchange(send_s.reshape(owners, slots, width_d)).reshape(rows, width_d)
+
     tok_rel = jnp.concatenate(
         [
             lax.dynamic_slice_in_dim(tokens, order[j] * wide, wide, 1)
@@ -415,40 +424,35 @@
         axis=1,
     )
     tok_rel = jnp.repeat(tok_rel, topk, axis=0) if topk > 1 else tok_rel
-    both = jnp.concatenate([scaled.reshape(entries, width_d), tok_rel], axis=1)
-    both = mm(pick, both).astype(BF).reshape(owners, slots, 2 * width_d)
-    load = 2 * hot_dev * narrow
-    extra = -(-load // (slots * 512)) * 512
-    hot_send = jnp.pad(hot_send.reshape(owners, load), ((0, 0), (0, slots * extra - load)))
-    send = jnp.concatenate([both, hot_send.reshape(owners, slots, extra)], axis=2)
-    received = exchange(send)
-    hot_recv = received[:, :, 2 * width_d :].reshape(owners, slots * extra)[:, :load]
-    hot_recv = hot_recv.reshape(owners * few, PIECES * narrow)
-    received = received.reshape(rows, 2 * width_d + extra)
-
-    hot_near = jnp.concatenate(list(after(tuple(hot_near), send, *gu_far, *down_far)), axis=0)
+    send_x = mm(pick, tok_rel).astype(BF).reshape(owners, slots, width_d)
+    rows_x = exchange(send_x).reshape(rows, width_d)
+
+    hot_near = jnp.concatenate(list(after(tuple(hot_near), send_x, *gu_far, *down_far)), axis=0)
     hot_ws = [hot_near] + ([swap(hot_near)] if cores == 2 else [])
-    hot_x, hot_s, partial = popular_partials(selection(source), hot_recv, hot_ws, hid)
+    hot_x, hot_s, partial = popular_partials(selection(step), hot_recv, hot_ws, hid)
     share = depths * hot_dev
     level_in = [hop(partial[j * share : (j + 1) * share], j) for j in range(1, across)]
     if cores == 2:
         gu_far = gu_far + [swap(block) for block in gu_near[1:]]
-        down_far = down_far + [swap(block) for block in down_near[1:]]
+    level_in = list(after(tuple(level_in), rows_s))
     level = partial[:share].astype(F32)
     for value in level_in:
         level = level + value.astype(F32)
     level = level.astype(BF)
     level = [level[j * hot_dev : (j + 1) * hot_dev] for j in range(depths)]
     depth_in = [hop(level[j], j * across) for j in range(1, depths)]
+    rows_x = after(rows_x, *depth_in)
     hot_own = popular_middle(level[0], depth_in, hid)
     line = [hot_own] + [hop(hot_own, j * across) for j in range(1, depths)]
-    work = after(received, hot_own)
-    back, hidden, d_act = expert(order, work, gu_near + gu_far, down_near + down_far)
+    down_near = list(after(tuple(down_near), hot_own))
+    if cores == 2:
+        down_far = down_far + [swap(block) for block in down_near[1:]]
+    back, hidden, d_act = expert(order, rows_s, after(rows_x, hot_own), gu_near + gu_far, down_near + down_far)
 
     def columns_of(r):
         return jnp.concatenate(
             [
-                received[:, width_d + (k * chips + r) * wide : width_d + (k * chips + r + 1) * wide]
+                rows_x[:, (k * chips + r) * wide : (k * chips + r + 1) * wide]
                 for k in range(cores)
             ],
             axis=1,
@@ -456,17 +460,16 @@
 
     xs = [columns_of(0)] + [shift(columns_of(r), -r) for r in range(1, chips)]
     ds = [d_act] + [shift(d_act, -r) for r in range(1, chips)]
-    back = after(back, xs[-1], *line[1:])
+    back = after(back, *line[1:])
     back = exchange(back.reshape(owners, slots, 2 * width_d)).reshape(rows, 2 * width_d)
 
     line = jnp.concatenate(list(after(tuple(line), d_act)))
     lines = [line] + [hop(line, j) for j in range(1, across)]
-    lines = list(after(tuple(lines), ds[-1]))
     hot_back, *hot_grads = popular_back(
         selection(step), lines, hot_x, hot_s, hot_ws, hid, inverse
     )
 
-    dn_parts = down_grads(order, hidden, received, width_d, groups, inverse)
+    dn_parts = down_grads(order, hidden, rows_s, width_d, groups, inverse)
     dn_sum = list(dn_parts[:chips])
     if cores == 2:
         dn_in = [swap(part) for part in dn_parts[chips:]]
@@ -482,10 +485,6 @@
     hot_back = hot_back.reshape(across, depths, few, PIECES * narrow)
     hot_back = [hot_back[0]] + [hop(hot_back[j], j) for j in range(1, across)]
     hot_back = jnp.stack(hot_back, axis=1)
-    hot_back = [hot_back[0]] + [hop(hot_back[j], j * across) for j in range(1, depths)]
-    hot_back = jnp.concatenate(hot_back).reshape(owners * few, PIECES * narrow)
-    hot_back = mm(turn, hot_back).astype(BF)
-
     xs_late = list(after(tuple(xs), d_act))
     gu_in = None
     if cores == 2:
@@ -502,6 +501,11 @@
     grad_hot = hot_total.astype(BF).reshape(3, hid, narrow)
     xs_last = list(after(tuple(xs_late), *hot_far, *dn_recv))
     grad_gu = gate_up_grads(xs_last, ds, 0, wide, inverse, gu_in)
+
+    hot_back = [hot_back[0]] + [hop(hot_back[j], j * across) for j in range(1, depths)]
+    hot_back = list(after(tuple(hot_back), grad_gu))
+    hot_back = jnp.concatenate(hot_back).reshape(owners * few, PIECES * narrow)
+    hot_back = mm(turn, hot_back).astype(BF)
 
     hot_back = hot_back.reshape(owners, few, PIECES, narrow)
     hot_back = hot_back.transpose(2, 1, 0, 3).reshape(2, hot_dev, width_d)

time: 260 us -> 216 us (0.83)
  waiting for transfers between devices: 136 us -> 83.8 us
  starting transfers between devices: 38.8 us -> 45.8 us
  matrix products: 4.51 us -> 9.14 us
  local copies, waits for them, and re-layouts: 23.6 us -> 20.8 us
    ppermute x7, waiting for transfers between devices: 95.7 us -> 43.6 us  [shift(): return lax.ppermute(value, 'dp', pairs)]
    ppermute x12 -> x16, starting transfers between devices: 18.4 us -> 26 us  [hop(): return lax.ppermute(value, 'expert', [(i, i ^ j) for i in range(owners)])]
    dot_general x7 -> x9, matrix products: 4.51 us -> 9.14 us  [mm(): return lax.dot_general(a, b, dims, preferred_element_type=F32)]
    unnamed x57 -> x78, local copies, waits for them, and re-layouts: 5.74 us -> 3.49 us
    all_to_all x2 -> x3, starting transfers between devices: 11.8 us -> 11.3 us  [exchange(): lax.all_to_all(blocks, 'expert', split_axis=0, concat_axis=0, tiled=True)]
    ppermute x12 -> x16, waiting for transfers between devices: 40.4 us -> 40.2 us  [hop(): return lax.ppermute(value, 'expert', [(i, i ^ j) for i in range(owners)])]
  transfers between devices with their start and end apart: 30 -> 35, of which waited for: 9 -> 7; matrix products, arithmetic and copies ran while one was open for 11% -> 18% of each run, Pallas kernels for 14% -> 17%
where the time goes in v1:
time: 216 us; the launch traced here: 215 us
  waiting for transfers between devices  83.8 us (39%)
  starting transfers between devices  45.8 us (21%)
  Pallas kernels  37.3 us (17%)
  local copies, waits for them, and re-layouts  20.8 us (10%)
  other arithmetic  16.3 us (8%)
  matrix products  9.14 us (4%)
    ppermute x7, waiting for transfers between devices, shift(): return lax.ppermute(value, 'dp', pairs)  43.6 us
    ppermute x16, waiting for transfers between devices, hop(): return lax.ppermute(value, 'expert', [(i, i ^ j) for i in range(owners)])  40.2 us
    ppermute x16, starting transfers between devices, hop(): return lax.ppermute(value, 'expert', [(i, i ^ j) for i in range(owners)])  26 us
    pallas_call x1, Pallas kernels, expert(): pl.pallas_call(body, in_specs=[SMEM, INSIDE, INSIDE] + [ANYWHERE] * (2 *...  12.5 us
    all_to_all x3, starting transfers between devices, exchange(): lax.all_to_all(blocks, 'expert', split_axis=0, concat_axis=0, tiled=True)  11.3 us
    pallas_call x2, Pallas kernels, gate_up_grads(): pl.pallas_call(body, grid=(width // step,), in_specs=[pl.BlockSpec((rows,...  9.61 us
    dot_general x9, matrix products, mm(): return lax.dot_general(a, b, dims, preferred_element_type=F32)  9.14 us
    ppermute x7, starting transfers between devices, shift(): return lax.ppermute(value, 'dp', pairs)  7.94 us
  transfers between devices with their start and end apart: 35, of which 7 were waited for; matrix products, arithmetic and copies ran while one was open for 18% of the time, Pallas kernels for 17%

profile of v1, /device:TPU:0, one launch (start us, length us, event | category | flops | bytes accessed | tf_op | source)
XLA Modules:
  0.0 214.8 jit_solution(1088761723007188286)
XLA Ops:
  1.3 1.1 pad_maximum_fusion.3
  2.4 3.0 %collective-permute-start.4 = (bf16[576,320]{1,0:T(8,128)(2,1)S(1)}, bf16[576,320]{1,0:T(8,128)(2,1)S(1)}, u32[]{:S(2)}, u32[]{:S(2)}) collective-permute-start(bf16[576,320]{1,0:T(8,128)(2,1)S(1)} %bitcast.86), channel_id=1, source_target_pairs={{0,16},{8,24},{16,0},{24,8},{1,17},{9,25},{17,1},{25,9},{2,18},{10... | collective-permute-start | bytes 1105928 | tf_op jit(solution)/shard_map/ppermute | solution.py:345
  5.4 1.3 convolution_convert_fusion.4
  9.0 1.6 collective-permute-start
  11.2 2.6 %collective-permute-start.1 = (bf16[2,4,2560]{2,1,0:T(4,128)(2,1)}, bf16[2,4,2560]{2,1,0:T(4,128)(2,1)}, u32[]{:S(2)}, u32[]{:S(2)}) collective-permute-start(bf16[2,4,2560]{2,1,0:T(4,128)(2,1)} %squeeze.63), channel_id=1, source_target_pairs={{0,4},{1,5},{2,6},{3,7},{4,0},{5,1},{6,2},{7,3},{8,12},{9,13},{10,... | collective-permute-start | bytes 122888 | tf_op jit(solution)/shard_map/ppermute | solution.py:366
  14.2 1.4 convolution_convert_fusion.1
  15.7 3.7 %all-to-all-start = ((bf16[8,24,2560]{2,1,0:T(8,128)(2,1)}), bf16[8,24,2560]{2,1,0:T(8,128)(2,1)S(1)}, u32[]{:S(2)}, u32[]{:S(2)}) async-start(bf16[8,24,2560]{2,1,0:T(8,128)(2,1)} %bitcast.6), calls=%async_computation | async-start | bytes 1966080 | tf_op jit(solution)/shard_map/all_to_all | solution.py:322
  20.1 0.8 constant_dynamic-slice_fusion.3
  20.9 0.8 squeeze.64
  21.8 2.5 %convolution_convert_fusion = bf16[192,2560]{1,0:T(8,128)(2,1)} fusion(bf16[128,640]{1,0:T(8,128)(2,1)} %get-tuple-element.91, bf16[128,640]{1,0:T(8,128)(2,1)} %get-tuple-element.89, bf16[128,640]{1,0:T(8,128)(2,1)} %get-tuple-element.90, bf16[128,640]{1,0:T(8,128)(2,1)} %get-tuple-element.88, s32[128]{0:T(128)S(1)} %multiply_add_fusion), kind=kOutput, calls=%fused_computation | convolution fusion | flops 128966656 | bytes 1638912 | tf_op jit(solution)/shard_map/dot_general | solution.py:22
  24.3 3.6 %collective-permute-start.2 = (bf16[2,4,2560]{2,1,0:T(4,128)(2,1)S(1)}, bf16[2,4,2560]{2,1,0:T(4,128)(2,1)S(1)}, u32[]{:S(2)}, u32[]{:S(2)}) collective-permute-start(bf16[2,4,2560]{2,1,0:T(4,128)(2,1)S(1)} %squeeze.64), channel_id=1, source_target_pairs={{0,6},{1,7},{2,4},{3,5},{4,2},{5,3},{6,0},{7,1},{8,14},{9,15},{10,... | collective-permute-start | bytes 122888 | tf_op jit(solution)/shard_map/ppermute | solution.py:366
  29.1 10.8 %collective-permute-done.2 = bf16[2,4,2560]{2,1,0:T(4,128)(2,1)S(1)} collective-permute-done((bf16[2,4,2560]{2,1,0:T(4,128)(2,1)S(1)}, bf16[2,4,2560]{2,1,0:T(4,128)(2,1)S(1)}, u32[]{:S(2)}, u32[]{:S(2)}) %collective-permute-start.2) | collective-permute-done | bytes 40992 | tf_op jit(solution)/shard_map/ppermute | solution.py:366
  40.0 1.0 pad_maximum_fusion.5
  41.2 1.5 copy.41
  42.7 1.4 collective-permute-start.3
  44.4 0.7 convert_element_type.103.sel_ref
  45.0 2.6 %collective-permute-done.3 = bf16[4,4,2560]{2,1,0:T(4,128)(2,1)S(1)} collective-permute-done((bf16[4,4,2560]{2,1,0:T(4,128)(2,1)S(1)}, bf16[4,4,2560]{2,1,0:T(4,128)(2,1)S(1)}, u32[]{:S(2)}, u32[]{:S(2)}) %collective-permute-start.3) | collective-permute-done | bytes 81952 | tf_op jit(solution)/shard_map/ppermute | solution.py:366
  47.8 0.7 reshape.357.in_ref
  48.5 2.2 %copy.42.refs_1_.refs_3_ = bf16[1152,320]{1,0:T(8,128)(2,1)} copy(bf16[1152,320]{0,1:T(8,128)(2,1)} %collective-permute-done.7) | data formatting | bytes 1474560 | tf_op jit(solution)/shard_map/ppermute | solution.py:349
  50.7 3.8 %popular_partials.1 = (bf16[128,320]{1,0:T(8,128)(2,1)}, bf16[128,320]{1,0:T(8,128)(2,1)}, bf16[128,2304]{1,0:T(8,128)(2,1)}) custom-call(bf16[4,128,32]{2,1,0:T(8,128)(2,1)} %convert_element_type.103.sel_ref, bf16[32,2560]{1,0:T(8,128)(2,1)} %reshape.357.in_ref, bf16[1152,320]{1,0:T(8,128)(2,1)} %copy-done, bf16[1152,320]{1,0:T(8,128)(2,1)} %copy.42.refs_1_.refs_3_), custom_call_target="tpu_custom_call" | custom-call | flops 1 | bytes 1 | tf_op jit(solution)/shard_map/popular_partials/pallas_call | solution.py:221
  54.5 1.8 slice.125
  56.2 1.3 collective-permute-start.8
  58.1 16.6 %collective-permute-done.12.refs_1_ = bf16[640,1536]{1,0:T(8,128)(2,1)} collective-permute-done((bf16[640,1536]{1,0:T(8,128)(2,1)}, bf16[640,1536]{1,0:T(8,128)(2,1)}, u32[]{:S(2)}, u32[]{:S(2)}) %collective-permute-start.12) | collective-permute-done | bytes 1966112 | tf_op jit(solution)/shard_map/ppermute | solution.py:345
  74.7 3.7 %all-to-all-start.1 = ((bf16[8,24,2560]{2,1,0:T(8,128)(2,1)}), bf16[8,24,2560]{2,1,0:T(8,128)(2,1)S(1)}, u32[]{:S(2)}, u32[]{:S(2)}) async-start(bf16[8,24,2560]{2,1,0:T(8,128)(2,1)} %bitcast.8), calls=%async_computation.1 | async-start | bytes 1966080 | tf_op jit(solution)/shard_map/all_to_all | solution.py:322
  78.5 1.0 add_convert_fusion.5
  79.5 0.7 fusion.40
  80.2 2.6 %collective-permute-start.10 = (bf16[16,2304]{1,0:T(8,128)(2,1)S(1)}, bf16[16,2304]{1,0:T(8,128)(2,1)S(1)}, u32[]{:S(2)}, u32[]{:S(2)}) collective-permute-start(bf16[16,2304]{1,0:T(8,128)(2,1)S(1)} %get-tuple-element.94), channel_id=1, source_target_pairs={{0,4},{1,5},{2,6},{3,7},{4,0},{5,1},{6,2},{7,3},{8,12},{9,13},{10,... | collective-permute-start | bytes 221192 | tf_op jit(solution)/shard_map/ppermute | solution.py:366
  82.8 1.4 collective-permute-start.11
  84.3 24.4 %collective-permute-done.10.refs_1_ = bf16[16,2304]{1,0:T(8,128)(2,1)S(1)} collective-permute-done((bf16[16,2304]{1,0:T(8,128)(2,1)S(1)}, bf16[16,2304]{1,0:T(8,128)(2,1)S(1)}, u32[]{:S(2)}, u32[]{:S(2)}) %collective-permute-start.10) | collective-permute-done | bytes 73760 | tf_op jit(solution)/shard_map/ppermute | solution.py:366
  109.4 1.7 popular_middle.1
  111.1 0.7 pad_add_fusion.1.order_ref
  111.8 1.7 collective-permute-start.16
  113.5 0.8 collective-permute-start.17
  114.4 1.8 collective-permute-start.18
  116.3 1.0 pad_maximum_fusion.2
  118.2 12.5 %expert.1 = (bf16[192,5120]{1,0:T(8,128)(2,1)}, bf16[192,768]{1,0:T(8,128)(2,1)}, bf16[192,1536]{1,0:T(8,128)(2,1)}) custom-call(s32[4]{0:T(128)} %pad_add_fusion.1.order_ref, bf16[192,2560]{1,0:T(8,128)(2,1)} %bitcast.79, bf16[192,2560]{1,0:T(8,128)(2,1)} %bitcast.82, bf16[640,1536]{1,0:T(8,128)(2,1)} %bitcast.19.refs_0_, ...), custom_call_target="tpu_custom_call" | custom-call | flops 1 | bytes 1 | tf_op jit(solution)/shard_map/expert/pallas_call | solution.py:115
  130.8 5.9 %down_grads.1 = (bf16[192,2560]{1,0:T(8,128)(2,1)}, bf16[192,2560]{1,0:T(8,128)(2,1)}, bf16[192,2560]{1,0:T(8,128)(2,1)}, bf16[192,2560]{1,0:T(8,128)(2,1)}) custom-call(s32[4]{0:T(128)} %pad_add_fusion.1.order_ref, bf16[192,768]{1,0:T(8,128)(2,1)} %get-tuple-element.65.h_ref, bf16[192,2560]{1,0:T(8,128)(2,1)} %bitcast.80), custom_call_target="tpu_custom_call" | custom-call | flops 1 | bytes 1 | tf_op jit(solution)/shard_map/down_grads/pallas_call | solution.py:180
  136.8 1.4 collective-permute-start.19
  138.2 0.8 pad_maximum_fusion.1.refs_0_
  139.1 1.2 collective-permute-start.29
  140.2 3.8 %all-to-all-start.2 = ((bf16[8,24,5120]{2,1,0:T(8,128)(2,1)}), bf16[8,24,5120]{2,1,0:T(8,128)(2,1)S(1)}, u32[]{:S(2)}, u32[]{:S(2)}) async-start(bf16[8,24,5120]{2,1,0:T(8,128)(2,1)} %bitcast.84), calls=%async_computation.2 | async-start | bytes 3932160 | tf_op jit(solution)/shard_map/all_to_all | solution.py:322
  144.1 2.3 %collective-permute-done.19.refs_1_ = bf16[64,2304]{1,0:T(8,128)(2,1)} collective-permute-done((bf16[64,2304]{1,0:T(8,128)(2,1)S(1)}, bf16[64,2304]{1,0:T(8,128)(2,1)}, u32[]{:S(2)}, u32[]{:S(2)}) %collective-permute-start.19) | collective-permute-done | bytes 294944 | tf_op jit(solution)/shard_map/ppermute | solution.py:366
  146.4 3.8 %popular_back.1 = (bf16[32,2560]{1,0:T(8,128)(2,1)}, bf16[1152,320]{1,0:T(8,128)(2,1)}, bf16[1152,320]{1,0:T(8,128)(2,1)}) custom-call(bf16[4,128,32]{2,1,0:T(8,128)(2,1)} %convert_element_type.103.sel_ref, bf16[128,320]{1,0:T(8,128)(2,1)} %get-tuple-element.53.x_ref, bf16[128,320]{1,0:T(8,128)(2,1)} %get-tuple-element.54.s_ref, ...), custom_call_target="tpu_custom_call" | custom-call | flops 1 | bytes 1 | tf_op jit(solution)/shard_map/popular_back/pallas_call | solution.py:301
  150.1 2.3 %copy.47 = bf16[1152,320]{0,1:T(8,128)(2,1)} copy(bf16[1152,320]{1,0:T(8,128)(2,1)} %get-tuple-element.64) | data formatting | bytes 1474560 | tf_op jit(solution)/shard_map/popular_back/pallas_call | solution.py:301
  152.5 1.4 collective-permute-start.20
  154.5 0.8 copy-done.7
  155.3 4.5 %gate_up_grads.2 = bf16[640,1536]{1,0:T(8,128)(2,1)} custom-call(bf16[192,1280]{1,0:T(8,128)(2,1)} %pad_maximum_fusion.1.refs_0_, bf16[192,1280]{1,0:T(8,128)(2,1)} %collective-permute-done.24.refs_1_, bf16[192,1536]{1,0:T(8,128)(2,1)} %get-tuple-element.55.refs_2_, bf16[192,1536]{1,0:T(8,128)(2,1)} %copy-done.7), custom_call_target="tpu_custom_call" | custom-call | flops 1 | bytes 1 | tf_op jit(solution)/shard_map/gate_up_grads/pallas_call | solution.py:152
  159.8 2.4 %add_convert_fusion.2 = bf16[192,2560]{1,0:T(8,128)(2,1)} fusion(bf16[192,2560]{1,0:T(8,128)(2,1)} %collective-permute-done.27, bf16[192,2560]{1,0:T(8,128)(2,1)S(1)} %copy-done.8), kind=kLoop, calls=%fused_computation.14 | loop fusion | flops 1966080 | bytes 2949120 | tf_op jit(solution)/shard_map/convert_element_type | solution.py:477
  162.2 1.2 collective-permute-start.28
  163.4 1.7 copy.48
  165.1 1.4 add_convert_fusion.3
  166.5 0.9 copy-done.3
  167.5 0.9 collective-permute-start.26
  168.7 0.9 collective-permute-start.21
  169.6 26.4 %collective-permute-done.26 = bf16[576,320]{1,0:T(8,128)(2,1)S(1)} collective-permute-done((bf16[576,320]{1,0:T(8,128)(2,1)S(1)}, bf16[576,320]{1,0:T(8,128)(2,1)S(1)}, u32[]{:S(2)}, u32[]{:S(2)}) %collective-permute-start.26) | collective-permute-done | bytes 368672 | tf_op jit(solution)/shard_map/ppermute | solution.py:345
  196.0 0.9 collective-permute-start.22
  197.0 1.1 add_convert_fusion.4
  198.1 0.7 slice.177
  198.8 0.7 slice.178
  199.5 2.3 %collective-permute-start.23 = (bf16[2,4,2560]{2,1,0:T(4,128)(2,1)S(1)}, bf16[2,4,2560]{2,1,0:T(4,128)(2,1)S(1)}, u32[]{:S(2)}, u32[]{:S(2)}) collective-permute-start(bf16[2,4,2560]{2,1,0:T(4,128)(2,1)S(1)} %get-tuple-element.98), channel_id=1, source_target_pairs={{0,6},{1,7},{2,4},{3,5},{4,2},{5,3},{6,0},{7,1},{8,14},{9,15},{10,... | collective-permute-start | bytes 122888 | tf_op jit(solution)/shard_map/ppermute | solution.py:366
  201.8 2.9 %fusion.4 = bf16[1,192,2560]{2,1,0:T(8,128)(2,1)} fusion(bf16[192,2560]{1,0:T(8,128)(2,1)} %collective-permute-done.28, bf16[192,2560]{1,0:T(8,128)(2,1)} %collective-permute-done.31, bf16[192,2560]{1,0:T(8,128)(2,1)S(1)} %copy-done.9), kind=kLoop, calls=%fused_computation.19 | loop fusion | flops 3932160 | bytes 3932160 | tf_op jit(solution)/shard_map/broadcast_in_dim | solution.py:540
  204.7 5.1 %gate_up_grads.3 = bf16[640,1536]{1,0:T(8,128)(2,1)} custom-call(bf16[192,1280]{1,0:T(8,128)(2,1)} %pad_maximum_fusion.1.refs_0_, bf16[192,1280]{1,0:T(8,128)(2,1)} %collective-permute-done.24.refs_1_, bf16[192,1536]{1,0:T(8,128)(2,1)} %get-tuple-element.55.refs_2_, bf16[192,1536]{1,0:T(8,128)(2,1)} %copy-done.7, ...), custom_call_target="tpu_custom_call" | custom-call | flops 1 | bytes 1 | tf_op jit(solution)/shard_map/gate_up_grads/pallas_call | solution.py:152
  212.0 1.3 fusion.2
  213.5 1.3 fusion.1
  (162 shorter events, 11.7 us)
Async XLA Ops:
  0.6 6.1 %copy-start.24 = (s32[16]{0:T(128)S(1)}, s32[16]{0:T(128)}, u32[]{:S(2)}) copy-start(s32[16]{0:T(128)} %param.14) | copy-start | bytes 196
  0.6 6.1 %copy-start.4 = (bf16[128,2560]{1,0:T(8,128)(2,1)S(1)}, bf16[128,2560]{1,0:T(8,128)(2,1)}, u32[]{:S(2)}) copy-start(bf16[128,2560]{1,0:T(8,128)(2,1)} %param.11) | copy-start | bytes 1966084
  0.7 6.1 %copy-start.35 = (f32[16]{0:T(128)S(1)}, f32[16]{0:T(128)}, u32[]{:S(2)}) copy-start(f32[16]{0:T(128)} %param.15) | copy-start | bytes 196
  0.7 40.3 %collective-permute-start.5 = (bf16[640,1536]{1,0:T(8,128)(2,1)}, bf16[640,1536]{1,0:T(8,128)(2,1)}, u32[]{:S(2)}, u32[]{:S(2)}) collective-permute-start(bf16[640,1536]{1,0:T(8,128)(2,1)} %bitcast.19.refs_0_), channel_id=1, source_target_pairs={{0,8},{8,0},{16,24},{24,16},{1,9},{9,1},{17,25},{25,17},{2,10},{10... | collective-permute-start | bytes 5898248 | tf_op jit(solution)/shard_map/ppermute | solution.py:349
  1.2 39.8 %collective-permute-start.6 = (bf16[192,2560]{1,0:T(8,128)(2,1)}, bf16[192,2560]{1,0:T(8,128)(2,1)S(1)}, u32[]{:S(2)}, u32[]{:S(2)}) collective-permute-start(bf16[192,2560]{1,0:T(8,128)(2,1)} %bitcast.88), channel_id=1, source_target_pairs={{0,8},{8,0},{16,24},{24,16},{1,9},{9,1},{17,25},{25,17},{2,10},{10... | collective-permute-start | bytes 2949128 | tf_op jit(solution)/shard_map/ppermute | solution.py:349
  2.4 21.9 %collective-permute-start.4 = (bf16[576,320]{1,0:T(8,128)(2,1)S(1)}, bf16[576,320]{1,0:T(8,128)(2,1)S(1)}, u32[]{:S(2)}, u32[]{:S(2)}) collective-permute-start(bf16[576,320]{1,0:T(8,128)(2,1)S(1)} %bitcast.86), channel_id=1, source_target_pairs={{0,16},{8,24},{16,0},{24,8},{1,17},{9,25},{17,1},{25,9},{2,18},{10... | collective-permute-start | bytes 1105928 | tf_op jit(solution)/shard_map/ppermute | solution.py:345
  5.4 2.1 copy-start.27
  7.0 6.7 %copy-start.26 = (s32[128,1]{0,1:T(1,128)S(1)}, s32[128,1]{0,1:T(1,128)}, u32[]{:S(2)}) copy-start(s32[128,1]{0,1:T(1,128)} %param.12) | copy-start | bytes 1540
  7.0 7.2 %copy-start.31 = (f32[128,1]{0,1:T(1,128)S(1)}, f32[128,1]{0,1:T(1,128)}, u32[]{:S(2)}) copy-start(f32[128,1]{0,1:T(1,128)} %param.13) | copy-start | bytes 1540
  9.0 19.6 %collective-permute-start = (bf16[2,4,2560]{2,1,0:T(4,128)(2,1)}, bf16[2,4,2560]{2,1,0:T(4,128)(2,1)}, u32[]{:S(2)}, u32[]{:S(2)}) collective-permute-start(bf16[2,4,2560]{2,1,0:T(4,128)(2,1)} %squeeze.62), channel_id=1, source_target_pairs={{0,2},{1,3},{2,0},{3,1},{4,6},{5,7},{6,4},{7,5},{8,10},{9,11},{10,... | collective-permute-start | bytes 122888 | tf_op jit(solution)/shard_map/ppermute | solution.py:366
  11.2 18.0 %collective-permute-start.1 = (bf16[2,4,2560]{2,1,0:T(4,128)(2,1)}, bf16[2,4,2560]{2,1,0:T(4,128)(2,1)}, u32[]{:S(2)}, u32[]{:S(2)}) collective-permute-start(bf16[2,4,2560]{2,1,0:T(4,128)(2,1)} %squeeze.63), channel_id=1, source_target_pairs={{0,4},{1,5},{2,6},{3,7},{4,0},{5,1},{6,2},{7,3},{8,12},{9,13},{10,... | collective-permute-start | bytes 122888 | tf_op jit(solution)/shard_map/ppermute | solution.py:366
  14.2 7.5 %copy-start.29 = (s32[128]{0:T(128)}, s32[128]{0:T(128)S(1)}, u32[]{:S(2)}) copy-start(s32[128]{0:T(128)S(1)} %multiply_add_fusion) | copy-start | bytes 1540
  15.7 4.4 %copy-start.5 = (bf16[128,2560]{1,0:T(8,128)(2,1)S(1)}, bf16[128,2560]{1,0:T(8,128)(2,1)}, u32[]{:S(2)}) copy-start(bf16[128,2560]{1,0:T(8,128)(2,1)} %param.10) | copy-start | bytes 1966084
  15.7 59.0 %all-to-all-start = ((bf16[8,24,2560]{2,1,0:T(8,128)(2,1)}), bf16[8,24,2560]{2,1,0:T(8,128)(2,1)S(1)}, u32[]{:S(2)}, u32[]{:S(2)}) async-start(bf16[8,24,2560]{2,1,0:T(8,128)(2,1)} %bitcast.6), calls=%async_computation | async-start | bytes 1966080 | tf_op jit(solution)/shard_map/all_to_all | solution.py:322
  20.9 7.0 %copy-start.33 = (pred[128]{0:T(512)(128)(4,1)S(1)}, pred[128]{0:T(512)(128)(4,1)}, u32[]{:S(2)}) copy-start(pred[128]{0:T(512)(128)(4,1)} %get-tuple-element.114) | copy-start | bytes 388
  20.9 7.0 %copy-start.34 = (pred[128]{0:T(512)(128)(4,1)S(1)}, pred[128]{0:T(512)(128)(4,1)}, u32[]{:S(2)}) copy-start(pred[128]{0:T(512)(128)(4,1)} %get-tuple-element.115) | copy-start | bytes 388
  24.3 15.7 %copy-start.15 = (bf16[576,320]{1,0:T(8,128)(2,1)}, bf16[576,320]{1,0:T(8,128)(2,1)S(1)}, u32[]{:S(2)}) copy-start(bf16[576,320]{1,0:T(8,128)(2,1)S(1)} %collective-permute-done.4) | copy-start | bytes 1105924
  24.3 15.7 %collective-permute-start.2 = (bf16[2,4,2560]{2,1,0:T(4,128)(2,1)S(1)}, bf16[2,4,2560]{2,1,0:T(4,128)(2,1)S(1)}, u32[]{:S(2)}, u32[]{:S(2)}) collective-permute-start(bf16[2,4,2560]{2,1,0:T(4,128)(2,1)S(1)} %squeeze.64), channel_id=1, source_target_pairs={{0,6},{1,7},{2,4},{3,5},{4,2},{5,3},{6,0},{7,1},{8,14},{9,15},{10,... | collective-permute-start | bytes 122888 | tf_op jit(solution)/shard_map/ppermute | solution.py:366
  28.6 46.1 %collective-permute-start.12 = (bf16[640,1536]{1,0:T(8,128)(2,1)}, bf16[640,1536]{1,0:T(8,128)(2,1)}, u32[]{:S(2)}, u32[]{:S(2)}) collective-permute-start(bf16[640,1536]{1,0:T(8,128)(2,1)} %bitcast.19.refs_0_), channel_id=1, source_target_pairs={{0,16},{8,24},{16,0},{24,8},{1,17},{9,25},{17,1},{25,9},{2,18},{10... | collective-permute-start | bytes 5898248 | tf_op jit(solution)/shard_map/ppermute | solution.py:345
  40.0 1.1 copy-start.16
  41.0 1.7 copy-start.11
  41.1 3.1 %copy-start.22 = (pred[1,128,32]{1,2,0:T(8,128)(4,1)S(1)}, pred[1,128,32]{1,2,0:T(8,128)(4,1)}, u32[]{:S(2)}) copy-start(pred[1,128,32]{1,2,0:T(8,128)(4,1)} %get-tuple-element.112) | copy-start | bytes 12292
  41.1 3.1 %copy-start.23 = (pred[1,128,32]{1,2,0:T(8,128)(4,1)S(1)}, pred[1,128,32]{1,2,0:T(8,128)(4,1)}, u32[]{:S(2)}) copy-start(pred[1,128,32]{1,2,0:T(8,128)(4,1)} %get-tuple-element.113) | copy-start | bytes 12292
  41.2 7.3 %copy-start = (bf16[1152,320]{1,0:T(8,128)(2,1)}, bf16[1152,320]{1,0:T(8,128)(2,1)S(1)}, u32[]{:S(2)}) copy-start(bf16[1152,320]{1,0:T(8,128)(2,1)S(1)} %constant_dynamic-update-slice_fusion.refs_0_.refs_2_) | copy-start | bytes 2211844
  42.7 5.8 %collective-permute-start.7 = (bf16[1152,320]{0,1:T(8,128)(2,1)}, bf16[1152,320]{0,1:T(8,128)(2,1)}, u32[]{:S(2)}, u32[]{:S(2)}) collective-permute-start(bf16[1152,320]{0,1:T(8,128)(2,1)} %copy.41), channel_id=1, source_target_pairs={{0,8},{8,0},{16,24},{24,16},{1,9},{9,1},{17,25},{25,17},{2,10},{10... | collective-permute-start | bytes 2211848 | tf_op jit(solution)/shard_map/ppermute | solution.py:349
  42.7 4.9 %collective-permute-start.3 = (bf16[4,4,2560]{2,1,0:T(4,128)(2,1)S(1)}, bf16[4,4,2560]{2,1,0:T(4,128)(2,1)S(1)}, u32[]{:S(2)}, u32[]{:S(2)}) collective-permute-start(bf16[4,4,2560]{2,1,0:T(4,128)(2,1)S(1)} %get-tuple-element.105), channel_id=1, source_target_pairs={{0,1},{1,0},{2,3},{3,2},{4,5},{5,4},{6,7},{7,6},{8,9},{9,8},{10,11... | collective-permute-start | bytes 245768 | tf_op jit(solution)/shard_map/ppermute | solution.py:366
  50.7 6.9 %copy-start.10 = (bf16[1,192,2560]{2,1,0:T(8,128)(2,1)S(1)}, bf16[1,192,2560]{2,1,0:T(8,128)(2,1)}, u32[]{:S(2)}) copy-start(bf16[1,192,2560]{2,1,0:T(8,128)(2,1)} %param.17) | copy-start | bytes 2949124
  54.5 24.0 %copy-start.13 = (bf16[128,2304]{1,0:T(8,128)(2,1)S(1)}, bf16[128,2304]{1,0:T(8,128)(2,1)}, u32[]{:S(2)}) copy-start(bf16[128,2304]{1,0:T(8,128)(2,1)} %get-tuple-element.43) | copy-start | bytes 1769476
  56.2 22.2 %collective-permute-start.8 = (bf16[64,2304]{1,0:T(8,128)(2,1)}, bf16[64,2304]{1,0:T(8,128)(2,1)}, u32[]{:S(2)}, u32[]{:S(2)}) collective-permute-start(bf16[64,2304]{1,0:T(8,128)(2,1)} %slice.125), channel_id=1, source_target_pairs={{0,1},{1,0},{2,3},{3,2},{4,5},{5,4},{6,7},{7,6},{8,9},{9,8},{10,11... | collective-permute-start | bytes 884744 | tf_op jit(solution)/shard_map/ppermute | solution.py:366
  57.6 53.5 %collective-permute-start.14 = (bf16[192,2560]{1,0:T(8,128)(2,1)S(1)}, bf16[192,2560]{1,0:T(8,128)(2,1)}, u32[]{:S(2)}, u32[]{:S(2)}) collective-permute-start(bf16[192,2560]{1,0:T(8,128)(2,1)S(1)} %bitcast.90), channel_id=1, source_target_pairs={{0,16},{8,24},{16,0},{24,8},{1,17},{9,25},{17,1},{25,9},{2,18},{10... | collective-permute-start | bytes 2949128 | tf_op jit(solution)/shard_map/ppermute | solution.py:345
  74.7 43.2 %collective-permute-start.13 = (bf16[640,1536]{1,0:T(8,128)(2,1)}, bf16[640,1536]{1,0:T(8,128)(2,1)}, u32[]{:S(2)}, u32[]{:S(2)}) collective-permute-start(bf16[640,1536]{1,0:T(8,128)(2,1)} %collective-permute-done.12.refs_1_), channel_id=1, source_target_pairs={{0,8},{8,0},{16,24},{24,16},{1,9},{9,1},{17,25},{25,17},{2,10},{10... | collective-permute-start | bytes 5898248 | tf_op jit(solution)/shard_map/ppermute | solution.py:349
  74.7 4.8 %copy-start.1 = (bf16[8,24,2560]{2,1,0:T(8,128)(2,1)}, bf16[8,24,2560]{2,1,0:T(8,128)(2,1)S(1)}, u32[]{:S(2)}) copy-start(bf16[8,24,2560]{2,1,0:T(8,128)(2,1)S(1)} %all-to-all-done) | copy-start | bytes 2949124
  74.7 41.5 %all-to-all-start.1 = ((bf16[8,24,2560]{2,1,0:T(8,128)(2,1)}), bf16[8,24,2560]{2,1,0:T(8,128)(2,1)S(1)}, u32[]{:S(2)}, u32[]{:S(2)}) async-start(bf16[8,24,2560]{2,1,0:T(8,128)(2,1)} %bitcast.8), calls=%async_computation.1 | async-start | bytes 1966080 | tf_op jit(solution)/shard_map/all_to_all | solution.py:322
  80.2 28.5 %collective-permute-start.10 = (bf16[16,2304]{1,0:T(8,128)(2,1)S(1)}, bf16[16,2304]{1,0:T(8,128)(2,1)S(1)}, u32[]{:S(2)}, u32[]{:S(2)}) collective-permute-start(bf16[16,2304]{1,0:T(8,128)(2,1)S(1)} %get-tuple-element.94), channel_id=1, source_target_pairs={{0,4},{1,5},{2,6},{3,7},{4,0},{5,1},{6,2},{7,3},{8,12},{9,13},{10,... | collective-permute-start | bytes 221192 | tf_op jit(solution)/shard_map/ppermute | solution.py:366
  82.8 25.9 %collective-permute-start.11 = (bf16[16,2304]{1,0:T(8,128)(2,1)S(1)}, bf16[16,2304]{1,0:T(8,128)(2,1)S(1)}, u32[]{:S(2)}, u32[]{:S(2)}) collective-permute-start(bf16[16,2304]{1,0:T(8,128)(2,1)S(1)} %get-tuple-element.92), channel_id=1, source_target_pairs={{0,6},{1,7},{2,4},{3,5},{4,2},{5,3},{6,0},{7,1},{8,14},{9,15},{10,... | collective-permute-start | bytes 221192 | tf_op jit(solution)/shard_map/ppermute | solution.py:366
  84.3 24.4 %collective-permute-start.9 = (bf16[16,2304]{1,0:T(8,128)(2,1)S(1)}, bf16[16,2304]{1,0:T(8,128)(2,1)S(1)}, u32[]{:S(2)}, u32[]{:S(2)}) collective-permute-start(bf16[16,2304]{1,0:T(8,128)(2,1)S(1)} %get-tuple-element.95), channel_id=1, source_target_pairs={{0,2},{1,3},{2,0},{3,1},{4,6},{5,7},{6,4},{7,5},{8,10},{9,11},{10,... | collective-permute-start | bytes 221192 | tf_op jit(solution)/shard_map/ppermute | solution.py:366
  111.1 6.2 %collective-permute-start.15 = (bf16[192,2560]{1,0:T(8,128)(2,1)}, bf16[192,2560]{1,0:T(8,128)(2,1)S(1)}, u32[]{:S(2)}, u32[]{:S(2)}) collective-permute-start(bf16[192,2560]{1,0:T(8,128)(2,1)} %collective-permute-done.14.refs_5_), channel_id=1, source_target_pairs={{0,8},{8,0},{16,24},{24,16},{1,9},{9,1},{17,25},{25,17},{2,10},{10... | collective-permute-start | bytes 2949128 | tf_op jit(solution)/shard_map/ppermute | solution.py:349
  111.8 19.0 %collective-permute-start.16 = (bf16[16,2304]{1,0:T(8,128)(2,1)}, bf16[16,2304]{1,0:T(8,128)(2,1)S(1)}, u32[]{:S(2)}, u32[]{:S(2)}) collective-permute-start(bf16[16,2304]{1,0:T(8,128)(2,1)} %popular_middle.1), channel_id=1, source_target_pairs={{0,2},{1,3},{2,0},{3,1},{4,6},{5,7},{6,4},{7,5},{8,10},{9,11},{10,... | collective-permute-start | bytes 221192 | tf_op jit(solution)/shard_map/ppermute | solution.py:366
  113.5 17.2 %collective-permute-start.17 = (bf16[16,2304]{1,0:T(8,128)(2,1)}, bf16[16,2304]{1,0:T(8,128)(2,1)S(1)}, u32[]{:S(2)}, u32[]{:S(2)}) collective-permute-start(bf16[16,2304]{1,0:T(8,128)(2,1)} %popular_middle.1), channel_id=1, source_target_pairs={{0,4},{1,5},{2,6},{3,7},{4,0},{5,1},{6,2},{7,3},{8,12},{9,13},{10,... | collective-permute-start | bytes 221192 | tf_op jit(solution)/shard_map/ppermute | solution.py:366
  114.4 16.4 %collective-permute-start.18 = (bf16[16,2304]{1,0:T(8,128)(2,1)}, bf16[16,2304]{1,0:T(8,128)(2,1)S(1)}, u32[]{:S(2)}, u32[]{:S(2)}) collective-permute-start(bf16[16,2304]{1,0:T(8,128)(2,1)} %popular_middle.1), channel_id=1, source_target_pairs={{0,6},{1,7},{2,4},{3,5},{4,2},{5,3},{6,0},{7,1},{8,14},{9,15},{10,... | collective-permute-start | bytes 221192 | tf_op jit(solution)/shard_map/ppermute | solution.py:366
  116.2 1.1 copy-start.2
  117.3 13.5 %copy-start.17 = (bf16[16,2304]{1,0:T(8,128)(2,1)S(1)}, bf16[16,2304]{1,0:T(8,128)(2,1)}, u32[]{:S(2)}) copy-start(bf16[16,2304]{1,0:T(8,128)(2,1)} %popular_middle.1) | copy-start | bytes 221188
  117.3 26.8 %collective-permute-start.24 = (bf16[192,1280]{1,0:T(8,128)(2,1)}, bf16[192,1280]{1,0:T(8,128)(2,1)}, u32[]{:S(2)}, u32[]{:S(2)}) collective-permute-start(bf16[192,1280]{1,0:T(8,128)(2,1)} %pad_maximum_fusion.2), channel_id=1, source_target_pairs={{0,16},{8,24},{16,0},{24,8},{1,17},{9,25},{17,1},{25,9},{2,18},{10... | collective-permute-start | bytes 1474568 | tf_op jit(solution)/shard_map/ppermute | solution.py:345
  130.8 8.3 %copy-start.6 = (bf16[192,1536]{1,0:T(8,128)(2,1)S(1)}, bf16[192,1536]{1,0:T(8,128)(2,1)}, u32[]{:S(2)}) copy-start(bf16[192,1536]{1,0:T(8,128)(2,1)} %get-tuple-element.55.refs_2_) | copy-start | bytes 1769476
  136.7 23.1 %collective-permute-start.27 = (bf16[192,2560]{1,0:T(8,128)(2,1)}, bf16[192,2560]{1,0:T(8,128)(2,1)}, u32[]{:S(2)}, u32[]{:S(2)}) collective-permute-start(bf16[192,2560]{1,0:T(8,128)(2,1)} %get-tuple-element.67), channel_id=1, source_target_pairs={{0,8},{8,0},{16,24},{24,16},{1,9},{9,1},{17,25},{25,17},{2,10},{10... | collective-permute-start | bytes 2949128 | tf_op jit(solution)/shard_map/ppermute | solution.py:349
  136.8 3.5 %copy-start.14 = (bf16[64,2304]{1,0:T(8,128)(2,1)}, bf16[64,2304]{1,0:T(8,128)(2,1)S(1)}, u32[]{:S(2)}) copy-start(bf16[64,2304]{1,0:T(8,128)(2,1)S(1)} %constant_dynamic-update-slice_fusion.2.refs_0_) | copy-start | bytes 884740
  136.8 9.6 %collective-permute-start.19 = (bf16[64,2304]{1,0:T(8,128)(2,1)S(1)}, bf16[64,2304]{1,0:T(8,128)(2,1)}, u32[]{:S(2)}, u32[]{:S(2)}) collective-permute-start(bf16[64,2304]{1,0:T(8,128)(2,1)S(1)} %constant_dynamic-update-slice_fusion.2.refs_0_), channel_id=1, source_target_pairs={{0,1},{1,0},{2,3},{3,2},{4,5},{5,4},{6,7},{7,6},{8,9},{9,8},{10,11... | collective-permute-start | bytes 884744 | tf_op jit(solution)/shard_map/ppermute | solution.py:366
  139.1 15.4 %collective-permute-start.29 = (bf16[192,1536]{1,0:T(8,128)(2,1)S(1)}, bf16[192,1536]{1,0:T(8,128)(2,1)S(1)}, u32[]{:S(2)}, u32[]{:S(2)}) collective-permute-start(bf16[192,1536]{1,0:T(8,128)(2,1)S(1)} %copy-done.6), channel_id=1, source_target_pairs={{0,16},{8,24},{16,0},{24,8},{1,17},{9,25},{17,1},{25,9},{2,18},{10... | collective-permute-start | bytes 1769480 | tf_op jit(solution)/shard_map/ppermute | solution.py:345
  140.2 59.3 %collective-permute-start.31 = (bf16[192,2560]{1,0:T(8,128)(2,1)}, bf16[192,2560]{1,0:T(8,128)(2,1)}, u32[]{:S(2)}, u32[]{:S(2)}) collective-permute-start(bf16[192,2560]{1,0:T(8,128)(2,1)} %get-tuple-element.75), channel_id=1, source_target_pairs={{0,8},{8,0},{16,24},{24,16},{1,9},{9,1},{17,25},{25,17},{2,10},{10... | collective-permute-start | bytes 2949128 | tf_op jit(solution)/shard_map/ppermute | solution.py:349
  140.2 70.5 %all-to-all-start.2 = ((bf16[8,24,5120]{2,1,0:T(8,128)(2,1)}), bf16[8,24,5120]{2,1,0:T(8,128)(2,1)S(1)}, u32[]{:S(2)}, u32[]{:S(2)}) async-start(bf16[8,24,5120]{2,1,0:T(8,128)(2,1)} %bitcast.84), calls=%async_computation.2 | async-start | bytes 3932160 | tf_op jit(solution)/shard_map/all_to_all | solution.py:322
  150.1 2.3 %copy-start.18 = (bf16[32,2560]{1,0:T(8,128)(2,1)S(1)}, bf16[32,2560]{1,0:T(8,128)(2,1)}, u32[]{:S(2)}) copy-start(bf16[32,2560]{1,0:T(8,128)(2,1)} %get-tuple-element.60) | copy-start | bytes 491524
  152.4 11.0 %collective-permute-start.25 = (bf16[1152,320]{0,1:T(8,128)(2,1)}, bf16[1152,320]{0,1:T(8,128)(2,1)}, u32[]{:S(2)}, u32[]{:S(2)}) collective-permute-start(bf16[1152,320]{0,1:T(8,128)(2,1)} %copy.47), channel_id=1, source_target_pairs={{0,8},{8,0},{16,24},{24,16},{1,9},{9,1},{17,25},{25,17},{2,10},{10... | collective-permute-start | bytes 2211848 | tf_op jit(solution)/shard_map/ppermute | solution.py:349
  152.5 7.4 %copy-start.8 = (bf16[192,2560]{1,0:T(8,128)(2,1)S(1)}, bf16[192,2560]{1,0:T(8,128)(2,1)}, u32[]{:S(2)}) copy-start(bf16[192,2560]{1,0:T(8,128)(2,1)} %get-tuple-element.66) | copy-start | bytes 2949124
  152.5 16.1 %collective-permute-start.20 = (bf16[4,4,2560]{2,1,0:T(4,128)(2,1)S(1)}, bf16[4,4,2560]{2,1,0:T(4,128)(2,1)S(1)}, u32[]{:S(2)}, u32[]{:S(2)}) collective-permute-start(bf16[4,4,2560]{2,1,0:T(4,128)(2,1)S(1)} %squeeze.69), channel_id=1, source_target_pairs={{0,1},{1,0},{2,3},{3,2},{4,5},{5,4},{6,7},{7,6},{8,9},{9,8},{10,11... | collective-permute-start | bytes 245768 | tf_op jit(solution)/shard_map/ppermute | solution.py:366
  159.8 44.8 %collective-permute-start.30 = (bf16[640,1536]{1,0:T(8,128)(2,1)}, bf16[640,1536]{1,0:T(8,128)(2,1)}, u32[]{:S(2)}, u32[]{:S(2)}) collective-permute-start(bf16[640,1536]{1,0:T(8,128)(2,1)} %gate_up_grads.2), channel_id=1, source_target_pairs={{0,8},{8,0},{16,24},{24,16},{1,9},{9,1},{17,25},{25,17},{2,10},{10... | collective-permute-start | bytes 5898248 | tf_op jit(solution)/shard_map/ppermute | solution.py:349
  162.2 39.6 %collective-permute-start.28 = (bf16[192,2560]{1,0:T(8,128)(2,1)}, bf16[192,2560]{1,0:T(8,128)(2,1)}, u32[]{:S(2)}, u32[]{:S(2)}) collective-permute-start(bf16[192,2560]{1,0:T(8,128)(2,1)} %add_convert_fusion.2), channel_id=1, source_target_pairs={{0,16},{8,24},{16,0},{24,8},{1,17},{9,25},{17,1},{25,9},{2,18},{10... | collective-permute-start | bytes 2949128 | tf_op jit(solution)/shard_map/ppermute | solution.py:345
  165.1 3.3 %copy-start.25 = (s32[16]{0:T(128)S(1)}, s32[16]{0:T(128)}, u32[]{:S(2)}) copy-start(s32[16]{0:T(128)} %param.14) | copy-start | bytes 196
  165.1 3.3 %copy-start.36 = (f32[16]{0:T(128)S(1)}, f32[16]{0:T(128)}, u32[]{:S(2)}) copy-start(f32[16]{0:T(128)} %param.15) | copy-start | bytes 196
  167.5 28.6 %collective-permute-start.26 = (bf16[576,320]{1,0:T(8,128)(2,1)S(1)}, bf16[576,320]{1,0:T(8,128)(2,1)S(1)}, u32[]{:S(2)}, u32[]{:S(2)}) collective-permute-start(bf16[576,320]{1,0:T(8,128)(2,1)S(1)} %slice.169), channel_id=1, source_target_pairs={{0,16},{8,24},{16,0},{24,8},{1,17},{9,25},{17,1},{25,9},{2,18},{10... | collective-permute-start | bytes 1105928 | tf_op jit(solution)/shard_map/ppermute | solution.py:345
  168.6 33.2 %copy-start.9 = (bf16[192,2560]{1,0:T(8,128)(2,1)S(1)}, bf16[192,2560]{1,0:T(8,128)(2,1)}, u32[]{:S(2)}) copy-start(bf16[192,2560]{1,0:T(8,128)(2,1)} %get-tuple-element.74) | copy-start | bytes 2949124
  168.7 41.0 %collective-permute-start.21 = (bf16[2,4,2560]{2,1,0:T(4,128)(2,1)S(1)}, bf16[2,4,2560]{2,1,0:T(4,128)(2,1)S(1)}, u32[]{:S(2)}, u32[]{:S(2)}) collective-permute-start(bf16[2,4,2560]{2,1,0:T(4,128)(2,1)S(1)} %get-tuple-element.100), channel_id=1, source_target_pairs={{0,2},{1,3},{2,0},{3,1},{4,6},{5,7},{6,4},{7,5},{8,10},{9,11},{10,... | collective-permute-start | bytes 122888 | tf_op jit(solution)/shard_map/ppermute | solution.py:366
  196.0 13.7 %collective-permute-start.22 = (bf16[2,4,2560]{2,1,0:T(4,128)(2,1)S(1)}, bf16[2,4,2560]{2,1,0:T(4,128)(2,1)S(1)}, u32[]{:S(2)}, u32[]{:S(2)}) collective-permute-start(bf16[2,4,2560]{2,1,0:T(4,128)(2,1)S(1)} %get-tuple-element.101), channel_id=1, source_target_pairs={{0,4},{1,5},{2,6},{3,7},{4,0},{5,1},{6,2},{7,3},{8,12},{9,13},{10,... | collective-permute-start | bytes 122888 | tf_op jit(solution)/shard_map/ppermute | solution.py:366
  199.5 10.3 %collective-permute-start.23 = (bf16[2,4,2560]{2,1,0:T(4,128)(2,1)S(1)}, bf16[2,4,2560]{2,1,0:T(4,128)(2,1)S(1)}, u32[]{:S(2)}, u32[]{:S(2)}) collective-permute-start(bf16[2,4,2560]{2,1,0:T(4,128)(2,1)S(1)} %get-tuple-element.98), channel_id=1, source_target_pairs={{0,6},{1,7},{2,4},{3,5},{4,2},{5,3},{6,0},{7,1},{8,14},{9,15},{10,... | collective-permute-start | bytes 122888 | tf_op jit(solution)/shard_map/ppermute | solution.py:366
  204.6 5.3 %copy-start.28 = (s32[32]{0:T(128)S(1)}, s32[32]{0:T(128)}, u32[]{:S(2)}) copy-start(s32[32]{0:T(128)} %copy-done.27) | copy-start | bytes 388
  (8 other events, 6.2 us)

commit v2 on v1

--- a/solution.py
+++ b/solution.py
@@ -427,12 +427,13 @@
     send_x = mm(pick, tok_rel).astype(BF).reshape(owners, slots, width_d)
     rows_x = exchange(send_x).reshape(rows, width_d)
 
-    hot_near = jnp.concatenate(list(after(tuple(hot_near), send_x, *gu_far, *down_far)), axis=0)
+    hot_near = jnp.concatenate(list(after(tuple(hot_near), send_x)), axis=0)
     hot_ws = [hot_near] + ([swap(hot_near)] if cores == 2 else [])
     hot_x, hot_s, partial = popular_partials(selection(step), hot_recv, hot_ws, hid)
     share = depths * hot_dev
     level_in = [hop(partial[j * share : (j + 1) * share], j) for j in range(1, across)]
     if cores == 2:
+        gu_near = list(after(tuple(gu_near), rows_x))
         gu_far = gu_far + [swap(block) for block in gu_near[1:]]
     level_in = list(after(tuple(level_in), rows_s))
     level = partial[:share].astype(F32)
@@ -492,6 +493,8 @@
 
     hot_sum = hot_grads[0]
     if cores == 2:
+        hot_sum = after(hot_sum, dn_in[0])
+    if cores == 2:
         hot_sum = (hot_sum.astype(F32) + swap(hot_grads[1]).astype(F32)).astype(BF)
     hot_sum = hot_sum.reshape(chips, 3 * hid, narrow)
     hot_total = hot_sum[0].astype(F32)
@@ -502,6 +505,8 @@
     xs_last = list(after(tuple(xs_late), *hot_far, *dn_recv))
     grad_gu = gate_up_grads(xs_last, ds, 0, wide, inverse, gu_in)
 
+    if cores == 2:
+        hot_back = after(hot_back, gu_in)
     hot_back = [hot_back[0]] + [hop(hot_back[j], j * across) for j in range(1, depths)]
     hot_back = list(after(tuple(hot_back), grad_gu))
     hot_back = jnp.concatenate(hot_back).reshape(owners * few, PIECES * narrow)

time: 216 us -> 201 us (0.931)
  waiting for transfers between devices: 83.8 us -> 67.9 us
  starting transfers between devices: 45.8 us -> 53 us
  other arithmetic: 16.3 us -> 12.8 us
    ppermute x7, waiting for transfers between devices: 43.6 us -> 23.4 us  [shift(): return lax.ppermute(value, 'dp', pairs)]
    all_to_all x3, waiting for transfers between devices: 0.01 us -> 18.8 us  [exchange(): lax.all_to_all(blocks, 'expert', split_axis=0, concat_axis=0, tiled=True)]
    ppermute x16, waiting for transfers between devices: 40.2 us -> 25.7 us  [hop(): return lax.ppermute(value, 'expert', [(i, i ^ j) for i in range(owners)])]
    ppermute x16, starting transfers between devices: 26 us -> 29.3 us  [hop(): return lax.ppermute(value, 'expert', [(i, i ^ j) for i in range(owners)])]
    all_to_all x3, starting transfers between devices: 11.3 us -> 14.4 us  [exchange(): lax.all_to_all(blocks, 'expert', split_axis=0, concat_axis=0, tiled=True)]
    unnamed x78 -> x70, local copies, waits for them, and re-layouts: 3.49 us -> 6.27 us
  transfers between devices with their start and end apart: 35 -> 35, of which waited for: 7 -> 9; matrix products, arithmetic and copies ran while one was open for 18% -> 15% of each run, Pallas kernels for 17% -> 19%
where the time goes in v2:
time: 201 us; the launch traced here: 200 us
  waiting for transfers between devices  67.9 us (34%)
  starting transfers between devices  53 us (26%)
  Pallas kernels  37.2 us (19%)
  local copies, waits for them, and re-layouts  19.6 us (10%)
  other arithmetic  12.8 us (6%)
  matrix products  7.55 us (4%)
    ppermute x16, starting transfers between devices, hop(): return lax.ppermute(value, 'expert', [(i, i ^ j) for i in range(owners)])  29.3 us
    ppermute x16, waiting for transfers between devices, hop(): return lax.ppermute(value, 'expert', [(i, i ^ j) for i in range(owners)])  25.7 us
    ppermute x7, waiting for transfers between devices, shift(): return lax.ppermute(value, 'dp', pairs)  23.4 us
    all_to_all x3, waiting for transfers between devices, exchange(): lax.all_to_all(blocks, 'expert', split_axis=0, concat_axis=0, tiled=True)  18.8 us
    all_to_all x3, starting transfers between devices, exchange(): lax.all_to_all(blocks, 'expert', split_axis=0, concat_axis=0, tiled=True)  14.4 us
    pallas_call x1, Pallas kernels, expert(): pl.pallas_call(body, in_specs=[SMEM, INSIDE, INSIDE] + [ANYWHERE] * (2 *...  12.5 us
    pallas_call x2, Pallas kernels, gate_up_grads(): pl.pallas_call(body, grid=(width // step,), in_specs=[pl.BlockSpec((rows,...  9.61 us
    ppermute x7, starting transfers between devices, shift(): return lax.ppermute(value, 'dp', pairs)  7.95 us
  transfers between devices with their start and end apart: 35, of which 9 were waited for; matrix products, arithmetic and copies ran while one was open for 15% of the time, Pallas kernels for 19%

profile of v2, /device:TPU:0, one launch (start us, length us, event | category | flops | bytes accessed | tf_op | source)
XLA Modules:
  0.0 199.6 jit_solution(744935147203555819)
XLA Ops:
  0.6 1.2 pad_maximum_fusion.3
  1.8 3.0 %collective-permute-start.4 = (bf16[576,320]{1,0:T(8,128)(2,1)S(1)}, bf16[576,320]{1,0:T(8,128)(2,1)S(1)}, u32[]{:S(2)}, u32[]{:S(2)}) collective-permute-start(bf16[576,320]{1,0:T(8,128)(2,1)S(1)} %bitcast.80), channel_id=1, source_target_pairs={{0,16},{8,24},{16,0},{24,8},{1,17},{9,25},{17,1},{25,9},{2,18},{10... | collective-permute-start | bytes 1105928 | tf_op jit(solution)/shard_map/ppermute | solution.py:345
  4.9 0.7 fusion.14
  5.8 0.8 select_reduce_fusion
  6.6 0.7 multiply_add_fusion
  7.3 2.1 %convolution_convert_fusion.1 = bf16[192,2560]{1,0:T(8,128)(2,1)} fusion(bf16[128,2560]{1,0:T(8,128)(2,1)S(1)} %copy-done.3, f32[128]{0:T(128)} %bitcast.96, s32[128]{0:T(128)S(1)} %multiply_add_fusion), kind=kOutput, calls=%fused_computation.1 | convolution fusion | flops 127328256 | bytes 1639424 | tf_op jit(solution)/shard_map/dot_general | solution.py:22
  9.4 5.9 %all-to-all-start = ((bf16[8,24,2560]{2,1,0:T(8,128)(2,1)}), bf16[8,24,2560]{2,1,0:T(8,128)(2,1)S(1)}, u32[]{:S(2)}, u32[]{:S(2)}) async-start(bf16[8,24,2560]{2,1,0:T(8,128)(2,1)} %bitcast.6), calls=%async_computation | async-start | bytes 1966080 | tf_op jit(solution)/shard_map/all_to_all | solution.py:322
  16.6 2.1 %collective-permute-start = (bf16[2,4,2560]{2,1,0:T(4,128)(2,1)S(1)}, bf16[2,4,2560]{2,1,0:T(4,128)(2,1)S(1)}, u32[]{:S(2)}, u32[]{:S(2)}) collective-permute-start(bf16[2,4,2560]{2,1,0:T(4,128)(2,1)S(1)} %squeeze.62), channel_id=1, source_target_pairs={{0,2},{1,3},{2,0},{3,1},{4,6},{5,7},{6,4},{7,5},{8,10},{9,11},{10,... | collective-permute-start | bytes 122888 | tf_op jit(solution)/shard_map/ppermute | solution.py:366
  18.7 2.4 %collective-permute-start.1 = (bf16[2,4,2560]{2,1,0:T(4,128)(2,1)S(1)}, bf16[2,4,2560]{2,1,0:T(4,128)(2,1)S(1)}, u32[]{:S(2)}, u32[]{:S(2)}) collective-permute-start(bf16[2,4,2560]{2,1,0:T(4,128)(2,1)S(1)} %squeeze.63), channel_id=1, source_target_pairs={{0,4},{1,5},{2,6},{3,7},{4,0},{5,1},{6,2},{7,3},{8,12},{9,13},{10,... | collective-permute-start | bytes 122888 | tf_op jit(solution)/shard_map/ppermute | solution.py:366
  21.4 1.4 convolution_convert_fusion
  23.4 18.8 %all-to-all-done = bf16[8,24,2560]{2,1,0:T(8,128)(2,1)S(1)} async-done(((bf16[8,24,2560]{2,1,0:T(8,128)(2,1)}), bf16[8,24,2560]{2,1,0:T(8,128)(2,1)S(1)}, u32[]{:S(2)}, u32[]{:S(2)}) %all-to-all-start) | async-done | bytes 983072 | tf_op jit(solution)/shard_map/all_to_all | solution.py:322
  42.2 3.7 %all-to-all-start.1 = ((bf16[8,24,2560]{2,1,0:T(8,128)(2,1)}), bf16[8,24,2560]{2,1,0:T(8,128)(2,1)S(1)}, u32[]{:S(2)}, u32[]{:S(2)}) async-start(bf16[8,24,2560]{2,1,0:T(8,128)(2,1)} %bitcast.8), calls=%async_computation.1 | async-start | bytes 1966080 | tf_op jit(solution)/shard_map/all_to_all | solution.py:322
  46.6 0.9 pad_maximum_fusion.5
  47.6 1.1 constant_dynamic-update-slice_fusion.refs_0_.refs_2_
  48.7 1.5 copy.41
  50.2 1.8 collective-permute-start.3
  52.2 0.7 convert_element_type.103.sel_ref
  52.9 4.7 %collective-permute-done.3 = bf16[4,4,2560]{2,1,0:T(4,128)(2,1)S(1)} collective-permute-done((bf16[4,4,2560]{2,1,0:T(4,128)(2,1)S(1)}, bf16[4,4,2560]{2,1,0:T(4,128)(2,1)S(1)}, u32[]{:S(2)}, u32[]{:S(2)}) %collective-permute-start.3) | collective-permute-done | bytes 81952 | tf_op jit(solution)/shard_map/ppermute | solution.py:366
  57.7 0.7 reshape.357.in_ref
  58.4 1.3 copy.42.refs_1_.refs_3_
  59.7 3.8 %popular_partials.1 = (bf16[128,320]{1,0:T(8,128)(2,1)}, bf16[128,320]{1,0:T(8,128)(2,1)}, bf16[128,2304]{1,0:T(8,128)(2,1)}) custom-call(bf16[4,128,32]{2,1,0:T(8,128)(2,1)} %convert_element_type.103.sel_ref, bf16[32,2560]{1,0:T(8,128)(2,1)} %reshape.357.in_ref, bf16[1152,320]{1,0:T(8,128)(2,1)} %copy-done, bf16[1152,320]{1,0:T(8,128)(2,1)} %copy.42.refs_1_.refs_3_), custom_call_target="tpu_custom_call" | custom-call | flops 1 | bytes 1 | tf_op jit(solution)/shard_map/popular_partials/pallas_call | solution.py:221
  63.5 1.0 slice.125
  64.5 1.3 collective-permute-start.6
  66.8 6.3 %collective-permute-done.6 = bf16[64,2304]{1,0:T(8,128)(2,1)S(1)} collective-permute-done((bf16[64,2304]{1,0:T(8,128)(2,1)S(1)}, bf16[64,2304]{1,0:T(8,128)(2,1)S(1)}, u32[]{:S(2)}, u32[]{:S(2)}) %collective-permute-start.6) | collective-permute-done | bytes 294944 | tf_op jit(solution)/shard_map/ppermute | solution.py:366
  73.2 1.3 add_convert_fusion.5
  74.4 0.7 fusion.33
  75.1 1.3 collective-permute-start.7
  76.4 3.1 %collective-permute-done.7.refs_0_ = bf16[16,2304]{1,0:T(8,128)(2,1)S(1)} collective-permute-done((bf16[16,2304]{1,0:T(8,128)(2,1)S(1)}, bf16[16,2304]{1,0:T(8,128)(2,1)S(1)}, u32[]{:S(2)}, u32[]{:S(2)}) %collective-permute-start.7) | collective-permute-done | bytes 73760 | tf_op jit(solution)/shard_map/ppermute | solution.py:366
  79.6 5.7 %collective-permute-start.8 = (bf16[16,2304]{1,0:T(8,128)(2,1)S(1)}, bf16[16,2304]{1,0:T(8,128)(2,1)S(1)}, u32[]{:S(2)}, u32[]{:S(2)}) collective-permute-start(bf16[16,2304]{1,0:T(8,128)(2,1)S(1)} %get-tuple-element.102), channel_id=1, source_target_pairs={{0,4},{1,5},{2,6},{3,7},{4,0},{5,1},{6,2},{7,3},{8,12},{9,13},{10,... | collective-permute-start | bytes 221192 | tf_op jit(solution)/shard_map/ppermute | solution.py:366
  85.3 3.9 %collective-permute-done.8.refs_1_ = bf16[16,2304]{1,0:T(8,128)(2,1)S(1)} collective-permute-done((bf16[16,2304]{1,0:T(8,128)(2,1)S(1)}, bf16[16,2304]{1,0:T(8,128)(2,1)S(1)}, u32[]{:S(2)}, u32[]{:S(2)}) %collective-permute-start.8) | collective-permute-done | bytes 73760 | tf_op jit(solution)/shard_map/ppermute | solution.py:366
  89.2 3.5 %collective-permute-start.9 = (bf16[16,2304]{1,0:T(8,128)(2,1)S(1)}, bf16[16,2304]{1,0:T(8,128)(2,1)S(1)}, u32[]{:S(2)}, u32[]{:S(2)}) collective-permute-start(bf16[16,2304]{1,0:T(8,128)(2,1)S(1)} %get-tuple-element.100), channel_id=1, source_target_pairs={{0,6},{1,7},{2,4},{3,5},{4,2},{5,3},{6,0},{7,1},{8,14},{9,15},{10,... | collective-permute-start | bytes 221192 | tf_op jit(solution)/shard_map/ppermute | solution.py:366
  92.7 2.7 %collective-permute-done.9.refs_2_ = bf16[16,2304]{1,0:T(8,128)(2,1)S(1)} collective-permute-done((bf16[16,2304]{1,0:T(8,128)(2,1)S(1)}, bf16[16,2304]{1,0:T(8,128)(2,1)S(1)}, u32[]{:S(2)}, u32[]{:S(2)}) %collective-permute-start.9) | collective-permute-done | bytes 73760 | tf_op jit(solution)/shard_map/ppermute | solution.py:366
  95.4 0.6 copy-done.22
  96.0 1.7 popular_middle.1
  98.6 4.0 %collective-permute-start.17 = (bf16[16,2304]{1,0:T(8,128)(2,1)S(1)}, bf16[16,2304]{1,0:T(8,128)(2,1)S(1)}, u32[]{:S(2)}, u32[]{:S(2)}) collective-permute-start(bf16[16,2304]{1,0:T(8,128)(2,1)S(1)} %copy-done.17), channel_id=1, source_target_pairs={{0,4},{1,5},{2,6},{3,7},{4,0},{5,1},{6,2},{7,3},{8,12},{9,13},{10,... | collective-permute-start | bytes 221192 | tf_op jit(solution)/shard_map/ppermute | solution.py:366
  104.0 1.3 copy-done.7
  105.3 12.5 %expert.1 = (bf16[192,5120]{1,0:T(8,128)(2,1)}, bf16[192,768]{1,0:T(8,128)(2,1)}, bf16[192,1536]{1,0:T(8,128)(2,1)}) custom-call(s32[4]{0:T(128)} %pad_add_fusion.1.order_ref, bf16[192,2560]{1,0:T(8,128)(2,1)} %bitcast.73, bf16[192,2560]{1,0:T(8,128)(2,1)} %bitcast.76, bf16[640,1536]{1,0:T(8,128)(2,1)} %bitcast.19.refs_0_, ...), custom_call_target="tpu_custom_call" | custom-call | flops 1 | bytes 1 | tf_op jit(solution)/shard_map/expert/pallas_call | solution.py:115
  118.2 0.8 pad_maximum_fusion.1.refs_0_
  119.0 1.1 collective-permute-start.22
  120.1 5.8 %down_grads.1 = (bf16[192,2560]{1,0:T(8,128)(2,1)}, bf16[192,2560]{1,0:T(8,128)(2,1)}, bf16[192,2560]{1,0:T(8,128)(2,1)}, bf16[192,2560]{1,0:T(8,128)(2,1)}) custom-call(s32[4]{0:T(128)} %pad_add_fusion.1.order_ref, bf16[192,768]{1,0:T(8,128)(2,1)} %get-tuple-element.71.h_ref, bf16[192,2560]{1,0:T(8,128)(2,1)} %bitcast.74), custom_call_target="tpu_custom_call" | custom-call | flops 1 | bytes 1 | tf_op jit(solution)/shard_map/down_grads/pallas_call | solution.py:180
  126.5 0.7 copy-done.18
  127.2 3.8 %popular_back.1 = (bf16[32,2560]{1,0:T(8,128)(2,1)}, bf16[1152,320]{1,0:T(8,128)(2,1)}, bf16[1152,320]{1,0:T(8,128)(2,1)}) custom-call(bf16[4,128,32]{2,1,0:T(8,128)(2,1)} %convert_element_type.103.sel_ref, bf16[128,320]{1,0:T(8,128)(2,1)} %get-tuple-element.59.x_ref, bf16[128,320]{1,0:T(8,128)(2,1)} %get-tuple-element.60.s_ref, ...), custom_call_target="tpu_custom_call" | custom-call | flops 1 | bytes 1 | tf_op jit(solution)/shard_map/popular_back/pallas_call | solution.py:301
  131.0 2.3 %copy.47 = bf16[1152,320]{0,1:T(8,128)(2,1)} copy(bf16[1152,320]{1,0:T(8,128)(2,1)} %get-tuple-element.74) | data formatting | bytes 1474560 | tf_op jit(solution)/shard_map/popular_back/pallas_call | solution.py:301
  133.4 1.8 collective-permute-start.20
  135.2 0.8 copy-done.6
  136.0 4.5 %gate_up_grads.2 = bf16[640,1536]{1,0:T(8,128)(2,1)} custom-call(bf16[192,1280]{1,0:T(8,128)(2,1)} %pad_maximum_fusion.1.refs_0_, bf16[192,1280]{1,0:T(8,128)(2,1)} %copy-done.8, bf16[192,1536]{1,0:T(8,128)(2,1)} %get-tuple-element.61.refs_2_, bf16[192,1536]{1,0:T(8,128)(2,1)} %copy-done.6), custom_call_target="tpu_custom_call" | custom-call | flops 1 | bytes 1 | tf_op jit(solution)/shard_map/gate_up_grads/pallas_call | solution.py:152
  140.9 4.8 %all-to-all-start.2 = ((bf16[8,24,5120]{2,1,0:T(8,128)(2,1)}), bf16[8,24,5120]{2,1,0:T(8,128)(2,1)S(1)}, u32[]{:S(2)}, u32[]{:S(2)}) async-start(bf16[8,24,5120]{2,1,0:T(8,128)(2,1)} %bitcast.78), calls=%async_computation.2 | async-start | bytes 3932160 | tf_op jit(solution)/shard_map/all_to_all | solution.py:322
  145.8 0.9 copy-done.11
  146.7 1.7 copy.48
  148.5 1.5 add_convert_fusion.3
  150.0 1.0 collective-permute-start.29
  151.0 1.4 add_convert_fusion.2
  152.5 1.2 collective-permute-start.31
  153.6 9.5 %collective-permute-done.29 = bf16[576,320]{1,0:T(8,128)(2,1)S(1)} collective-permute-done((bf16[576,320]{1,0:T(8,128)(2,1)S(1)}, bf16[576,320]{1,0:T(8,128)(2,1)S(1)}, u32[]{:S(2)}, u32[]{:S(2)}) %collective-permute-start.29) | collective-permute-done | bytes 368672 | tf_op jit(solution)/shard_map/ppermute | solution.py:345
  163.2 0.7 slice.174
  164.0 0.7 slice.175
  164.7 2.1 %collective-permute-start.24 = (bf16[2,4,2560]{2,1,0:T(4,128)(2,1)S(1)}, bf16[2,4,2560]{2,1,0:T(4,128)(2,1)S(1)}, u32[]{:S(2)}, u32[]{:S(2)}) collective-permute-start(bf16[2,4,2560]{2,1,0:T(4,128)(2,1)S(1)} %get-tuple-element.107), channel_id=1, source_target_pairs={{0,2},{1,3},{2,0},{3,1},{4,6},{5,7},{6,4},{7,5},{8,10},{9,11},{10,... | collective-permute-start | bytes 122888 | tf_op jit(solution)/shard_map/ppermute | solution.py:366
  166.8 2.4 %collective-permute-start.25 = (bf16[2,4,2560]{2,1,0:T(4,128)(2,1)S(1)}, bf16[2,4,2560]{2,1,0:T(4,128)(2,1)S(1)}, u32[]{:S(2)}, u32[]{:S(2)}) collective-permute-start(bf16[2,4,2560]{2,1,0:T(4,128)(2,1)S(1)} %get-tuple-element.106), channel_id=1, source_target_pairs={{0,4},{1,5},{2,6},{3,7},{4,0},{5,1},{6,2},{7,3},{8,12},{9,13},{10,... | collective-permute-start | bytes 122888 | tf_op jit(solution)/shard_map/ppermute | solution.py:366
  169.3 13.9 %collective-permute-done.31 = bf16[192,2560]{1,0:T(8,128)(2,1)S(1)} collective-permute-done((bf16[192,2560]{1,0:T(8,128)(2,1)S(1)}, bf16[192,2560]{1,0:T(8,128)(2,1)S(1)}, u32[]{:S(2)}, u32[]{:S(2)}) %collective-permute-start.31) | collective-permute-done | bytes 983072 | tf_op jit(solution)/shard_map/ppermute | solution.py:345
  183.3 1.3 fusion.4
  184.6 5.1 %gate_up_grads.3 = bf16[640,1536]{1,0:T(8,128)(2,1)} custom-call(bf16[192,1280]{1,0:T(8,128)(2,1)} %pad_maximum_fusion.1.refs_0_, bf16[192,1280]{1,0:T(8,128)(2,1)} %copy-done.8, bf16[192,1536]{1,0:T(8,128)(2,1)} %get-tuple-element.61.refs_2_, bf16[192,1536]{1,0:T(8,128)(2,1)} %copy-done.6, bf16[640,1536]{1,0:T(8,128)(2,1)} %collective-permute-done.23.refs_4_), custom_call_target="tpu_custom_call" | custom-call | flops 1 | bytes 1 | tf_op jit(solution)/shard_map/gate_up_grads/pallas_call | solution.py:152
  189.7 4.9 %collective-permute-done.25 = bf16[2,4,2560]{2,1,0:T(4,128)(2,1)S(1)} collective-permute-done((bf16[2,4,2560]{2,1,0:T(4,128)(2,1)S(1)}, bf16[2,4,2560]{2,1,0:T(4,128)(2,1)S(1)}, u32[]{:S(2)}, u32[]{:S(2)}) %collective-permute-start.25) | collective-permute-done | bytes 40992 | tf_op jit(solution)/shard_map/ppermute | solution.py:366
  196.8 1.3 fusion.2
  198.3 1.3 fusion.1
  (156 shorter events, 10.7 us)
Async XLA Ops:
  0.6 6.6 %copy-start.3 = (bf16[128,2560]{1,0:T(8,128)(2,1)S(1)}, bf16[128,2560]{1,0:T(8,128)(2,1)}, u32[]{:S(2)}) copy-start(bf16[128,2560]{1,0:T(8,128)(2,1)} %param.11) | copy-start | bytes 1966084
  1.8 21.0 %collective-permute-start.4 = (bf16[576,320]{1,0:T(8,128)(2,1)S(1)}, bf16[576,320]{1,0:T(8,128)(2,1)S(1)}, u32[]{:S(2)}, u32[]{:S(2)}) collective-permute-start(bf16[576,320]{1,0:T(8,128)(2,1)S(1)} %bitcast.80), channel_id=1, source_target_pairs={{0,16},{8,24},{16,0},{24,8},{1,17},{9,25},{17,1},{25,9},{2,18},{10... | collective-permute-start | bytes 1105928 | tf_op jit(solution)/shard_map/ppermute | solution.py:345
  7.3 14.1 %copy-start.26 = (s32[128]{0:T(128)}, s32[128]{0:T(128)S(1)}, u32[]{:S(2)}) copy-start(s32[128]{0:T(128)S(1)} %multiply_add_fusion) | copy-start | bytes 1540
  9.4 6.0 %copy-start.4 = (bf16[128,2560]{1,0:T(8,128)(2,1)S(1)}, bf16[128,2560]{1,0:T(8,128)(2,1)}, u32[]{:S(2)}) copy-start(bf16[128,2560]{1,0:T(8,128)(2,1)} %param.10) | copy-start | bytes 1966084
  9.4 6.0 %copy-start.24 = (s32[16]{0:T(128)S(1)}, s32[16]{0:T(128)}, u32[]{:S(2)}) copy-start(s32[16]{0:T(128)} %param.14) | copy-start | bytes 196
  9.4 6.2 %copy-start.31 = (f32[16]{0:T(128)S(1)}, f32[16]{0:T(128)}, u32[]{:S(2)}) copy-start(f32[16]{0:T(128)} %param.15) | copy-start | bytes 196
  9.4 32.8 %all-to-all-start = ((bf16[8,24,2560]{2,1,0:T(8,128)(2,1)}), bf16[8,24,2560]{2,1,0:T(8,128)(2,1)S(1)}, u32[]{:S(2)}, u32[]{:S(2)}) async-start(bf16[8,24,2560]{2,1,0:T(8,128)(2,1)} %bitcast.6), calls=%async_computation | async-start | bytes 1966080 | tf_op jit(solution)/shard_map/all_to_all | solution.py:322
  15.3 1.0 copy-start.28
  16.6 29.4 %collective-permute-start = (bf16[2,4,2560]{2,1,0:T(4,128)(2,1)S(1)}, bf16[2,4,2560]{2,1,0:T(4,128)(2,1)S(1)}, u32[]{:S(2)}, u32[]{:S(2)}) collective-permute-start(bf16[2,4,2560]{2,1,0:T(4,128)(2,1)S(1)} %squeeze.62), channel_id=1, source_target_pairs={{0,2},{1,3},{2,0},{3,1},{4,6},{5,7},{6,4},{7,5},{8,10},{9,11},{10,... | collective-permute-start | bytes 122888 | tf_op jit(solution)/shard_map/ppermute | solution.py:366
  18.7 27.3 %collective-permute-start.1 = (bf16[2,4,2560]{2,1,0:T(4,128)(2,1)S(1)}, bf16[2,4,2560]{2,1,0:T(4,128)(2,1)S(1)}, u32[]{:S(2)}, u32[]{:S(2)}) collective-permute-start(bf16[2,4,2560]{2,1,0:T(4,128)(2,1)S(1)} %squeeze.63), channel_id=1, source_target_pairs={{0,4},{1,5},{2,6},{3,7},{4,0},{5,1},{6,2},{7,3},{8,12},{9,13},{10,... | collective-permute-start | bytes 122888 | tf_op jit(solution)/shard_map/ppermute | solution.py:366
  21.1 24.9 %collective-permute-start.2 = (bf16[2,4,2560]{2,1,0:T(4,128)(2,1)S(1)}, bf16[2,4,2560]{2,1,0:T(4,128)(2,1)S(1)}, u32[]{:S(2)}, u32[]{:S(2)}) collective-permute-start(bf16[2,4,2560]{2,1,0:T(4,128)(2,1)S(1)} %squeeze.64), channel_id=1, source_target_pairs={{0,6},{1,7},{2,4},{3,5},{4,2},{5,3},{6,0},{7,1},{8,14},{9,15},{10,... | collective-permute-start | bytes 122888 | tf_op jit(solution)/shard_map/ppermute | solution.py:366
  22.8 23.8 %copy-start.16 = (bf16[576,320]{1,0:T(8,128)(2,1)}, bf16[576,320]{1,0:T(8,128)(2,1)S(1)}, u32[]{:S(2)}) copy-start(bf16[576,320]{1,0:T(8,128)(2,1)S(1)} %collective-permute-done.4) | copy-start | bytes 1105924
  22.8 50.3 %collective-permute-start.10 = (bf16[640,1536]{1,0:T(8,128)(2,1)}, bf16[640,1536]{1,0:T(8,128)(2,1)}, u32[]{:S(2)}, u32[]{:S(2)}) collective-permute-start(bf16[640,1536]{1,0:T(8,128)(2,1)} %bitcast.19.refs_0_), channel_id=1, source_target_pairs={{0,16},{8,24},{16,0},{24,8},{1,17},{9,25},{17,1},{25,9},{2,18},{10... | collective-permute-start | bytes 5898248 | tf_op jit(solution)/shard_map/ppermute | solution.py:345
  42.2 5.4 %copy-start.1 = (bf16[8,24,2560]{2,1,0:T(8,128)(2,1)}, bf16[8,24,2560]{2,1,0:T(8,128)(2,1)S(1)}, u32[]{:S(2)}) copy-start(bf16[8,24,2560]{2,1,0:T(8,128)(2,1)S(1)} %all-to-all-done) | copy-start | bytes 2949124
  42.2 30.9 %all-to-all-start.1 = ((bf16[8,24,2560]{2,1,0:T(8,128)(2,1)}), bf16[8,24,2560]{2,1,0:T(8,128)(2,1)S(1)}, u32[]{:S(2)}, u32[]{:S(2)}) async-start(bf16[8,24,2560]{2,1,0:T(8,128)(2,1)} %bitcast.8), calls=%async_computation.1 | async-start | bytes 1966080 | tf_op jit(solution)/shard_map/all_to_all | solution.py:322
  48.7 9.7 %copy-start = (bf16[1152,320]{1,0:T(8,128)(2,1)}, bf16[1152,320]{1,0:T(8,128)(2,1)S(1)}, u32[]{:S(2)}) copy-start(bf16[1152,320]{1,0:T(8,128)(2,1)S(1)} %constant_dynamic-update-slice_fusion.refs_0_.refs_2_) | copy-start | bytes 2211844
  50.1 8.2 %collective-permute-start.5 = (bf16[1152,320]{0,1:T(8,128)(2,1)}, bf16[1152,320]{0,1:T(8,128)(2,1)S(1)}, u32[]{:S(2)}, u32[]{:S(2)}) collective-permute-start(bf16[1152,320]{0,1:T(8,128)(2,1)} %copy.41), channel_id=1, source_target_pairs={{0,8},{8,0},{16,24},{24,16},{1,9},{9,1},{17,25},{25,17},{2,10},{10... | collective-permute-start | bytes 2211848 | tf_op jit(solution)/shard_map/ppermute | solution.py:349
  50.2 7.4 %collective-permute-start.3 = (bf16[4,4,2560]{2,1,0:T(4,128)(2,1)S(1)}, bf16[4,4,2560]{2,1,0:T(4,128)(2,1)S(1)}, u32[]{:S(2)}, u32[]{:S(2)}) collective-permute-start(bf16[4,4,2560]{2,1,0:T(4,128)(2,1)S(1)} %get-tuple-element.112), channel_id=1, source_target_pairs={{0,1},{1,0},{2,3},{3,2},{4,5},{5,4},{6,7},{7,6},{8,9},{9,8},{10,11... | collective-permute-start | bytes 245768 | tf_op jit(solution)/shard_map/ppermute | solution.py:366
  59.7 6.1 %copy-start.13 = (bf16[1,192,2560]{2,1,0:T(8,128)(2,1)S(1)}, bf16[1,192,2560]{2,1,0:T(8,128)(2,1)}, u32[]{:S(2)}) copy-start(bf16[1,192,2560]{2,1,0:T(8,128)(2,1)} %param.17) | copy-start | bytes 2949124
  64.5 8.7 %collective-permute-start.6 = (bf16[64,2304]{1,0:T(8,128)(2,1)S(1)}, bf16[64,2304]{1,0:T(8,128)(2,1)S(1)}, u32[]{:S(2)}, u32[]{:S(2)}) collective-permute-start(bf16[64,2304]{1,0:T(8,128)(2,1)S(1)} %slice.125), channel_id=1, source_target_pairs={{0,1},{1,0},{2,3},{3,2},{4,5},{5,4},{6,7},{7,6},{8,9},{9,8},{10,11... | collective-permute-start | bytes 884744 | tf_op jit(solution)/shard_map/ppermute | solution.py:366
  65.8 36.8 %collective-permute-start.11 = (bf16[640,1536]{1,0:T(8,128)(2,1)}, bf16[640,1536]{1,0:T(8,128)(2,1)}, u32[]{:S(2)}, u32[]{:S(2)}) collective-permute-start(bf16[640,1536]{1,0:T(8,128)(2,1)} %bitcast.19.refs_0_), channel_id=1, source_target_pairs={{0,8},{8,0},{16,24},{24,16},{1,9},{9,1},{17,25},{25,17},{2,10},{10... | collective-permute-start | bytes 5898248 | tf_op jit(solution)/shard_map/ppermute | solution.py:349
  65.8 32.7 %collective-permute-start.14 = (bf16[192,2560]{1,0:T(8,128)(2,1)S(1)}, bf16[192,2560]{1,0:T(8,128)(2,1)}, u32[]{:S(2)}, u32[]{:S(2)}) collective-permute-start(bf16[192,2560]{1,0:T(8,128)(2,1)S(1)} %bitcast.83), channel_id=1, source_target_pairs={{0,8},{8,0},{16,24},{24,16},{1,9},{9,1},{17,25},{25,17},{2,10},{10... | collective-permute-start | bytes 2949128 | tf_op jit(solution)/shard_map/ppermute | solution.py:349
  66.3 31.4 %collective-permute-start.13 = (bf16[192,2560]{1,0:T(8,128)(2,1)S(1)}, bf16[192,2560]{1,0:T(8,128)(2,1)}, u32[]{:S(2)}, u32[]{:S(2)}) collective-permute-start(bf16[192,2560]{1,0:T(8,128)(2,1)S(1)} %bitcast.84), channel_id=1, source_target_pairs={{0,16},{8,24},{16,0},{24,8},{1,17},{9,25},{17,1},{25,9},{2,18},{10... | collective-permute-start | bytes 2949128 | tf_op jit(solution)/shard_map/ppermute | solution.py:345
  73.1 25.3 %copy-start.2 = (bf16[8,24,2560]{2,1,0:T(8,128)(2,1)}, bf16[8,24,2560]{2,1,0:T(8,128)(2,1)S(1)}, u32[]{:S(2)}) copy-start(bf16[8,24,2560]{2,1,0:T(8,128)(2,1)S(1)} %all-to-all-done.1) | copy-start | bytes 2949124
  73.1 30.5 %collective-permute-start.12 = (bf16[640,1536]{1,0:T(8,128)(2,1)}, bf16[640,1536]{1,0:T(8,128)(2,1)S(1)}, u32[]{:S(2)}, u32[]{:S(2)}) collective-permute-start(bf16[640,1536]{1,0:T(8,128)(2,1)} %collective-permute-done.10.refs_1_), channel_id=1, source_target_pairs={{0,8},{8,0},{16,24},{24,16},{1,9},{9,1},{17,25},{25,17},{2,10},{10... | collective-permute-start | bytes 5898248 | tf_op jit(solution)/shard_map/ppermute | solution.py:349
  75.1 4.4 %collective-permute-start.7 = (bf16[16,2304]{1,0:T(8,128)(2,1)S(1)}, bf16[16,2304]{1,0:T(8,128)(2,1)S(1)}, u32[]{:S(2)}, u32[]{:S(2)}) collective-permute-start(bf16[16,2304]{1,0:T(8,128)(2,1)S(1)} %get-tuple-element.103), channel_id=1, source_target_pairs={{0,2},{1,3},{2,0},{3,1},{4,6},{5,7},{6,4},{7,5},{8,10},{9,11},{10,... | collective-permute-start | bytes 221192 | tf_op jit(solution)/shard_map/ppermute | solution.py:366
  79.6 15.8 %copy-start.20 = (bf16[16,2304]{1,0:T(8,128)(2,1)}, bf16[16,2304]{1,0:T(8,128)(2,1)S(1)}, u32[]{:S(2)}) copy-start(bf16[16,2304]{1,0:T(8,128)(2,1)S(1)} %collective-permute-done.7.refs_0_) | copy-start | bytes 221188
  79.6 9.6 %collective-permute-start.8 = (bf16[16,2304]{1,0:T(8,128)(2,1)S(1)}, bf16[16,2304]{1,0:T(8,128)(2,1)S(1)}, u32[]{:S(2)}, u32[]{:S(2)}) collective-permute-start(bf16[16,2304]{1,0:T(8,128)(2,1)S(1)} %get-tuple-element.102), channel_id=1, source_target_pairs={{0,4},{1,5},{2,6},{3,7},{4,0},{5,1},{6,2},{7,3},{8,12},{9,13},{10,... | collective-permute-start | bytes 221192 | tf_op jit(solution)/shard_map/ppermute | solution.py:366
  89.2 6.2 %copy-start.21 = (bf16[16,2304]{1,0:T(8,128)(2,1)}, bf16[16,2304]{1,0:T(8,128)(2,1)S(1)}, u32[]{:S(2)}) copy-start(bf16[16,2304]{1,0:T(8,128)(2,1)S(1)} %collective-permute-done.8.refs_1_) | copy-start | bytes 221188
  89.2 6.2 %collective-permute-start.9 = (bf16[16,2304]{1,0:T(8,128)(2,1)S(1)}, bf16[16,2304]{1,0:T(8,128)(2,1)S(1)}, u32[]{:S(2)}, u32[]{:S(2)}) collective-permute-start(bf16[16,2304]{1,0:T(8,128)(2,1)S(1)} %get-tuple-element.100), channel_id=1, source_target_pairs={{0,6},{1,7},{2,4},{3,5},{4,2},{5,3},{6,0},{7,1},{8,14},{9,15},{10,... | collective-permute-start | bytes 221192 | tf_op jit(solution)/shard_map/ppermute | solution.py:366
  97.7 0.9 copy-start.17
  97.7 5.3 %collective-permute-start.15 = (bf16[192,2560]{1,0:T(8,128)(2,1)}, bf16[192,2560]{1,0:T(8,128)(2,1)S(1)}, u32[]{:S(2)}, u32[]{:S(2)}) collective-permute-start(bf16[192,2560]{1,0:T(8,128)(2,1)} %collective-permute-done.13.refs_5_), channel_id=1, source_target_pairs={{0,8},{8,0},{16,24},{24,16},{1,9},{9,1},{17,25},{25,17},{2,10},{10... | collective-permute-start | bytes 2949128 | tf_op jit(solution)/shard_map/ppermute | solution.py:349
  98.4 19.4 %collective-permute-start.16 = (bf16[16,2304]{1,0:T(8,128)(2,1)}, bf16[16,2304]{1,0:T(8,128)(2,1)S(1)}, u32[]{:S(2)}, u32[]{:S(2)}) collective-permute-start(bf16[16,2304]{1,0:T(8,128)(2,1)} %popular_middle.1), channel_id=1, source_target_pairs={{0,2},{1,3},{2,0},{3,1},{4,6},{5,7},{6,4},{7,5},{8,10},{9,11},{10,... | collective-permute-start | bytes 221192 | tf_op jit(solution)/shard_map/ppermute | solution.py:366
  98.6 19.2 %collective-permute-start.17 = (bf16[16,2304]{1,0:T(8,128)(2,1)S(1)}, bf16[16,2304]{1,0:T(8,128)(2,1)S(1)}, u32[]{:S(2)}, u32[]{:S(2)}) collective-permute-start(bf16[16,2304]{1,0:T(8,128)(2,1)S(1)} %copy-done.17), channel_id=1, source_target_pairs={{0,4},{1,5},{2,6},{3,7},{4,0},{5,1},{6,2},{7,3},{8,12},{9,13},{10,... | collective-permute-start | bytes 221192 | tf_op jit(solution)/shard_map/ppermute | solution.py:366
  102.6 15.2 %collective-permute-start.18 = (bf16[16,2304]{1,0:T(8,128)(2,1)S(1)}, bf16[16,2304]{1,0:T(8,128)(2,1)S(1)}, u32[]{:S(2)}, u32[]{:S(2)}) collective-permute-start(bf16[16,2304]{1,0:T(8,128)(2,1)S(1)} %copy-done.17), channel_id=1, source_target_pairs={{0,6},{1,7},{2,4},{3,5},{4,2},{5,3},{6,0},{7,1},{8,14},{9,15},{10,... | collective-permute-start | bytes 221192 | tf_op jit(solution)/shard_map/ppermute | solution.py:366
  103.0 1.0 copy-start.14
  103.0 23.5 %collective-permute-start.21 = (bf16[192,1280]{1,0:T(8,128)(2,1)S(1)}, bf16[192,1280]{1,0:T(8,128)(2,1)S(1)}, u32[]{:S(2)}, u32[]{:S(2)}) collective-permute-start(bf16[192,1280]{1,0:T(8,128)(2,1)S(1)} %pad_maximum_fusion.2), channel_id=1, source_target_pairs={{0,16},{8,24},{16,0},{24,8},{1,17},{9,25},{17,1},{25,9},{2,18},{10... | collective-permute-start | bytes 1474568 | tf_op jit(solution)/shard_map/ppermute | solution.py:345
  104.0 1.3 copy-start.7
  117.7 1.3 copy-start.5
  117.8 8.7 %copy-start.15 = (bf16[64,2304]{1,0:T(8,128)(2,1)}, bf16[64,2304]{1,0:T(8,128)(2,1)S(1)}, u32[]{:S(2)}) copy-start(bf16[64,2304]{1,0:T(8,128)(2,1)S(1)} %constant_dynamic-update-slice_fusion.2.refs_0_) | copy-start | bytes 884740
  117.9 8.6 %collective-permute-start.19 = (bf16[64,2304]{1,0:T(8,128)(2,1)S(1)}, bf16[64,2304]{1,0:T(8,128)(2,1)S(1)}, u32[]{:S(2)}, u32[]{:S(2)}) collective-permute-start(bf16[64,2304]{1,0:T(8,128)(2,1)S(1)} %constant_dynamic-update-slice_fusion.2.refs_0_), channel_id=1, source_target_pairs={{0,1},{1,0},{2,3},{3,2},{4,5},{5,4},{6,7},{7,6},{8,9},{9,8},{10,11... | collective-permute-start | bytes 884744 | tf_op jit(solution)/shard_map/ppermute | solution.py:366
  119.0 16.2 %collective-permute-start.22 = (bf16[192,1536]{1,0:T(8,128)(2,1)S(1)}, bf16[192,1536]{1,0:T(8,128)(2,1)S(1)}, u32[]{:S(2)}, u32[]{:S(2)}) collective-permute-start(bf16[192,1536]{1,0:T(8,128)(2,1)S(1)} %copy-done.5), channel_id=1, source_target_pairs={{0,16},{8,24},{16,0},{24,8},{1,17},{9,25},{17,1},{25,9},{2,18},{10... | collective-permute-start | bytes 1769480 | tf_op jit(solution)/shard_map/ppermute | solution.py:345
  126.0 19.8 %collective-permute-start.27 = (bf16[192,2560]{1,0:T(8,128)(2,1)}, bf16[192,2560]{1,0:T(8,128)(2,1)S(1)}, u32[]{:S(2)}, u32[]{:S(2)}) collective-permute-start(bf16[192,2560]{1,0:T(8,128)(2,1)} %get-tuple-element.72), channel_id=1, source_target_pairs={{0,8},{8,0},{16,24},{24,16},{1,9},{9,1},{17,25},{25,17},{2,10},{10... | collective-permute-start | bytes 2949128 | tf_op jit(solution)/shard_map/ppermute | solution.py:349
  126.0 25.0 %collective-permute-start.30 = (bf16[192,2560]{1,0:T(8,128)(2,1)}, bf16[192,2560]{1,0:T(8,128)(2,1)}, u32[]{:S(2)}, u32[]{:S(2)}) collective-permute-start(bf16[192,2560]{1,0:T(8,128)(2,1)} %get-tuple-element.76), channel_id=1, source_target_pairs={{0,8},{8,0},{16,24},{24,16},{1,9},{9,1},{17,25},{25,17},{2,10},{10... | collective-permute-start | bytes 2949128 | tf_op jit(solution)/shard_map/ppermute | solution.py:349
  126.5 4.5 %copy-start.8 = (bf16[192,1280]{1,0:T(8,128)(2,1)}, bf16[192,1280]{1,0:T(8,128)(2,1)S(1)}, u32[]{:S(2)}) copy-start(bf16[192,1280]{1,0:T(8,128)(2,1)S(1)} %collective-permute-done.21.refs_1_) | copy-start | bytes 1474564
  131.0 2.3 %copy-start.19 = (bf16[32,2560]{1,0:T(8,128)(2,1)S(1)}, bf16[32,2560]{1,0:T(8,128)(2,1)}, u32[]{:S(2)}) copy-start(bf16[32,2560]{1,0:T(8,128)(2,1)} %get-tuple-element.66) | copy-start | bytes 491524
  133.3 13.4 %collective-permute-start.28 = (bf16[1152,320]{0,1:T(8,128)(2,1)}, bf16[1152,320]{0,1:T(8,128)(2,1)}, u32[]{:S(2)}, u32[]{:S(2)}) collective-permute-start(bf16[1152,320]{0,1:T(8,128)(2,1)} %copy.47), channel_id=1, source_target_pairs={{0,8},{8,0},{16,24},{24,16},{1,9},{9,1},{17,25},{25,17},{2,10},{10... | collective-permute-start | bytes 2211848 | tf_op jit(solution)/shard_map/ppermute | solution.py:349
  133.4 7.3 %copy-start.25 = (s32[16]{0:T(128)S(1)}, s32[16]{0:T(128)}, u32[]{:S(2)}) copy-start(s32[16]{0:T(128)} %param.14) | copy-start | bytes 196
  133.4 7.3 %copy-start.32 = (f32[16]{0:T(128)S(1)}, f32[16]{0:T(128)}, u32[]{:S(2)}) copy-start(f32[16]{0:T(128)} %param.15) | copy-start | bytes 196
  133.4 12.2 %collective-permute-start.20 = (bf16[4,4,2560]{2,1,0:T(4,128)(2,1)S(1)}, bf16[4,4,2560]{2,1,0:T(4,128)(2,1)S(1)}, u32[]{:S(2)}, u32[]{:S(2)}) collective-permute-start(bf16[4,4,2560]{2,1,0:T(4,128)(2,1)S(1)} %squeeze.69), channel_id=1, source_target_pairs={{0,1},{1,0},{2,3},{3,2},{4,5},{5,4},{6,7},{7,6},{8,9},{9,8},{10,11... | collective-permute-start | bytes 245768 | tf_op jit(solution)/shard_map/ppermute | solution.py:366
  135.2 0.8 copy-start.6
  140.5 24.1 %collective-permute-start.23 = (bf16[640,1536]{1,0:T(8,128)(2,1)}, bf16[640,1536]{1,0:T(8,128)(2,1)}, u32[]{:S(2)}, u32[]{:S(2)}) collective-permute-start(bf16[640,1536]{1,0:T(8,128)(2,1)} %gate_up_grads.2), channel_id=1, source_target_pairs={{0,8},{8,0},{16,24},{24,16},{1,9},{9,1},{17,25},{25,17},{2,10},{10... | collective-permute-start | bytes 5898248 | tf_op jit(solution)/shard_map/ppermute | solution.py:349
  140.9 54.7 %all-to-all-start.2 = ((bf16[8,24,5120]{2,1,0:T(8,128)(2,1)}), bf16[8,24,5120]{2,1,0:T(8,128)(2,1)S(1)}, u32[]{:S(2)}, u32[]{:S(2)}) async-start(bf16[8,24,5120]{2,1,0:T(8,128)(2,1)} %bitcast.78), calls=%async_computation.2 | async-start | bytes 3932160 | tf_op jit(solution)/shard_map/all_to_all | solution.py:322
  145.8 0.9 copy-start.11
  148.5 2.5 %copy-start.9 = (bf16[192,2560]{1,0:T(8,128)(2,1)S(1)}, bf16[192,2560]{1,0:T(8,128)(2,1)}, u32[]{:S(2)}) copy-start(bf16[192,2560]{1,0:T(8,128)(2,1)} %get-tuple-element.75) | copy-start | bytes 2949124
  150.0 13.1 %collective-permute-start.29 = (bf16[576,320]{1,0:T(8,128)(2,1)S(1)}, bf16[576,320]{1,0:T(8,128)(2,1)S(1)}, u32[]{:S(2)}, u32[]{:S(2)}) collective-permute-start(bf16[576,320]{1,0:T(8,128)(2,1)S(1)} %slice.166), channel_id=1, source_target_pairs={{0,16},{8,24},{16,0},{24,8},{1,17},{9,25},{17,1},{25,9},{2,18},{10... | collective-permute-start | bytes 1105928 | tf_op jit(solution)/shard_map/ppermute | solution.py:345
  152.4 30.8 %copy-start.10 = (bf16[192,2560]{1,0:T(8,128)(2,1)S(1)}, bf16[192,2560]{1,0:T(8,128)(2,1)}, u32[]{:S(2)}) copy-start(bf16[192,2560]{1,0:T(8,128)(2,1)} %get-tuple-element.83) | copy-start | bytes 2949124
  152.4 30.8 %copy-start.12 = (bf16[192,2560]{1,0:T(8,128)(2,1)S(1)}, bf16[192,2560]{1,0:T(8,128)(2,1)}, u32[]{:S(2)}) copy-start(bf16[192,2560]{1,0:T(8,128)(2,1)} %copy-done.11) | copy-start | bytes 2949124
  152.5 30.8 %collective-permute-start.31 = (bf16[192,2560]{1,0:T(8,128)(2,1)S(1)}, bf16[192,2560]{1,0:T(8,128)(2,1)S(1)}, u32[]{:S(2)}, u32[]{:S(2)}) collective-permute-start(bf16[192,2560]{1,0:T(8,128)(2,1)S(1)} %add_convert_fusion.2), channel_id=1, source_target_pairs={{0,16},{8,24},{16,0},{24,8},{1,17},{9,25},{17,1},{25,9},{2,18},{10... | collective-permute-start | bytes 2949128 | tf_op jit(solution)/shard_map/ppermute | solution.py:345
  164.7 25.0 %collective-permute-start.24 = (bf16[2,4,2560]{2,1,0:T(4,128)(2,1)S(1)}, bf16[2,4,2560]{2,1,0:T(4,128)(2,1)S(1)}, u32[]{:S(2)}, u32[]{:S(2)}) collective-permute-start(bf16[2,4,2560]{2,1,0:T(4,128)(2,1)S(1)} %get-tuple-element.107), channel_id=1, source_target_pairs={{0,2},{1,3},{2,0},{3,1},{4,6},{5,7},{6,4},{7,5},{8,10},{9,11},{10,... | collective-permute-start | bytes 122888 | tf_op jit(solution)/shard_map/ppermute | solution.py:366
  166.8 27.8 %collective-permute-start.25 = (bf16[2,4,2560]{2,1,0:T(4,128)(2,1)S(1)}, bf16[2,4,2560]{2,1,0:T(4,128)(2,1)S(1)}, u32[]{:S(2)}, u32[]{:S(2)}) collective-permute-start(bf16[2,4,2560]{2,1,0:T(4,128)(2,1)S(1)} %get-tuple-element.106), channel_id=1, source_target_pairs={{0,4},{1,5},{2,6},{3,7},{4,0},{5,1},{6,2},{7,3},{8,12},{9,13},{10,... | collective-permute-start | bytes 122888 | tf_op jit(solution)/shard_map/ppermute | solution.py:366
  169.2 25.4 %collective-permute-start.26 = (bf16[2,4,2560]{2,1,0:T(4,128)(2,1)S(1)}, bf16[2,4,2560]{2,1,0:T(4,128)(2,1)S(1)}, u32[]{:S(2)}, u32[]{:S(2)}) collective-permute-start(bf16[2,4,2560]{2,1,0:T(4,128)(2,1)S(1)} %slice_bitcast_fusion.9), channel_id=1, source_target_pairs={{0,6},{1,7},{2,4},{3,5},{4,2},{5,3},{6,0},{7,1},{8,14},{9,15},{10,... | collective-permute-start | bytes 122888 | tf_op jit(solution)/shard_map/ppermute | solution.py:366
  184.6 10.2 %copy-start.29 = (s32[32]{0:T(128)S(1)}, s32[32]{0:T(128)}, u32[]{:S(2)}) copy-start(s32[32]{0:T(128)} %copy-done.28) | copy-start | bytes 388
  189.7 5.9 %copy-start.27 = (s32[128]{0:T(128)S(1)}, s32[128]{0:T(128)}, u32[]{:S(2)}) copy-start(s32[128]{0:T(128)} %copy-done.26) | copy-start | bytes 1540
  (4 other events, 2.7 us)

commit v3 on v1

--- a/solution.py
+++ b/solution.py
@@ -164,24 +164,26 @@
     )(*xs, *ds, *extra)
 
 
-def down_grads(order, hidden, rows_s, wide, count, scale):
+def down_grads(order, hidden, rows_s, wide, count, share, scale):
     rows, half = hidden.shape
     deep = half // count
     step = 512 if wide % 512 == 0 else wide
 
     def body(order_ref, h_ref, s_ref, *refs):
-        outs, scratch = refs[:count], refs[count]
+        outs, scratch = refs[:-1], refs[-1]
         scratch[...] = mm(h_ref[...], s_ref[...], TN) * scale
         for j in range(count):
             place = pl.multiple_of(order_ref[j] * deep, deep)
-            outs[j][...] = scratch[pl.ds(place, deep), :].astype(BF)
-
-    shapes = [struct(deep, wide)] * count
+            at = j % share * deep
+            block = scratch[pl.ds(place, deep), :].astype(BF)
+            outs[j // share][at : at + deep, :] = block
+
+    shapes = [struct(share * deep, wide)] * (count // share)
     return pl.pallas_call(
         body,
         grid=(wide // step,),
         in_specs=[SMEM, whole(hidden), pl.BlockSpec((rows, step), lambda i: (0, i))],
-        out_specs=[pl.BlockSpec((deep, step), lambda i: (0, i))] * count,
+        out_specs=[pl.BlockSpec((share * deep, step), lambda i: (0, i))] * (count // share),
         out_shape=shapes,
         scratch_shapes=[pltpu.VMEM((half, step), F32)],
         compiler_params=params(),
@@ -374,8 +376,6 @@
     gu_own = after(w_gate_up[0], hot_near[-1])
     gu_near = [w_gate_up[0]] + [shift(gu_own, r) for r in range(1, chips)]
     down_near = [w_down[0]] + [shift(down_own, r) for r in range(1, chips)]
-    gu_far = [swap(w_gate_up[0])] if cores == 2 else []
-    down_far = [swap(w_down[0])] if cores == 2 else []
 
     flat, pos = slot_positions(routes, owners)
     dest = flat * slots + pos
@@ -427,14 +427,16 @@
     send_x = mm(pick, tok_rel).astype(BF).reshape(owners, slots, width_d)
     rows_x = exchange(send_x).reshape(rows, width_d)
 
-    hot_near = jnp.concatenate(list(after(tuple(hot_near), send_x, *gu_far, *down_far)), axis=0)
+    hot_near = jnp.concatenate(list(after(tuple(hot_near), send_x)), axis=0)
     hot_ws = [hot_near] + ([swap(hot_near)] if cores == 2 else [])
     hot_x, hot_s, partial = popular_partials(selection(step), hot_recv, hot_ws, hid)
     share = depths * hot_dev
     level_in = [hop(partial[j * share : (j + 1) * share], j) for j in range(1, across)]
+    gu_far = down_far = []
     if cores == 2:
-        gu_far = gu_far + [swap(block) for block in gu_near[1:]]
-    level_in = list(after(tuple(level_in), rows_s))
+        gu_near = list(after(tuple(gu_near), rows_x))
+        gu_far = [swap(block) for block in gu_near[1:]]
+    level_in = list(after(tuple(level_in), rows_s, *gu_near[1:]))
     level = partial[:share].astype(F32)
     for value in level_in:
         level = level + value.astype(F32)
@@ -446,7 +448,8 @@
     line = [hot_own] + [hop(hot_own, j * across) for j in range(1, depths)]
     down_near = list(after(tuple(down_near), hot_own))
     if cores == 2:
-        down_far = down_far + [swap(block) for block in down_near[1:]]
+        gu_far = [swap(after(w_gate_up[0], hot_own))] + gu_far
+        down_far = [swap(block) for block in down_near]
     back, hidden, d_act = expert(order, rows_s, after(rows_x, hot_own), gu_near + gu_far, down_near + down_far)
 
     def columns_of(r):
@@ -469,13 +472,12 @@
         selection(step), lines, hot_x, hot_s, hot_ws, hid, inverse
     )
 
-    dn_parts = down_grads(order, hidden, rows_s, width_d, groups, inverse)
-    dn_sum = list(dn_parts[:chips])
+    deep = w_down.shape[1]
+    dn_parts = down_grads(order, hidden, rows_s, width_d, groups, chips, inverse)
+    dn_sum = dn_parts[0]
     if cores == 2:
-        dn_in = [swap(part) for part in dn_parts[chips:]]
-        dn_sum = [
-            (one.astype(F32) + two.astype(F32)).astype(BF) for one, two in zip(dn_sum, dn_in)
-        ]
+        dn_sum = (dn_sum.astype(F32) + swap(dn_parts[1]).astype(F32)).astype(BF)
+    dn_sum = [dn_sum[r * deep : (r + 1) * deep] for r in range(chips)]
     dn_total = dn_sum[0].astype(F32)
     dn_recv = [shift(dn_sum[r], -r) for r in range(1, chips)]
     for value in dn_recv:

time: 216 us -> 213 us (0.986)
  matrix products: 9.14 us -> 6.89 us
    all_to_all x3, waiting for transfers between devices: 0.01 us -> 18.9 us  [exchange(): lax.all_to_all(blocks, 'expert', split_axis=0, concat_axis=0, tiled=True)]
    ppermute x16, waiting for transfers between devices: 40.2 us -> 24.2 us  [hop(): return lax.ppermute(value, 'expert', [(i, i ^ j) for i in range(owners)])]
    unnamed x78 -> x58, local copies, waits for them, and re-layouts: 3.49 us -> 6.98 us
    ppermute x7, waiting for transfers between devices: 43.6 us -> 40.5 us  [shift(): return lax.ppermute(value, 'dp', pairs)]
    ppermute x16, starting transfers between devices: 26 us -> 23 us  [hop(): return lax.ppermute(value, 'expert', [(i, i ^ j) for i in range(owners)])]
    all_to_all x3, starting transfers between devices: 11.3 us -> 13.6 us  [exchange(): lax.all_to_all(blocks, 'expert', split_axis=0, concat_axis=0, tiled=True)]
    dot_general x9, matrix products: 9.14 us -> 6.89 us  [mm(): return lax.dot_general(a, b, dims, preferred_element_type=F32)]
  transfers between devices with their start and end apart: 35 -> 34, of which waited for: 7 -> 12; matrix products, arithmetic and copies ran while one was open for 18% -> 15% of each run, Pallas kernels for 17% -> 15%
where the time goes in v3:
time: 213 us; the launch traced here: 212 us
  waiting for transfers between devices  85 us (40%)
  starting transfers between devices  44.1 us (21%)
  Pallas kernels  37.3 us (18%)
  local copies, waits for them, and re-layouts  22.1 us (10%)
  other arithmetic  15.1 us (7%)
  matrix products  6.89 us (3%)
    ppermute x7, waiting for transfers between devices, shift(): return lax.ppermute(value, 'dp', pairs)  40.5 us
    ppermute x16, waiting for transfers between devices, hop(): return lax.ppermute(value, 'expert', [(i, i ^ j) for i in range(owners)])  24.2 us
    ppermute x16, starting transfers between devices, hop(): return lax.ppermute(value, 'expert', [(i, i ^ j) for i in range(owners)])  23 us
    all_to_all x3, waiting for transfers between devices, exchange(): lax.all_to_all(blocks, 'expert', split_axis=0, concat_axis=0, tiled=True)  18.9 us
    all_to_all x3, starting transfers between devices, exchange(): lax.all_to_all(blocks, 'expert', split_axis=0, concat_axis=0, tiled=True)  13.6 us
    pallas_call x1, Pallas kernels, expert(): pl.pallas_call(body, in_specs=[SMEM, INSIDE, INSIDE] + [ANYWHERE] * (2 *...  12.5 us
    pallas_call x2, Pallas kernels, gate_up_grads(): pl.pallas_call(body, grid=(width // step,), in_specs=[pl.BlockSpec((rows,...  9.61 us
    unnamed x58, local copies, waits for them, and re-layouts  6.98 us
  transfers between devices with their start and end apart: 34, of which 12 were waited for; matrix products, arithmetic and copies ran while one was open for 15% of the time, Pallas kernels for 15%

profile of v3, /device:TPU:0, one launch (start us, length us, event | category | flops | bytes accessed | tf_op | source)
XLA Modules:
  0.0 211.8 jit_solution(11142925631556068995)
XLA Ops:
  0.6 1.2 pad_maximum_fusion.3
  1.8 3.0 %collective-permute-start.4 = (bf16[576,320]{1,0:T(8,128)(2,1)S(1)}, bf16[576,320]{1,0:T(8,128)(2,1)S(1)}, u32[]{:S(2)}, u32[]{:S(2)}) collective-permute-start(bf16[576,320]{1,0:T(8,128)(2,1)S(1)} %bitcast.89), channel_id=1, source_target_pairs={{0,16},{8,24},{16,0},{24,8},{1,17},{9,25},{17,1},{25,9},{2,18},{10... | collective-permute-start | bytes 1105928 | tf_op jit(solution)/shard_map/ppermute | solution.py:347
  4.9 0.7 fusion.14
  5.8 0.8 select_reduce_fusion
  6.6 0.7 multiply_add_fusion
  7.4 1.4 convolution_convert_fusion
  8.7 5.9 %all-to-all-start.1 = ((bf16[8,24,2560]{2,1,0:T(8,128)(2,1)}), bf16[8,24,2560]{2,1,0:T(8,128)(2,1)S(1)}, u32[]{:S(2)}, u32[]{:S(2)}) async-start(bf16[8,24,2560]{2,1,0:T(8,128)(2,1)} %bitcast.91), calls=%async_computation.1 | async-start | bytes 1966080 | tf_op jit(solution)/shard_map/all_to_all | solution.py:324
  15.9 2.1 collective-permute-start
  18.0 2.4 %collective-permute-start.1 = (bf16[2,4,2560]{2,1,0:T(4,128)(2,1)S(1)}, bf16[2,4,2560]{2,1,0:T(4,128)(2,1)S(1)}, u32[]{:S(2)}, u32[]{:S(2)}) collective-permute-start(bf16[2,4,2560]{2,1,0:T(4,128)(2,1)S(1)} %squeeze.62), channel_id=1, source_target_pairs={{0,4},{1,5},{2,6},{3,7},{4,0},{5,1},{6,2},{7,3},{8,12},{9,13},{10,... | collective-permute-start | bytes 122888 | tf_op jit(solution)/shard_map/ppermute | solution.py:368
  20.6 1.4 convolution_convert_fusion.1
  22.7 18.9 %all-to-all-done.1 = bf16[8,24,2560]{2,1,0:T(8,128)(2,1)S(1)} async-done(((bf16[8,24,2560]{2,1,0:T(8,128)(2,1)}), bf16[8,24,2560]{2,1,0:T(8,128)(2,1)S(1)}, u32[]{:S(2)}, u32[]{:S(2)}) %all-to-all-start.1) | async-done | bytes 983072 | tf_op jit(solution)/shard_map/all_to_all | solution.py:324
  41.6 3.7 %all-to-all-start = ((bf16[8,24,2560]{2,1,0:T(8,128)(2,1)}), bf16[8,24,2560]{2,1,0:T(8,128)(2,1)S(1)}, u32[]{:S(2)}, u32[]{:S(2)}) async-start(bf16[8,24,2560]{2,1,0:T(8,128)(2,1)} %bitcast.6), calls=%async_computation | async-start | bytes 1966080 | tf_op jit(solution)/shard_map/all_to_all | solution.py:324
  45.6 1.1 constant_dynamic-update-slice_fusion.refs_0_.refs_2_
  46.6 1.4 copy.41
  48.2 1.8 collective-permute-start.3
  50.1 0.7 convert_element_type.94.sel_ref
  50.8 6.0 %collective-permute-done.3 = bf16[4,4,2560]{2,1,0:T(4,128)(2,1)S(1)} collective-permute-done((bf16[4,4,2560]{2,1,0:T(4,128)(2,1)S(1)}, bf16[4,4,2560]{2,1,0:T(4,128)(2,1)S(1)}, u32[]{:S(2)}, u32[]{:S(2)}) %collective-permute-start.3) | collective-permute-done | bytes 81952 | tf_op jit(solution)/shard_map/ppermute | solution.py:368
  57.0 0.7 reshape.357.in_ref
  57.7 2.2 %copy.42.refs_1_.refs_3_ = bf16[1152,320]{1,0:T(8,128)(2,1)} copy(bf16[1152,320]{0,1:T(8,128)(2,1)} %collective-permute-done.5) | data formatting | bytes 1474560 | tf_op jit(solution)/shard_map/ppermute | solution.py:351
  59.9 3.7 %popular_partials.1 = (bf16[128,320]{1,0:T(8,128)(2,1)}, bf16[128,320]{1,0:T(8,128)(2,1)}, bf16[128,2304]{1,0:T(8,128)(2,1)}) custom-call(bf16[4,128,32]{2,1,0:T(8,128)(2,1)} %convert_element_type.94.sel_ref, bf16[32,2560]{1,0:T(8,128)(2,1)} %reshape.357.in_ref, bf16[1152,320]{1,0:T(8,128)(2,1)} %copy-done, bf16[1152,320]{1,0:T(8,128)(2,1)} %copy.42.refs_1_.refs_3_), custom_call_target="tpu_custom_call" | custom-call | flops 1 | bytes 1 | tf_op jit(solution)/shard_map/popular_partials/pallas_call | solution.py:223
  63.6 1.0 slice.131
  65.6 6.9 %collective-permute-done.6 = bf16[64,2304]{1,0:T(8,128)(2,1)S(1)} collective-permute-done((bf16[64,2304]{1,0:T(8,128)(2,1)S(1)}, bf16[64,2304]{1,0:T(8,128)(2,1)S(1)}, u32[]{:S(2)}, u32[]{:S(2)}) %collective-permute-start.6) | collective-permute-done | bytes 294944 | tf_op jit(solution)/shard_map/ppermute | solution.py:368
  72.5 1.2 add_convert_fusion.4
  74.4 4.2 %collective-permute-start.10 = (bf16[16,2304]{1,0:T(8,128)(2,1)S(1)}, bf16[16,2304]{1,0:T(8,128)(2,1)S(1)}, u32[]{:S(2)}, u32[]{:S(2)}) collective-permute-start(bf16[16,2304]{1,0:T(8,128)(2,1)S(1)} %get-tuple-element.94), channel_id=1, source_target_pairs={{0,6},{1,7},{2,4},{3,5},{4,2},{5,3},{6,0},{7,1},{8,14},{9,15},{10,... | collective-permute-start | bytes 221192 | tf_op jit(solution)/shard_map/ppermute | solution.py:368
  79.2 1.9 collective-permute-done.10.refs_2_
  81.1 1.9 collective-permute-done.8.refs_0_
  83.0 0.9 collective-permute-done.9.refs_1_
  84.5 1.8 popular_middle.1
  86.3 2.5 %collective-permute-done.13.refs_5_ = bf16[192,2560]{1,0:T(8,128)(2,1)} collective-permute-done((bf16[192,2560]{1,0:T(8,128)(2,1)}, bf16[192,2560]{1,0:T(8,128)(2,1)}, u32[]{:S(2)}, u32[]{:S(2)}) %collective-permute-start.13) | collective-permute-done | bytes 983072 | tf_op jit(solution)/shard_map/ppermute | solution.py:347
  90.5 1.4 collective-permute-done.14.refs_6_
  91.8 1.8 collective-permute-start.17
  93.7 1.0 copy-done.14
  94.7 2.5 %collective-permute-start.18 = (bf16[16,2304]{1,0:T(8,128)(2,1)}, bf16[16,2304]{1,0:T(8,128)(2,1)S(1)}, u32[]{:S(2)}, u32[]{:S(2)}) collective-permute-start(bf16[16,2304]{1,0:T(8,128)(2,1)} %popular_middle.1), channel_id=1, source_target_pairs={{0,6},{1,7},{2,4},{3,5},{4,2},{5,3},{6,0},{7,1},{8,14},{9,15},{10,... | collective-permute-start | bytes 221192 | tf_op jit(solution)/shard_map/ppermute | solution.py:368
  97.4 1.3 copy-done.9
  98.6 1.3 copy-done.10
  99.9 12.5 %expert.1 = (bf16[192,5120]{1,0:T(8,128)(2,1)}, bf16[192,768]{1,0:T(8,128)(2,1)}, bf16[192,1536]{1,0:T(8,128)(2,1)}) custom-call(s32[4]{0:T(128)} %pad_add_fusion.1.order_ref, bf16[192,2560]{1,0:T(8,128)(2,1)} %bitcast.81, bf16[192,2560]{1,0:T(8,128)(2,1)} %bitcast.80, bf16[640,1536]{1,0:T(8,128)(2,1)} %bitcast.86, ...), custom_call_target="tpu_custom_call" | custom-call | flops 1 | bytes 1 | tf_op jit(solution)/shard_map/expert/pallas_call | solution.py:115
  112.5 5.9 %down_grads.1 = (bf16[384,2560]{1,0:T(8,128)(2,1)}, bf16[384,2560]{1,0:T(8,128)(2,1)}) custom-call(s32[4]{0:T(128)} %pad_add_fusion.1.order_ref, bf16[192,768]{1,0:T(8,128)(2,1)} %get-tuple-element.69.h_ref, bf16[192,2560]{1,0:T(8,128)(2,1)} %bitcast.82), custom_call_target="tpu_custom_call" | custom-call | flops 1 | bytes 1 | tf_op jit(solution)/shard_map/down_grads/pallas_call | solution.py:182
  118.4 1.6 collective-permute-start.19
  120.0 0.8 pad_maximum_fusion.2
  121.3 6.6 %collective-permute-done.19.refs_1_ = bf16[64,2304]{1,0:T(8,128)(2,1)S(1)} collective-permute-done((bf16[64,2304]{1,0:T(8,128)(2,1)S(1)}, bf16[64,2304]{1,0:T(8,128)(2,1)S(1)}, u32[]{:S(2)}, u32[]{:S(2)}) %collective-permute-start.19) | collective-permute-done | bytes 294944 | tf_op jit(solution)/shard_map/ppermute | solution.py:368
  127.9 0.7 copy-done.19
  128.6 3.8 %popular_back.1 = (bf16[32,2560]{1,0:T(8,128)(2,1)}, bf16[1152,320]{1,0:T(8,128)(2,1)}, bf16[1152,320]{1,0:T(8,128)(2,1)}) custom-call(bf16[4,128,32]{2,1,0:T(8,128)(2,1)} %convert_element_type.94.sel_ref, bf16[128,320]{1,0:T(8,128)(2,1)} %get-tuple-element.57.x_ref, bf16[128,320]{1,0:T(8,128)(2,1)} %get-tuple-element.58.s_ref, bf16[64,2304]{1,0:T(8,128)(2,1)} %copy-done.16, ...), custom_call_target="tpu_custom_call" | custom-call | flops 1 | bytes 1 | tf_op jit(solution)/shard_map/popular_back/pallas_call | solution.py:303
  132.4 2.3 %copy.47 = bf16[1152,320]{0,1:T(8,128)(2,1)} copy(bf16[1152,320]{1,0:T(8,128)(2,1)} %get-tuple-element.68) | data formatting | bytes 1474560 | tf_op jit(solution)/shard_map/popular_back/pallas_call | solution.py:303
  134.7 0.8 pad_maximum_fusion.1.refs_0_
  136.0 3.9 %all-to-all-start.2 = ((bf16[8,24,5120]{2,1,0:T(8,128)(2,1)}), bf16[8,24,5120]{2,1,0:T(8,128)(2,1)S(1)}, u32[]{:S(2)}, u32[]{:S(2)}) async-start(bf16[8,24,5120]{2,1,0:T(8,128)(2,1)} %bitcast.87), calls=%async_computation.2 | async-start | bytes 3932160 | tf_op jit(solution)/shard_map/all_to_all | solution.py:324
  140.1 1.8 collective-permute-start.20
  141.9 9.4 %collective-permute-done.29.refs_3_ = bf16[192,1536]{1,0:T(8,128)(2,1)S(1)} collective-permute-done((bf16[192,1536]{1,0:T(8,128)(2,1)S(1)}, bf16[192,1536]{1,0:T(8,128)(2,1)S(1)}, u32[]{:S(2)}, u32[]{:S(2)}) %collective-permute-start.29) | collective-permute-done | bytes 589856 | tf_op jit(solution)/shard_map/ppermute | solution.py:347
  151.3 0.8 copy-done.8
  152.1 4.5 %gate_up_grads.2 = bf16[640,1536]{1,0:T(8,128)(2,1)} custom-call(bf16[192,1280]{1,0:T(8,128)(2,1)} %pad_maximum_fusion.1.refs_0_, bf16[192,1280]{1,0:T(8,128)(2,1)} %collective-permute-done.24.refs_1_, bf16[192,1536]{1,0:T(8,128)(2,1)} %get-tuple-element.59.refs_2_, bf16[192,1536]{1,0:T(8,128)(2,1)} %copy-done.8), custom_call_target="tpu_custom_call" | custom-call | flops 1 | bytes 1 | tf_op jit(solution)/shard_map/gate_up_grads/pallas_call | solution.py:152
  156.6 1.7 copy.48
  158.3 2.6 %add_convert_fusion = bf16[384,2560]{1,0:T(8,128)(2,1)S(1)} fusion(bf16[384,2560]{1,0:T(8,128)(2,1)} %collective-permute-done.27, bf16[384,2560]{1,0:T(8,128)(2,1)} %get-tuple-element.70), kind=kLoop, calls=%fused_computation | loop fusion | flops 3932160 | bytes 5898240 | tf_op jit(solution)/shard_map/convert_element_type | solution.py:479
  160.9 1.0 slice.178
  163.1 0.9 copy-done.4
  163.9 1.2 collective-permute-start.26
  165.6 1.8 collective-permute-start.22
  167.4 28.4 %collective-permute-done.26 = bf16[576,320]{1,0:T(8,128)(2,1)S(1)} collective-permute-done((bf16[576,320]{1,0:T(8,128)(2,1)S(1)}, bf16[576,320]{1,0:T(8,128)(2,1)S(1)}, u32[]{:S(2)}, u32[]{:S(2)}) %collective-permute-start.26) | collective-permute-done | bytes 368672 | tf_op jit(solution)/shard_map/ppermute | solution.py:347
  195.8 1.3 collective-permute-start.23
  197.1 1.1 add_convert_fusion.3
  198.2 0.7 slice.187
  199.0 0.7 slice.188
  199.6 5.1 %gate_up_grads.3 = bf16[640,1536]{1,0:T(8,128)(2,1)} custom-call(bf16[192,1280]{1,0:T(8,128)(2,1)} %pad_maximum_fusion.1.refs_0_, bf16[192,1280]{1,0:T(8,128)(2,1)} %collective-permute-done.24.refs_1_, bf16[192,1536]{1,0:T(8,128)(2,1)} %get-tuple-element.59.refs_2_, bf16[192,1536]{1,0:T(8,128)(2,1)} %copy-done.8, ...), custom_call_target="tpu_custom_call" | custom-call | flops 1 | bytes 1 | tf_op jit(solution)/shard_map/gate_up_grads/pallas_call | solution.py:152
  205.7 2.7 %fusion.4 = bf16[1,192,2560]{2,1,0:T(8,128)(2,1)} fusion(bf16[192,2560]{1,0:T(8,128)(2,1)} %collective-permute-done.28, bf16[384,2560]{1,0:T(8,128)(2,1)} %copy-done.3), kind=kLoop, calls=%fused_computation.18 | loop fusion | flops 1966080 | bytes 2949120 | tf_op jit(solution)/shard_map/broadcast_in_dim | solution.py:542
  209.0 1.3 fusion.2
  210.5 1.3 fusion.1
  (141 shorter events, 11.7 us)
Async XLA Ops:
  0.6 6.7 %copy-start.5 = (bf16[128,2560]{1,0:T(8,128)(2,1)S(1)}, bf16[128,2560]{1,0:T(8,128)(2,1)}, u32[]{:S(2)}) copy-start(bf16[128,2560]{1,0:T(8,128)(2,1)} %param.10) | copy-start | bytes 1966084
  1.8 6.9 %copy-start.11 = (bf16[3,192,320]{2,1,0:T(8,128)(2,1)}, bf16[3,192,320]{2,1,0:T(8,128)(2,1)S(1)}, u32[]{:S(2)}) copy-start(bf16[3,192,320]{2,1,0:T(8,128)(2,1)S(1)} %pad_maximum_fusion.3) | copy-start | bytes 1105924
  1.8 20.2 %collective-permute-start.4 = (bf16[576,320]{1,0:T(8,128)(2,1)S(1)}, bf16[576,320]{1,0:T(8,128)(2,1)S(1)}, u32[]{:S(2)}, u32[]{:S(2)}) collective-permute-start(bf16[576,320]{1,0:T(8,128)(2,1)S(1)} %bitcast.89), channel_id=1, source_target_pairs={{0,16},{8,24},{16,0},{24,8},{1,17},{9,25},{17,1},{25,9},{2,18},{10... | collective-permute-start | bytes 1105928 | tf_op jit(solution)/shard_map/ppermute | solution.py:347
  7.3 7.3 %copy-start.24 = (s32[16]{0:T(128)S(1)}, s32[16]{0:T(128)}, u32[]{:S(2)}) copy-start(s32[16]{0:T(128)} %param.14) | copy-start | bytes 196
  8.7 6.2 %copy-start.6 = (bf16[128,2560]{1,0:T(8,128)(2,1)S(1)}, bf16[128,2560]{1,0:T(8,128)(2,1)}, u32[]{:S(2)}) copy-start(bf16[128,2560]{1,0:T(8,128)(2,1)} %param.11) | copy-start | bytes 1966084
  8.7 6.2 %copy-start.26 = (f32[16]{0:T(128)S(1)}, f32[16]{0:T(128)}, u32[]{:S(2)}) copy-start(f32[16]{0:T(128)} %param.15) | copy-start | bytes 196
  8.7 32.8 %all-to-all-start.1 = ((bf16[8,24,2560]{2,1,0:T(8,128)(2,1)}), bf16[8,24,2560]{2,1,0:T(8,128)(2,1)S(1)}, u32[]{:S(2)}, u32[]{:S(2)}) async-start(bf16[8,24,2560]{2,1,0:T(8,128)(2,1)} %bitcast.91), calls=%async_computation.1 | async-start | bytes 1966080 | tf_op jit(solution)/shard_map/all_to_all | solution.py:324
  14.7 5.9 %copy-start.25 = (f32[128,1]{0,1:T(1,128)S(1)}, f32[128,1]{0,1:T(1,128)}, u32[]{:S(2)}) copy-start(f32[128,1]{0,1:T(1,128)} %param.13) | copy-start | bytes 1540
  15.9 29.4 %collective-permute-start = (bf16[2,4,2560]{2,1,0:T(4,128)(2,1)S(1)}, bf16[2,4,2560]{2,1,0:T(4,128)(2,1)S(1)}, u32[]{:S(2)}, u32[]{:S(2)}) collective-permute-start(bf16[2,4,2560]{2,1,0:T(4,128)(2,1)S(1)} %squeeze.61), channel_id=1, source_target_pairs={{0,2},{1,3},{2,0},{3,1},{4,6},{5,7},{6,4},{7,5},{8,10},{9,11},{10,... | collective-permute-start | bytes 122888 | tf_op jit(solution)/shard_map/ppermute | solution.py:368
  18.0 27.3 %collective-permute-start.1 = (bf16[2,4,2560]{2,1,0:T(4,128)(2,1)S(1)}, bf16[2,4,2560]{2,1,0:T(4,128)(2,1)S(1)}, u32[]{:S(2)}, u32[]{:S(2)}) collective-permute-start(bf16[2,4,2560]{2,1,0:T(4,128)(2,1)S(1)} %squeeze.62), channel_id=1, source_target_pairs={{0,4},{1,5},{2,6},{3,7},{4,0},{5,1},{6,2},{7,3},{8,12},{9,13},{10,... | collective-permute-start | bytes 122888 | tf_op jit(solution)/shard_map/ppermute | solution.py:368
  20.5 24.9 %collective-permute-start.2 = (bf16[2,4,2560]{2,1,0:T(4,128)(2,1)S(1)}, bf16[2,4,2560]{2,1,0:T(4,128)(2,1)S(1)}, u32[]{:S(2)}, u32[]{:S(2)}) collective-permute-start(bf16[2,4,2560]{2,1,0:T(4,128)(2,1)S(1)} %squeeze.63), channel_id=1, source_target_pairs={{0,6},{1,7},{2,4},{3,5},{4,2},{5,3},{6,0},{7,1},{8,14},{9,15},{10,... | collective-permute-start | bytes 122888 | tf_op jit(solution)/shard_map/ppermute | solution.py:368
  20.6 24.9 %copy-start.12 = (bf16[3,192,320]{2,1,0:T(8,128)(2,1)S(1)}, bf16[3,192,320]{2,1,0:T(8,128)(2,1)}, u32[]{:S(2)}) copy-start(bf16[3,192,320]{2,1,0:T(8,128)(2,1)} %copy-done.11) | copy-start | bytes 1105924
  22.1 23.3 %copy-start.17 = (bf16[576,320]{1,0:T(8,128)(2,1)}, bf16[576,320]{1,0:T(8,128)(2,1)S(1)}, u32[]{:S(2)}) copy-start(bf16[576,320]{1,0:T(8,128)(2,1)S(1)} %collective-permute-done.4) | copy-start | bytes 1105924
  22.1 43.5 %collective-permute-start.7 = (bf16[640,1536]{1,0:T(8,128)(2,1)}, bf16[640,1536]{1,0:T(8,128)(2,1)}, u32[]{:S(2)}, u32[]{:S(2)}) collective-permute-start(bf16[640,1536]{1,0:T(8,128)(2,1)} %bitcast.84), channel_id=1, source_target_pairs={{0,16},{8,24},{16,0},{24,8},{1,17},{9,25},{17,1},{25,9},{2,18},{10... | collective-permute-start | bytes 5898248 | tf_op jit(solution)/shard_map/ppermute | solution.py:347
  41.6 55.7 %copy-start.1 = (bf16[8,24,2560]{2,1,0:T(8,128)(2,1)}, bf16[8,24,2560]{2,1,0:T(8,128)(2,1)S(1)}, u32[]{:S(2)}) copy-start(bf16[8,24,2560]{2,1,0:T(8,128)(2,1)S(1)} %all-to-all-done.1) | copy-start | bytes 2949124
  41.6 31.0 %all-to-all-start = ((bf16[8,24,2560]{2,1,0:T(8,128)(2,1)}), bf16[8,24,2560]{2,1,0:T(8,128)(2,1)S(1)}, u32[]{:S(2)}, u32[]{:S(2)}) async-start(bf16[8,24,2560]{2,1,0:T(8,128)(2,1)} %bitcast.6), calls=%async_computation | async-start | bytes 1966080 | tf_op jit(solution)/shard_map/all_to_all | solution.py:324
  46.6 13.2 %copy-start = (bf16[1152,320]{1,0:T(8,128)(2,1)}, bf16[1152,320]{1,0:T(8,128)(2,1)S(1)}, u32[]{:S(2)}) copy-start(bf16[1152,320]{1,0:T(8,128)(2,1)S(1)} %constant_dynamic-update-slice_fusion.refs_0_.refs_2_) | copy-start | bytes 2211844
  48.1 9.6 %collective-permute-start.5 = (bf16[1152,320]{0,1:T(8,128)(2,1)}, bf16[1152,320]{0,1:T(8,128)(2,1)}, u32[]{:S(2)}, u32[]{:S(2)}) collective-permute-start(bf16[1152,320]{0,1:T(8,128)(2,1)} %copy.41), channel_id=1, source_target_pairs={{0,8},{8,0},{16,24},{24,16},{1,9},{9,1},{17,25},{25,17},{2,10},{10... | collective-permute-start | bytes 2211848 | tf_op jit(solution)/shard_map/ppermute | solution.py:351
  48.2 8.7 %collective-permute-start.3 = (bf16[4,4,2560]{2,1,0:T(4,128)(2,1)S(1)}, bf16[4,4,2560]{2,1,0:T(4,128)(2,1)S(1)}, u32[]{:S(2)}, u32[]{:S(2)}) collective-permute-start(bf16[4,4,2560]{2,1,0:T(4,128)(2,1)S(1)} %get-tuple-element.107), channel_id=1, source_target_pairs={{0,1},{1,0},{2,3},{3,2},{4,5},{5,4},{6,7},{7,6},{8,9},{9,8},{10,11... | collective-permute-start | bytes 245768 | tf_op jit(solution)/shard_map/ppermute | solution.py:368
  64.6 7.9 %collective-permute-start.6 = (bf16[64,2304]{1,0:T(8,128)(2,1)S(1)}, bf16[64,2304]{1,0:T(8,128)(2,1)S(1)}, u32[]{:S(2)}, u32[]{:S(2)}) collective-permute-start(bf16[64,2304]{1,0:T(8,128)(2,1)S(1)} %slice.131), channel_id=1, source_target_pairs={{0,1},{1,0},{2,3},{3,2},{4,5},{5,4},{6,7},{7,6},{8,9},{9,8},{10,11... | collective-permute-start | bytes 884744 | tf_op jit(solution)/shard_map/ppermute | solution.py:368
  64.9 23.9 %collective-permute-start.13 = (bf16[192,2560]{1,0:T(8,128)(2,1)}, bf16[192,2560]{1,0:T(8,128)(2,1)}, u32[]{:S(2)}, u32[]{:S(2)}) collective-permute-start(bf16[192,2560]{1,0:T(8,128)(2,1)} %bitcast.20.refs_4_), channel_id=1, source_target_pairs={{0,16},{8,24},{16,0},{24,8},{1,17},{9,25},{17,1},{25,9},{2,18},{10... | collective-permute-start | bytes 2949128 | tf_op jit(solution)/shard_map/ppermute | solution.py:347
  72.5 24.8 %copy-start.2 = (bf16[8,24,2560]{2,1,0:T(8,128)(2,1)}, bf16[8,24,2560]{2,1,0:T(8,128)(2,1)S(1)}, u32[]{:S(2)}) copy-start(bf16[8,24,2560]{2,1,0:T(8,128)(2,1)S(1)} %all-to-all-done) | copy-start | bytes 2949124
  74.4 6.7 %collective-permute-start.10 = (bf16[16,2304]{1,0:T(8,128)(2,1)S(1)}, bf16[16,2304]{1,0:T(8,128)(2,1)S(1)}, u32[]{:S(2)}, u32[]{:S(2)}) collective-permute-start(bf16[16,2304]{1,0:T(8,128)(2,1)S(1)} %get-tuple-element.94), channel_id=1, source_target_pairs={{0,6},{1,7},{2,4},{3,5},{4,2},{5,3},{6,0},{7,1},{8,14},{9,15},{10,... | collective-permute-start | bytes 221192 | tf_op jit(solution)/shard_map/ppermute | solution.py:368
  78.6 4.4 %collective-permute-start.8 = (bf16[16,2304]{1,0:T(8,128)(2,1)S(1)}, bf16[16,2304]{1,0:T(8,128)(2,1)S(1)}, u32[]{:S(2)}, u32[]{:S(2)}) collective-permute-start(bf16[16,2304]{1,0:T(8,128)(2,1)S(1)} %get-tuple-element.97), channel_id=1, source_target_pairs={{0,2},{1,3},{2,0},{3,1},{4,6},{5,7},{6,4},{7,5},{8,10},{9,11},{10,... | collective-permute-start | bytes 221192 | tf_op jit(solution)/shard_map/ppermute | solution.py:368
  78.6 5.3 %collective-permute-start.9 = (bf16[16,2304]{1,0:T(8,128)(2,1)S(1)}, bf16[16,2304]{1,0:T(8,128)(2,1)S(1)}, u32[]{:S(2)}, u32[]{:S(2)}) collective-permute-start(bf16[16,2304]{1,0:T(8,128)(2,1)S(1)} %get-tuple-element.96), channel_id=1, source_target_pairs={{0,4},{1,5},{2,6},{3,7},{4,0},{5,1},{6,2},{7,3},{8,12},{9,13},{10,... | collective-permute-start | bytes 221192 | tf_op jit(solution)/shard_map/ppermute | solution.py:368
  79.2 18.1 %collective-permute-start.12 = (bf16[640,1536]{1,0:T(8,128)(2,1)}, bf16[640,1536]{1,0:T(8,128)(2,1)S(1)}, u32[]{:S(2)}, u32[]{:S(2)}) collective-permute-start(bf16[640,1536]{1,0:T(8,128)(2,1)} %collective-permute-done.7.refs_1_), channel_id=1, source_target_pairs={{0,8},{8,0},{16,24},{24,16},{1,9},{9,1},{17,25},{25,17},{2,10},{10... | collective-permute-start | bytes 5898248 | tf_op jit(solution)/shard_map/ppermute | solution.py:351
  81.1 2.8 %copy-start.21 = (bf16[16,2304]{1,0:T(8,128)(2,1)}, bf16[16,2304]{1,0:T(8,128)(2,1)S(1)}, u32[]{:S(2)}) copy-start(bf16[16,2304]{1,0:T(8,128)(2,1)S(1)} %collective-permute-done.10.refs_2_) | copy-start | bytes 221188
  83.0 0.9 copy-start.22
  83.9 0.6 copy-start.23
  86.3 11.1 %collective-permute-start.11 = (bf16[640,1536]{1,0:T(8,128)(2,1)}, bf16[640,1536]{1,0:T(8,128)(2,1)S(1)}, u32[]{:S(2)}, u32[]{:S(2)}) collective-permute-start(bf16[640,1536]{1,0:T(8,128)(2,1)} %bitcast.85), channel_id=1, source_target_pairs={{0,8},{8,0},{16,24},{24,16},{1,9},{9,1},{17,25},{25,17},{2,10},{10... | collective-permute-start | bytes 5898248 | tf_op jit(solution)/shard_map/ppermute | solution.py:351
  88.8 3.1 %collective-permute-start.14 = (bf16[192,2560]{1,0:T(8,128)(2,1)}, bf16[192,2560]{1,0:T(8,128)(2,1)S(1)}, u32[]{:S(2)}, u32[]{:S(2)}) collective-permute-start(bf16[192,2560]{1,0:T(8,128)(2,1)} %bitcast.20.refs_4_), channel_id=1, source_target_pairs={{0,8},{8,0},{16,24},{24,16},{1,9},{9,1},{17,25},{25,17},{2,10},{10... | collective-permute-start | bytes 2949128 | tf_op jit(solution)/shard_map/ppermute | solution.py:351
  88.8 4.9 %collective-permute-start.15 = (bf16[192,2560]{1,0:T(8,128)(2,1)}, bf16[192,2560]{1,0:T(8,128)(2,1)S(1)}, u32[]{:S(2)}, u32[]{:S(2)}) collective-permute-start(bf16[192,2560]{1,0:T(8,128)(2,1)} %collective-permute-done.13.refs_5_), channel_id=1, source_target_pairs={{0,8},{8,0},{16,24},{24,16},{1,9},{9,1},{17,25},{25,17},{2,10},{10... | collective-permute-start | bytes 2949128 | tf_op jit(solution)/shard_map/ppermute | solution.py:351
  89.9 22.5 %collective-permute-start.16 = (bf16[16,2304]{1,0:T(8,128)(2,1)}, bf16[16,2304]{1,0:T(8,128)(2,1)S(1)}, u32[]{:S(2)}, u32[]{:S(2)}) collective-permute-start(bf16[16,2304]{1,0:T(8,128)(2,1)} %popular_middle.1), channel_id=1, source_target_pairs={{0,2},{1,3},{2,0},{3,1},{4,6},{5,7},{6,4},{7,5},{8,10},{9,11},{10,... | collective-permute-start | bytes 221192 | tf_op jit(solution)/shard_map/ppermute | solution.py:368
  91.8 1.9 copy-start.13
  91.8 20.6 %collective-permute-start.17 = (bf16[16,2304]{1,0:T(8,128)(2,1)}, bf16[16,2304]{1,0:T(8,128)(2,1)S(1)}, u32[]{:S(2)}, u32[]{:S(2)}) collective-permute-start(bf16[16,2304]{1,0:T(8,128)(2,1)} %popular_middle.1), channel_id=1, source_target_pairs={{0,4},{1,5},{2,6},{3,7},{4,0},{5,1},{6,2},{7,3},{8,12},{9,13},{10,... | collective-permute-start | bytes 221192 | tf_op jit(solution)/shard_map/ppermute | solution.py:368
  93.7 1.0 copy-start.14
  94.7 17.8 %collective-permute-start.18 = (bf16[16,2304]{1,0:T(8,128)(2,1)}, bf16[16,2304]{1,0:T(8,128)(2,1)S(1)}, u32[]{:S(2)}, u32[]{:S(2)}) collective-permute-start(bf16[16,2304]{1,0:T(8,128)(2,1)} %popular_middle.1), channel_id=1, source_target_pairs={{0,6},{1,7},{2,4},{3,5},{4,2},{5,3},{6,0},{7,1},{8,14},{9,15},{10,... | collective-permute-start | bytes 221192 | tf_op jit(solution)/shard_map/ppermute | solution.py:368
  97.3 15.1 %copy-start.18 = (bf16[16,2304]{1,0:T(8,128)(2,1)S(1)}, bf16[16,2304]{1,0:T(8,128)(2,1)}, u32[]{:S(2)}) copy-start(bf16[16,2304]{1,0:T(8,128)(2,1)} %popular_middle.1) | copy-start | bytes 221188
  97.3 1.3 copy-start.9
  98.6 1.3 copy-start.10
  118.4 39.9 %collective-permute-start.27 = (bf16[384,2560]{1,0:T(8,128)(2,1)}, bf16[384,2560]{1,0:T(8,128)(2,1)}, u32[]{:S(2)}, u32[]{:S(2)}) collective-permute-start(bf16[384,2560]{1,0:T(8,128)(2,1)} %get-tuple-element.71), channel_id=1, source_target_pairs={{0,8},{8,0},{16,24},{24,16},{1,9},{9,1},{17,25},{25,17},{2,10},{10... | collective-permute-start | bytes 5898248 | tf_op jit(solution)/shard_map/ppermute | solution.py:351
  118.4 9.5 %copy-start.16 = (bf16[64,2304]{1,0:T(8,128)(2,1)}, bf16[64,2304]{1,0:T(8,128)(2,1)S(1)}, u32[]{:S(2)}) copy-start(bf16[64,2304]{1,0:T(8,128)(2,1)S(1)} %constant_dynamic-update-slice_fusion.2.refs_0_) | copy-start | bytes 884740
  118.4 9.5 %collective-permute-start.19 = (bf16[64,2304]{1,0:T(8,128)(2,1)S(1)}, bf16[64,2304]{1,0:T(8,128)(2,1)S(1)}, u32[]{:S(2)}, u32[]{:S(2)}) collective-permute-start(bf16[64,2304]{1,0:T(8,128)(2,1)S(1)} %constant_dynamic-update-slice_fusion.2.refs_0_), channel_id=1, source_target_pairs={{0,1},{1,0},{2,3},{3,2},{4,5},{5,4},{6,7},{7,6},{8,9},{9,8},{10,11... | collective-permute-start | bytes 884744 | tf_op jit(solution)/shard_map/ppermute | solution.py:368
  120.8 19.2 %collective-permute-start.24 = (bf16[192,1280]{1,0:T(8,128)(2,1)}, bf16[192,1280]{1,0:T(8,128)(2,1)}, u32[]{:S(2)}, u32[]{:S(2)}) collective-permute-start(bf16[192,1280]{1,0:T(8,128)(2,1)} %pad_maximum_fusion.2), channel_id=1, source_target_pairs={{0,16},{8,24},{16,0},{24,8},{1,17},{9,25},{17,1},{25,9},{2,18},{10... | collective-permute-start | bytes 1474568 | tf_op jit(solution)/shard_map/ppermute | solution.py:347
  127.9 0.7 copy-start.19
  132.4 3.1 %copy-start.7 = (bf16[192,1536]{1,0:T(8,128)(2,1)S(1)}, bf16[192,1536]{1,0:T(8,128)(2,1)}, u32[]{:S(2)}) copy-start(bf16[192,1536]{1,0:T(8,128)(2,1)} %get-tuple-element.59.refs_2_) | copy-start | bytes 1769476
  134.7 21.9 %collective-permute-start.25 = (bf16[1152,320]{0,1:T(8,128)(2,1)}, bf16[1152,320]{0,1:T(8,128)(2,1)}, u32[]{:S(2)}, u32[]{:S(2)}) collective-permute-start(bf16[1152,320]{0,1:T(8,128)(2,1)} %copy.47), channel_id=1, source_target_pairs={{0,8},{8,0},{16,24},{24,16},{1,9},{9,1},{17,25},{25,17},{2,10},{10... | collective-permute-start | bytes 2211848 | tf_op jit(solution)/shard_map/ppermute | solution.py:351
  135.5 15.7 %collective-permute-start.29 = (bf16[192,1536]{1,0:T(8,128)(2,1)S(1)}, bf16[192,1536]{1,0:T(8,128)(2,1)S(1)}, u32[]{:S(2)}, u32[]{:S(2)}) collective-permute-start(bf16[192,1536]{1,0:T(8,128)(2,1)S(1)} %copy-done.7), channel_id=1, source_target_pairs={{0,16},{8,24},{16,0},{24,8},{1,17},{9,25},{17,1},{25,9},{2,18},{10... | collective-permute-start | bytes 1769480 | tf_op jit(solution)/shard_map/ppermute | solution.py:347
  136.0 4.0 %copy-start.20 = (bf16[32,2560]{1,0:T(8,128)(2,1)S(1)}, bf16[32,2560]{1,0:T(8,128)(2,1)}, u32[]{:S(2)}) copy-start(bf16[32,2560]{1,0:T(8,128)(2,1)} %get-tuple-element.64) | copy-start | bytes 491524
  136.0 72.4 %all-to-all-start.2 = ((bf16[8,24,5120]{2,1,0:T(8,128)(2,1)}), bf16[8,24,5120]{2,1,0:T(8,128)(2,1)S(1)}, u32[]{:S(2)}, u32[]{:S(2)}) async-start(bf16[8,24,5120]{2,1,0:T(8,128)(2,1)} %bitcast.87), calls=%async_computation.2 | async-start | bytes 3932160 | tf_op jit(solution)/shard_map/all_to_all | solution.py:324
  140.1 25.3 %collective-permute-start.20 = (bf16[4,4,2560]{2,1,0:T(4,128)(2,1)S(1)}, bf16[4,4,2560]{2,1,0:T(4,128)(2,1)S(1)}, u32[]{:S(2)}, u32[]{:S(2)}) collective-permute-start(bf16[4,4,2560]{2,1,0:T(4,128)(2,1)S(1)} %squeeze.68), channel_id=1, source_target_pairs={{0,1},{1,0},{2,3},{3,2},{4,5},{5,4},{6,7},{7,6},{8,9},{9,8},{10,11... | collective-permute-start | bytes 245768 | tf_op jit(solution)/shard_map/ppermute | solution.py:368
  151.3 0.8 copy-start.8
  156.6 43.1 %collective-permute-start.30 = (bf16[640,1536]{1,0:T(8,128)(2,1)}, bf16[640,1536]{1,0:T(8,128)(2,1)}, u32[]{:S(2)}, u32[]{:S(2)}) collective-permute-start(bf16[640,1536]{1,0:T(8,128)(2,1)} %gate_up_grads.2), channel_id=1, source_target_pairs={{0,8},{8,0},{16,24},{24,16},{1,9},{9,1},{17,25},{25,17},{2,10},{10... | collective-permute-start | bytes 5898248 | tf_op jit(solution)/shard_map/ppermute | solution.py:351
  160.9 2.1 copy-start.3
  160.9 1.8 copy-start.15
  161.9 37.7 %collective-permute-start.28 = (bf16[192,2560]{1,0:T(8,128)(2,1)}, bf16[192,2560]{1,0:T(8,128)(2,1)}, u32[]{:S(2)}, u32[]{:S(2)}) collective-permute-start(bf16[192,2560]{1,0:T(8,128)(2,1)} %slice.178), channel_id=1, source_target_pairs={{0,16},{8,24},{16,0},{24,8},{1,17},{9,25},{17,1},{25,9},{2,18},{10... | collective-permute-start | bytes 2949128 | tf_op jit(solution)/shard_map/ppermute | solution.py:347
  163.0 0.9 copy-start.4
  163.9 31.8 %collective-permute-start.26 = (bf16[576,320]{1,0:T(8,128)(2,1)S(1)}, bf16[576,320]{1,0:T(8,128)(2,1)S(1)}, u32[]{:S(2)}, u32[]{:S(2)}) collective-permute-start(bf16[576,320]{1,0:T(8,128)(2,1)S(1)} %slice.177), channel_id=1, source_target_pairs={{0,16},{8,24},{16,0},{24,8},{1,17},{9,25},{17,1},{25,9},{2,18},{10... | collective-permute-start | bytes 1105928 | tf_op jit(solution)/shard_map/ppermute | solution.py:347
  165.5 39.3 %collective-permute-start.21 = (bf16[2,4,2560]{2,1,0:T(4,128)(2,1)S(1)}, bf16[2,4,2560]{2,1,0:T(4,128)(2,1)S(1)}, u32[]{:S(2)}, u32[]{:S(2)}) collective-permute-start(bf16[2,4,2560]{2,1,0:T(4,128)(2,1)S(1)} %get-tuple-element.102), channel_id=1, source_target_pairs={{0,2},{1,3},{2,0},{3,1},{4,6},{5,7},{6,4},{7,5},{8,10},{9,11},{10,... | collective-permute-start | bytes 122888 | tf_op jit(solution)/shard_map/ppermute | solution.py:368
  165.6 39.2 %collective-permute-start.22 = (bf16[2,4,2560]{2,1,0:T(4,128)(2,1)S(1)}, bf16[2,4,2560]{2,1,0:T(4,128)(2,1)S(1)}, u32[]{:S(2)}, u32[]{:S(2)}) collective-permute-start(bf16[2,4,2560]{2,1,0:T(4,128)(2,1)S(1)} %get-tuple-element.103), channel_id=1, source_target_pairs={{0,4},{1,5},{2,6},{3,7},{4,0},{5,1},{6,2},{7,3},{8,12},{9,13},{10,... | collective-permute-start | bytes 122888 | tf_op jit(solution)/shard_map/ppermute | solution.py:368
  195.8 9.0 %collective-permute-start.23 = (bf16[2,4,2560]{2,1,0:T(4,128)(2,1)S(1)}, bf16[2,4,2560]{2,1,0:T(4,128)(2,1)S(1)}, u32[]{:S(2)}, u32[]{:S(2)}) collective-permute-start(bf16[2,4,2560]{2,1,0:T(4,128)(2,1)S(1)} %get-tuple-element.100), channel_id=1, source_target_pairs={{0,6},{1,7},{2,4},{3,5},{4,2},{5,3},{6,0},{7,1},{8,14},{9,15},{10,... | collective-permute-start | bytes 122888 | tf_op jit(solution)/shard_map/ppermute | solution.py:368

commit v4 on v2

--- a/solution.py
+++ b/solution.py
@@ -374,8 +374,6 @@
     gu_own = after(w_gate_up[0], hot_near[-1])
     gu_near = [w_gate_up[0]] + [shift(gu_own, r) for r in range(1, chips)]
     down_near = [w_down[0]] + [shift(down_own, r) for r in range(1, chips)]
-    gu_far = [swap(w_gate_up[0])] if cores == 2 else []
-    down_far = [swap(w_down[0])] if cores == 2 else []
 
     flat, pos = slot_positions(routes, owners)
     dest = flat * slots + pos
@@ -432,10 +430,11 @@
     hot_x, hot_s, partial = popular_partials(selection(step), hot_recv, hot_ws, hid)
     share = depths * hot_dev
     level_in = [hop(partial[j * share : (j + 1) * share], j) for j in range(1, across)]
+    gu_far = down_far = []
     if cores == 2:
         gu_near = list(after(tuple(gu_near), rows_x))
-        gu_far = gu_far + [swap(block) for block in gu_near[1:]]
-    level_in = list(after(tuple(level_in), rows_s))
+        gu_far = [swap(block) for block in gu_near[1:]]
+    level_in = list(after(tuple(level_in), rows_s, *gu_near[1:]))
     level = partial[:share].astype(F32)
     for value in level_in:
         level = level + value.astype(F32)
@@ -447,7 +446,8 @@
     line = [hot_own] + [hop(hot_own, j * across) for j in range(1, depths)]
     down_near = list(after(tuple(down_near), hot_own))
     if cores == 2:
-        down_far = down_far + [swap(block) for block in down_near[1:]]
+        gu_far = [swap(after(w_gate_up[0], hot_own))] + gu_far
+        down_far = [swap(block) for block in down_near]
     back, hidden, d_act = expert(order, rows_s, after(rows_x, hot_own), gu_near + gu_far, down_near + down_far)
 
     def columns_of(r):

time: 201 us -> 192 us (0.955)
  starting transfers between devices: 53 us -> 45.7 us
    ppermute x16, starting transfers between devices: 29.3 us -> 23.3 us  [hop(): return lax.ppermute(value, 'expert', [(i, i ^ j) for i in range(owners)])]
    ppermute x7, waiting for transfers between devices: 23.4 us -> 27.3 us  [shift(): return lax.ppermute(value, 'dp', pairs)]
    ppermute x16, waiting for transfers between devices: 25.7 us -> 21.9 us  [hop(): return lax.ppermute(value, 'expert', [(i, i ^ j) for i in range(owners)])]
    unnamed x70 -> x60, local copies, waits for them, and re-layouts: 6.27 us -> 4.29 us
  transfers between devices with their start and end apart: 35 -> 35, of which waited for: 9 -> 13; matrix products, arithmetic and copies ran while one was open for 15% -> 15% of each run, Pallas kernels for 19% -> 19%
where the time goes in v4:
time: 192 us; the launch traced here: 191 us
  waiting for transfers between devices  69.5 us (36%)
  starting transfers between devices  45.7 us (24%)
  Pallas kernels  37.1 us (19%)
  local copies, waits for them, and re-layouts  17.8 us (9%)
  other arithmetic  12.6 us (7%)
  matrix products  6.89 us (4%)
    ppermute x7, waiting for transfers between devices, shift(): return lax.ppermute(value, 'dp', pairs)  27.3 us
    ppermute x16, starting transfers between devices, hop(): return lax.ppermute(value, 'expert', [(i, i ^ j) for i in range(owners)])  23.3 us
    ppermute x16, waiting for transfers between devices, hop(): return lax.ppermute(value, 'expert', [(i, i ^ j) for i in range(owners)])  21.9 us
    all_to_all x3, waiting for transfers between devices, exchange(): lax.all_to_all(blocks, 'expert', split_axis=0, concat_axis=0, tiled=True)  18.9 us
    all_to_all x3, starting transfers between devices, exchange(): lax.all_to_all(blocks, 'expert', split_axis=0, concat_axis=0, tiled=True)  13.5 us
    pallas_call x1, Pallas kernels, expert(): pl.pallas_call(body, in_specs=[SMEM, INSIDE, INSIDE] + [ANYWHERE] * (2 *...  12.5 us
    pallas_call x2, Pallas kernels, gate_up_grads(): pl.pallas_call(body, grid=(width // step,), in_specs=[pl.BlockSpec((rows,...  9.6 us
    ppermute x7, starting transfers between devices, shift(): return lax.ppermute(value, 'dp', pairs)  7.68 us
  transfers between devices with their start and end apart: 35, of which 13 were waited for; matrix products, arithmetic and copies ran while one was open for 15% of the time, Pallas kernels for 19%

profile of v4, /device:TPU:0, one launch (start us, length us, event | category | flops | bytes accessed | tf_op | source)
XLA Modules:
  0.0 190.9 jit_solution(1271226847514238385)
XLA Ops:
  0.7 1.2 pad_maximum_fusion.3
  1.8 3.0 %collective-permute-start.4 = (bf16[576,320]{1,0:T(8,128)(2,1)S(1)}, bf16[576,320]{1,0:T(8,128)(2,1)S(1)}, u32[]{:S(2)}, u32[]{:S(2)}) collective-permute-start(bf16[576,320]{1,0:T(8,128)(2,1)S(1)} %bitcast.83), channel_id=1, source_target_pairs={{0,16},{8,24},{16,0},{24,8},{1,17},{9,25},{17,1},{25,9},{2,18},{10... | collective-permute-start | bytes 1105928 | tf_op jit(solution)/shard_map/ppermute | solution.py:345
  4.9 0.7 fusion.14
  5.8 0.8 select_reduce_fusion
  6.8 1.4 convolution_convert_fusion
  8.1 5.9 %all-to-all-start.1 = ((bf16[8,24,2560]{2,1,0:T(8,128)(2,1)}), bf16[8,24,2560]{2,1,0:T(8,128)(2,1)S(1)}, u32[]{:S(2)}, u32[]{:S(2)}) async-start(bf16[8,24,2560]{2,1,0:T(8,128)(2,1)} %bitcast.85), calls=%async_computation.1 | async-start | bytes 1966080 | tf_op jit(solution)/shard_map/all_to_all | solution.py:322
  15.3 2.1 %collective-permute-start = (bf16[2,4,2560]{2,1,0:T(4,128)(2,1)S(1)}, bf16[2,4,2560]{2,1,0:T(4,128)(2,1)S(1)}, u32[]{:S(2)}, u32[]{:S(2)}) collective-permute-start(bf16[2,4,2560]{2,1,0:T(4,128)(2,1)S(1)} %squeeze.61), channel_id=1, source_target_pairs={{0,2},{1,3},{2,0},{3,1},{4,6},{5,7},{6,4},{7,5},{8,10},{9,11},{10,... | collective-permute-start | bytes 122888 | tf_op jit(solution)/shard_map/ppermute | solution.py:366
  17.4 2.4 %collective-permute-start.1 = (bf16[2,4,2560]{2,1,0:T(4,128)(2,1)S(1)}, bf16[2,4,2560]{2,1,0:T(4,128)(2,1)S(1)}, u32[]{:S(2)}, u32[]{:S(2)}) collective-permute-start(bf16[2,4,2560]{2,1,0:T(4,128)(2,1)S(1)} %squeeze.62), channel_id=1, source_target_pairs={{0,4},{1,5},{2,6},{3,7},{4,0},{5,1},{6,2},{7,3},{8,12},{9,13},{10,... | collective-permute-start | bytes 122888 | tf_op jit(solution)/shard_map/ppermute | solution.py:366
  20.0 1.4 convolution_convert_fusion.1
  22.1 18.9 %all-to-all-done.1 = bf16[8,24,2560]{2,1,0:T(8,128)(2,1)S(1)} async-done(((bf16[8,24,2560]{2,1,0:T(8,128)(2,1)}), bf16[8,24,2560]{2,1,0:T(8,128)(2,1)S(1)}, u32[]{:S(2)}, u32[]{:S(2)}) %all-to-all-start.1) | async-done | bytes 983072 | tf_op jit(solution)/shard_map/all_to_all | solution.py:322
  41.0 3.7 %all-to-all-start = ((bf16[8,24,2560]{2,1,0:T(8,128)(2,1)}), bf16[8,24,2560]{2,1,0:T(8,128)(2,1)S(1)}, u32[]{:S(2)}, u32[]{:S(2)}) async-start(bf16[8,24,2560]{2,1,0:T(8,128)(2,1)} %bitcast.6), calls=%async_computation | async-start | bytes 1966080 | tf_op jit(solution)/shard_map/all_to_all | solution.py:322
  45.0 1.1 constant_dynamic-update-slice_fusion.refs_0_.refs_2_
  46.1 1.4 copy.41
  47.6 1.8 collective-permute-start.3
  49.5 0.7 convert_element_type.103.sel_ref
  50.2 6.0 %collective-permute-done.3 = bf16[4,4,2560]{2,1,0:T(4,128)(2,1)S(1)} collective-permute-done((bf16[4,4,2560]{2,1,0:T(4,128)(2,1)S(1)}, bf16[4,4,2560]{2,1,0:T(4,128)(2,1)S(1)}, u32[]{:S(2)}, u32[]{:S(2)}) %collective-permute-start.3) | collective-permute-done | bytes 81952 | tf_op jit(solution)/shard_map/ppermute | solution.py:366
  56.4 0.7 reshape.357.in_ref
  57.1 2.2 %copy.42.refs_1_.refs_3_ = bf16[1152,320]{1,0:T(8,128)(2,1)} copy(bf16[1152,320]{0,1:T(8,128)(2,1)} %collective-permute-done.5) | data formatting | bytes 1474560 | tf_op jit(solution)/shard_map/ppermute | solution.py:349
  59.3 3.7 %popular_partials.1 = (bf16[128,320]{1,0:T(8,128)(2,1)}, bf16[128,320]{1,0:T(8,128)(2,1)}, bf16[128,2304]{1,0:T(8,128)(2,1)}) custom-call(bf16[4,128,32]{2,1,0:T(8,128)(2,1)} %convert_element_type.103.sel_ref, bf16[32,2560]{1,0:T(8,128)(2,1)} %reshape.357.in_ref, bf16[1152,320]{1,0:T(8,128)(2,1)} %copy-done, bf16[1152,320]{1,0:T(8,128)(2,1)} %copy.42.refs_1_.refs_3_), custom_call_target="tpu_custom_call" | custom-call | flops 1 | bytes 1 | tf_op jit(solution)/shard_map/popular_partials/pallas_call | solution.py:221
  63.0 1.0 slice.125
  65.0 6.9 %collective-permute-done.6 = bf16[64,2304]{1,0:T(8,128)(2,1)S(1)} collective-permute-done((bf16[64,2304]{1,0:T(8,128)(2,1)S(1)}, bf16[64,2304]{1,0:T(8,128)(2,1)S(1)}, u32[]{:S(2)}, u32[]{:S(2)}) %collective-permute-start.6) | collective-permute-done | bytes 294944 | tf_op jit(solution)/shard_map/ppermute | solution.py:366
  71.9 1.2 add_convert_fusion.5
  73.2 0.7 fusion.33
  73.8 4.2 %collective-permute-start.10 = (bf16[16,2304]{1,0:T(8,128)(2,1)S(1)}, bf16[16,2304]{1,0:T(8,128)(2,1)S(1)}, u32[]{:S(2)}, u32[]{:S(2)}) collective-permute-start(bf16[16,2304]{1,0:T(8,128)(2,1)S(1)} %get-tuple-element.102), channel_id=1, source_target_pairs={{0,6},{1,7},{2,4},{3,5},{4,2},{5,3},{6,0},{7,1},{8,14},{9,15},{10,... | collective-permute-start | bytes 221192 | tf_op jit(solution)/shard_map/ppermute | solution.py:366
  78.6 1.9 collective-permute-done.10.refs_2_
  80.5 1.9 collective-permute-done.8.refs_0_
  82.4 0.9 collective-permute-done.9.refs_1_
  83.3 0.6 copy-done.23
  83.9 1.7 popular_middle.1
  85.7 2.5 %collective-permute-done.13.refs_5_ = bf16[192,2560]{1,0:T(8,128)(2,1)} collective-permute-done((bf16[192,2560]{1,0:T(8,128)(2,1)}, bf16[192,2560]{1,0:T(8,128)(2,1)}, u32[]{:S(2)}, u32[]{:S(2)}) %collective-permute-start.13) | collective-permute-done | bytes 983072 | tf_op jit(solution)/shard_map/ppermute | solution.py:345
  90.0 1.3 collective-permute-done.14.refs_6_
  91.3 1.9 collective-permute-start.17
  93.2 2.5 %collective-permute-start.18 = (bf16[16,2304]{1,0:T(8,128)(2,1)S(1)}, bf16[16,2304]{1,0:T(8,128)(2,1)S(1)}, u32[]{:S(2)}, u32[]{:S(2)}) collective-permute-start(bf16[16,2304]{1,0:T(8,128)(2,1)S(1)} %copy-done.18), channel_id=1, source_target_pairs={{0,6},{1,7},{2,4},{3,5},{4,2},{5,3},{6,0},{7,1},{8,14},{9,15},{10,... | collective-permute-start | bytes 221192 | tf_op jit(solution)/shard_map/ppermute | solution.py:366
  95.7 0.6 collective-permute-start.21
  96.3 0.7 copy-done.7
  97.0 1.3 copy-done.8
  98.3 12.5 %expert.1 = (bf16[192,5120]{1,0:T(8,128)(2,1)}, bf16[192,768]{1,0:T(8,128)(2,1)}, bf16[192,1536]{1,0:T(8,128)(2,1)}) custom-call(s32[4]{0:T(128)} %pad_add_fusion.1.order_ref, bf16[192,2560]{1,0:T(8,128)(2,1)} %bitcast.75, bf16[192,2560]{1,0:T(8,128)(2,1)} %bitcast.74, bf16[640,1536]{1,0:T(8,128)(2,1)} %bitcast.80, ...), custom_call_target="tpu_custom_call" | custom-call | flops 1 | bytes 1 | tf_op jit(solution)/shard_map/expert/pallas_call | solution.py:115
  110.9 1.6 collective-permute-start.19
  112.5 0.8 pad_maximum_fusion.1.refs_0_
  113.3 0.8 collective-permute-start.22
  114.1 5.8 %down_grads.1 = (bf16[192,2560]{1,0:T(8,128)(2,1)}, bf16[192,2560]{1,0:T(8,128)(2,1)}, bf16[192,2560]{1,0:T(8,128)(2,1)}, bf16[192,2560]{1,0:T(8,128)(2,1)}) custom-call(s32[4]{0:T(128)} %pad_add_fusion.1.order_ref, bf16[192,768]{1,0:T(8,128)(2,1)} %get-tuple-element.73.h_ref, bf16[192,2560]{1,0:T(8,128)(2,1)} %bitcast.76), custom_call_target="tpu_custom_call" | custom-call | flops 1 | bytes 1 | tf_op jit(solution)/shard_map/down_grads/pallas_call | solution.py:180
  120.5 0.7 copy-done.19
  121.2 3.8 %popular_back.1 = (bf16[32,2560]{1,0:T(8,128)(2,1)}, bf16[1152,320]{1,0:T(8,128)(2,1)}, bf16[1152,320]{1,0:T(8,128)(2,1)}) custom-call(bf16[4,128,32]{2,1,0:T(8,128)(2,1)} %convert_element_type.103.sel_ref, bf16[128,320]{1,0:T(8,128)(2,1)} %get-tuple-element.61.x_ref, bf16[128,320]{1,0:T(8,128)(2,1)} %get-tuple-element.62.s_ref, ...), custom_call_target="tpu_custom_call" | custom-call | flops 1 | bytes 1 | tf_op jit(solution)/shard_map/popular_back/pallas_call | solution.py:301
  125.0 1.6 copy.47
  126.8 0.8 collective-permute-start.20
  128.1 0.8 copy-done.6
  128.9 4.5 %gate_up_grads.2 = bf16[640,1536]{1,0:T(8,128)(2,1)} custom-call(bf16[192,1280]{1,0:T(8,128)(2,1)} %pad_maximum_fusion.1.refs_0_, bf16[192,1280]{1,0:T(8,128)(2,1)} %copy-done.9, bf16[192,1536]{1,0:T(8,128)(2,1)} %get-tuple-element.63.refs_2_, bf16[192,1536]{1,0:T(8,128)(2,1)} %copy-done.6), custom_call_target="tpu_custom_call" | custom-call | flops 1 | bytes 1 | tf_op jit(solution)/shard_map/gate_up_grads/pallas_call | solution.py:152
  133.6 3.8 %all-to-all-start.2 = ((bf16[8,24,5120]{2,1,0:T(8,128)(2,1)}), bf16[8,24,5120]{2,1,0:T(8,128)(2,1)S(1)}, u32[]{:S(2)}, u32[]{:S(2)}) async-start(bf16[8,24,5120]{2,1,0:T(8,128)(2,1)} %bitcast.81), calls=%async_computation.2 | async-start | bytes 3932160 | tf_op jit(solution)/shard_map/all_to_all | solution.py:322
  137.6 1.7 copy.48
  139.3 1.5 add_convert_fusion.3
  140.9 0.7 collective-permute-start.29
  141.5 1.4 add_convert_fusion.2
  143.0 1.5 collective-permute-start.31
  144.5 9.4 %collective-permute-done.29 = bf16[576,320]{1,0:T(8,128)(2,1)S(1)} collective-permute-done((bf16[576,320]{1,0:T(8,128)(2,1)S(1)}, bf16[576,320]{1,0:T(8,128)(2,1)S(1)}, u32[]{:S(2)}, u32[]{:S(2)}) %collective-permute-start.29) | collective-permute-done | bytes 368672 | tf_op jit(solution)/shard_map/ppermute | solution.py:345
  154.0 0.7 slice.174
  154.7 0.7 slice.175
  155.5 1.8 collective-permute-start.24
  157.3 2.4 %collective-permute-start.25 = (bf16[2,4,2560]{2,1,0:T(4,128)(2,1)S(1)}, bf16[2,4,2560]{2,1,0:T(4,128)(2,1)S(1)}, u32[]{:S(2)}, u32[]{:S(2)}) collective-permute-start(bf16[2,4,2560]{2,1,0:T(4,128)(2,1)S(1)} %get-tuple-element.108), channel_id=1, source_target_pairs={{0,4},{1,5},{2,6},{3,7},{4,0},{5,1},{6,2},{7,3},{8,12},{9,13},{10,... | collective-permute-start | bytes 122888 | tf_op jit(solution)/shard_map/ppermute | solution.py:366
  160.0 14.6 %collective-permute-done.31 = bf16[192,2560]{1,0:T(8,128)(2,1)S(1)} collective-permute-done((bf16[192,2560]{1,0:T(8,128)(2,1)S(1)}, bf16[192,2560]{1,0:T(8,128)(2,1)S(1)}, u32[]{:S(2)}, u32[]{:S(2)}) %collective-permute-start.31) | collective-permute-done | bytes 983072 | tf_op jit(solution)/shard_map/ppermute | solution.py:345
  174.6 2.6 %fusion.4 = bf16[1,192,2560]{2,1,0:T(8,128)(2,1)} fusion(bf16[192,2560]{1,0:T(8,128)(2,1)S(1)} %collective-permute-done.31, bf16[192,2560]{1,0:T(8,128)(2,1)} %collective-permute-done.27, bf16[192,2560]{1,0:T(8,128)(2,1)S(1)} %copy-done.13), kind=kLoop, calls=%fused_computation.19 | loop fusion | flops 3932160 | bytes 3932160 | tf_op jit(solution)/shard_map/broadcast_in_dim | solution.py:545
  177.1 5.1 %gate_up_grads.3 = bf16[640,1536]{1,0:T(8,128)(2,1)} custom-call(bf16[192,1280]{1,0:T(8,128)(2,1)} %pad_maximum_fusion.1.refs_0_, bf16[192,1280]{1,0:T(8,128)(2,1)} %copy-done.9, bf16[192,1536]{1,0:T(8,128)(2,1)} %get-tuple-element.63.refs_2_, bf16[192,1536]{1,0:T(8,128)(2,1)} %copy-done.6, bf16[640,1536]{1,0:T(8,128)(2,1)} %collective-permute-done.23.refs_4_), custom_call_target="tpu_custom_call" | custom-call | flops 1 | bytes 1 | tf_op jit(solution)/shard_map/gate_up_grads/pallas_call | solution.py:152
  182.3 4.3 %collective-permute-done.25 = bf16[2,4,2560]{2,1,0:T(4,128)(2,1)S(1)} collective-permute-done((bf16[2,4,2560]{2,1,0:T(4,128)(2,1)S(1)}, bf16[2,4,2560]{2,1,0:T(4,128)(2,1)S(1)}, u32[]{:S(2)}, u32[]{:S(2)}) %collective-permute-start.25) | collective-permute-done | bytes 40992 | tf_op jit(solution)/shard_map/ppermute | solution.py:366
  188.1 1.3 fusion.2
  189.6 1.3 fusion.1
  (146 shorter events, 10.0 us)
Async XLA Ops:
  0.6 6.0 %copy-start.25 = (s32[128,1]{0,1:T(1,128)S(1)}, s32[128,1]{0,1:T(1,128)}, u32[]{:S(2)}) copy-start(s32[128,1]{0,1:T(1,128)} %param.12) | copy-start | bytes 1540
  0.6 6.0 %copy-start.3 = (bf16[128,2560]{1,0:T(8,128)(2,1)S(1)}, bf16[128,2560]{1,0:T(8,128)(2,1)}, u32[]{:S(2)}) copy-start(bf16[128,2560]{1,0:T(8,128)(2,1)} %param.10) | copy-start | bytes 1966084
  1.8 6.3 %copy-start.10 = (bf16[3,192,320]{2,1,0:T(8,128)(2,1)}, bf16[3,192,320]{2,1,0:T(8,128)(2,1)S(1)}, u32[]{:S(2)}) copy-start(bf16[3,192,320]{2,1,0:T(8,128)(2,1)S(1)} %pad_maximum_fusion.3) | copy-start | bytes 1105924
  1.8 19.6 %collective-permute-start.4 = (bf16[576,320]{1,0:T(8,128)(2,1)S(1)}, bf16[576,320]{1,0:T(8,128)(2,1)S(1)}, u32[]{:S(2)}, u32[]{:S(2)}) collective-permute-start(bf16[576,320]{1,0:T(8,128)(2,1)S(1)} %bitcast.83), channel_id=1, source_target_pairs={{0,16},{8,24},{16,0},{24,8},{1,17},{9,25},{17,1},{25,9},{2,18},{10... | collective-permute-start | bytes 1105928 | tf_op jit(solution)/shard_map/ppermute | solution.py:345
  8.1 6.0 %copy-start.24 = (s32[16]{0:T(128)S(1)}, s32[16]{0:T(128)}, u32[]{:S(2)}) copy-start(s32[16]{0:T(128)} %param.14) | copy-start | bytes 196
  8.1 6.2 %copy-start.4 = (bf16[128,2560]{1,0:T(8,128)(2,1)S(1)}, bf16[128,2560]{1,0:T(8,128)(2,1)}, u32[]{:S(2)}) copy-start(bf16[128,2560]{1,0:T(8,128)(2,1)} %param.11) | copy-start | bytes 1966084
  8.1 6.2 %copy-start.27 = (f32[16]{0:T(128)S(1)}, f32[16]{0:T(128)}, u32[]{:S(2)}) copy-start(f32[16]{0:T(128)} %param.15) | copy-start | bytes 196
  8.1 32.9 %all-to-all-start.1 = ((bf16[8,24,2560]{2,1,0:T(8,128)(2,1)}), bf16[8,24,2560]{2,1,0:T(8,128)(2,1)S(1)}, u32[]{:S(2)}, u32[]{:S(2)}) async-start(bf16[8,24,2560]{2,1,0:T(8,128)(2,1)} %bitcast.85), calls=%async_computation.1 | async-start | bytes 1966080 | tf_op jit(solution)/shard_map/all_to_all | solution.py:322
  14.6 5.4 %copy-start.26 = (f32[128,1]{0,1:T(1,128)S(1)}, f32[128,1]{0,1:T(1,128)}, u32[]{:S(2)}) copy-start(f32[128,1]{0,1:T(1,128)} %param.13) | copy-start | bytes 1540
  15.3 29.4 %collective-permute-start = (bf16[2,4,2560]{2,1,0:T(4,128)(2,1)S(1)}, bf16[2,4,2560]{2,1,0:T(4,128)(2,1)S(1)}, u32[]{:S(2)}, u32[]{:S(2)}) collective-permute-start(bf16[2,4,2560]{2,1,0:T(4,128)(2,1)S(1)} %squeeze.61), channel_id=1, source_target_pairs={{0,2},{1,3},{2,0},{3,1},{4,6},{5,7},{6,4},{7,5},{8,10},{9,11},{10,... | collective-permute-start | bytes 122888 | tf_op jit(solution)/shard_map/ppermute | solution.py:366
  17.4 27.3 %collective-permute-start.1 = (bf16[2,4,2560]{2,1,0:T(4,128)(2,1)S(1)}, bf16[2,4,2560]{2,1,0:T(4,128)(2,1)S(1)}, u32[]{:S(2)}, u32[]{:S(2)}) collective-permute-start(bf16[2,4,2560]{2,1,0:T(4,128)(2,1)S(1)} %squeeze.62), channel_id=1, source_target_pairs={{0,4},{1,5},{2,6},{3,7},{4,0},{5,1},{6,2},{7,3},{8,12},{9,13},{10,... | collective-permute-start | bytes 122888 | tf_op jit(solution)/shard_map/ppermute | solution.py:366
  19.9 24.9 %collective-permute-start.2 = (bf16[2,4,2560]{2,1,0:T(4,128)(2,1)S(1)}, bf16[2,4,2560]{2,1,0:T(4,128)(2,1)S(1)}, u32[]{:S(2)}, u32[]{:S(2)}) collective-permute-start(bf16[2,4,2560]{2,1,0:T(4,128)(2,1)S(1)} %squeeze.63), channel_id=1, source_target_pairs={{0,6},{1,7},{2,4},{3,5},{4,2},{5,3},{6,0},{7,1},{8,14},{9,15},{10,... | collective-permute-start | bytes 122888 | tf_op jit(solution)/shard_map/ppermute | solution.py:366
  21.4 23.5 %copy-start.11 = (bf16[3,192,320]{2,1,0:T(8,128)(2,1)S(1)}, bf16[3,192,320]{2,1,0:T(8,128)(2,1)}, u32[]{:S(2)}) copy-start(bf16[3,192,320]{2,1,0:T(8,128)(2,1)} %copy-done.10) | copy-start | bytes 1105924
  21.5 23.3 %copy-start.17 = (bf16[576,320]{1,0:T(8,128)(2,1)}, bf16[576,320]{1,0:T(8,128)(2,1)S(1)}, u32[]{:S(2)}) copy-start(bf16[576,320]{1,0:T(8,128)(2,1)S(1)} %collective-permute-done.4) | copy-start | bytes 1105924
  21.5 43.5 %collective-permute-start.7 = (bf16[640,1536]{1,0:T(8,128)(2,1)}, bf16[640,1536]{1,0:T(8,128)(2,1)}, u32[]{:S(2)}, u32[]{:S(2)}) collective-permute-start(bf16[640,1536]{1,0:T(8,128)(2,1)} %bitcast.78), channel_id=1, source_target_pairs={{0,16},{8,24},{16,0},{24,8},{1,17},{9,25},{17,1},{25,9},{2,18},{10... | collective-permute-start | bytes 5898248 | tf_op jit(solution)/shard_map/ppermute | solution.py:345
  41.0 48.9 %copy-start.1 = (bf16[8,24,2560]{2,1,0:T(8,128)(2,1)}, bf16[8,24,2560]{2,1,0:T(8,128)(2,1)S(1)}, u32[]{:S(2)}) copy-start(bf16[8,24,2560]{2,1,0:T(8,128)(2,1)S(1)} %all-to-all-done.1) | copy-start | bytes 2949124
  41.0 31.0 %all-to-all-start = ((bf16[8,24,2560]{2,1,0:T(8,128)(2,1)}), bf16[8,24,2560]{2,1,0:T(8,128)(2,1)S(1)}, u32[]{:S(2)}, u32[]{:S(2)}) async-start(bf16[8,24,2560]{2,1,0:T(8,128)(2,1)} %bitcast.6), calls=%async_computation | async-start | bytes 1966080 | tf_op jit(solution)/shard_map/all_to_all | solution.py:322
  46.1 11.0 %copy-start = (bf16[1152,320]{1,0:T(8,128)(2,1)}, bf16[1152,320]{1,0:T(8,128)(2,1)S(1)}, u32[]{:S(2)}) copy-start(bf16[1152,320]{1,0:T(8,128)(2,1)S(1)} %constant_dynamic-update-slice_fusion.refs_0_.refs_2_) | copy-start | bytes 2211844
  47.5 9.6 %collective-permute-start.5 = (bf16[1152,320]{0,1:T(8,128)(2,1)}, bf16[1152,320]{0,1:T(8,128)(2,1)}, u32[]{:S(2)}, u32[]{:S(2)}) collective-permute-start(bf16[1152,320]{0,1:T(8,128)(2,1)} %copy.41), channel_id=1, source_target_pairs={{0,8},{8,0},{16,24},{24,16},{1,9},{9,1},{17,25},{25,17},{2,10},{10... | collective-permute-start | bytes 2211848 | tf_op jit(solution)/shard_map/ppermute | solution.py:349
  47.6 8.7 %collective-permute-start.3 = (bf16[4,4,2560]{2,1,0:T(4,128)(2,1)S(1)}, bf16[4,4,2560]{2,1,0:T(4,128)(2,1)S(1)}, u32[]{:S(2)}, u32[]{:S(2)}) collective-permute-start(bf16[4,4,2560]{2,1,0:T(4,128)(2,1)S(1)} %get-tuple-element.114), channel_id=1, source_target_pairs={{0,1},{1,0},{2,3},{3,2},{4,5},{5,4},{6,7},{7,6},{8,9},{9,8},{10,11... | collective-permute-start | bytes 245768 | tf_op jit(solution)/shard_map/ppermute | solution.py:366
  64.0 8.0 %collective-permute-start.6 = (bf16[64,2304]{1,0:T(8,128)(2,1)S(1)}, bf16[64,2304]{1,0:T(8,128)(2,1)S(1)}, u32[]{:S(2)}, u32[]{:S(2)}) collective-permute-start(bf16[64,2304]{1,0:T(8,128)(2,1)S(1)} %slice.125), channel_id=1, source_target_pairs={{0,1},{1,0},{2,3},{3,2},{4,5},{5,4},{6,7},{7,6},{8,9},{9,8},{10,11... | collective-permute-start | bytes 884744 | tf_op jit(solution)/shard_map/ppermute | solution.py:366
  64.3 23.9 %collective-permute-start.13 = (bf16[192,2560]{1,0:T(8,128)(2,1)}, bf16[192,2560]{1,0:T(8,128)(2,1)}, u32[]{:S(2)}, u32[]{:S(2)}) collective-permute-start(bf16[192,2560]{1,0:T(8,128)(2,1)} %bitcast.20.refs_4_), channel_id=1, source_target_pairs={{0,16},{8,24},{16,0},{24,8},{1,17},{9,25},{17,1},{25,9},{2,18},{10... | collective-permute-start | bytes 2949128 | tf_op jit(solution)/shard_map/ppermute | solution.py:345
  71.9 18.0 %copy-start.2 = (bf16[8,24,2560]{2,1,0:T(8,128)(2,1)}, bf16[8,24,2560]{2,1,0:T(8,128)(2,1)S(1)}, u32[]{:S(2)}) copy-start(bf16[8,24,2560]{2,1,0:T(8,128)(2,1)S(1)} %all-to-all-done) | copy-start | bytes 2949124
  73.8 6.7 %collective-permute-start.10 = (bf16[16,2304]{1,0:T(8,128)(2,1)S(1)}, bf16[16,2304]{1,0:T(8,128)(2,1)S(1)}, u32[]{:S(2)}, u32[]{:S(2)}) collective-permute-start(bf16[16,2304]{1,0:T(8,128)(2,1)S(1)} %get-tuple-element.102), channel_id=1, source_target_pairs={{0,6},{1,7},{2,4},{3,5},{4,2},{5,3},{6,0},{7,1},{8,14},{9,15},{10,... | collective-permute-start | bytes 221192 | tf_op jit(solution)/shard_map/ppermute | solution.py:366
  78.0 4.4 %collective-permute-start.8 = (bf16[16,2304]{1,0:T(8,128)(2,1)S(1)}, bf16[16,2304]{1,0:T(8,128)(2,1)S(1)}, u32[]{:S(2)}, u32[]{:S(2)}) collective-permute-start(bf16[16,2304]{1,0:T(8,128)(2,1)S(1)} %get-tuple-element.105), channel_id=1, source_target_pairs={{0,2},{1,3},{2,0},{3,1},{4,6},{5,7},{6,4},{7,5},{8,10},{9,11},{10,... | collective-permute-start | bytes 221192 | tf_op jit(solution)/shard_map/ppermute | solution.py:366
  78.0 5.3 %collective-permute-start.9 = (bf16[16,2304]{1,0:T(8,128)(2,1)S(1)}, bf16[16,2304]{1,0:T(8,128)(2,1)S(1)}, u32[]{:S(2)}, u32[]{:S(2)}) collective-permute-start(bf16[16,2304]{1,0:T(8,128)(2,1)S(1)} %get-tuple-element.104), channel_id=1, source_target_pairs={{0,4},{1,5},{2,6},{3,7},{4,0},{5,1},{6,2},{7,3},{8,12},{9,13},{10,... | collective-permute-start | bytes 221192 | tf_op jit(solution)/shard_map/ppermute | solution.py:366
  78.6 17.1 %collective-permute-start.12 = (bf16[640,1536]{1,0:T(8,128)(2,1)}, bf16[640,1536]{1,0:T(8,128)(2,1)S(1)}, u32[]{:S(2)}, u32[]{:S(2)}) collective-permute-start(bf16[640,1536]{1,0:T(8,128)(2,1)} %collective-permute-done.7.refs_1_), channel_id=1, source_target_pairs={{0,8},{8,0},{16,24},{24,16},{1,9},{9,1},{17,25},{25,17},{2,10},{10... | collective-permute-start | bytes 5898248 | tf_op jit(solution)/shard_map/ppermute | solution.py:349
  80.5 2.8 %copy-start.21 = (bf16[16,2304]{1,0:T(8,128)(2,1)}, bf16[16,2304]{1,0:T(8,128)(2,1)S(1)}, u32[]{:S(2)}) copy-start(bf16[16,2304]{1,0:T(8,128)(2,1)S(1)} %collective-permute-done.10.refs_2_) | copy-start | bytes 221188
  82.4 0.9 copy-start.22
  83.3 0.6 copy-start.23
  85.7 5.6 %copy-start.18 = (bf16[16,2304]{1,0:T(8,128)(2,1)S(1)}, bf16[16,2304]{1,0:T(8,128)(2,1)}, u32[]{:S(2)}) copy-start(bf16[16,2304]{1,0:T(8,128)(2,1)} %popular_middle.1) | copy-start | bytes 221188
  85.7 10.7 %collective-permute-start.11 = (bf16[640,1536]{1,0:T(8,128)(2,1)}, bf16[640,1536]{1,0:T(8,128)(2,1)S(1)}, u32[]{:S(2)}, u32[]{:S(2)}) collective-permute-start(bf16[640,1536]{1,0:T(8,128)(2,1)} %bitcast.79), channel_id=1, source_target_pairs={{0,8},{8,0},{16,24},{24,16},{1,9},{9,1},{17,25},{25,17},{2,10},{10... | collective-permute-start | bytes 5898248 | tf_op jit(solution)/shard_map/ppermute | solution.py:349
  88.2 3.1 %collective-permute-start.14 = (bf16[192,2560]{1,0:T(8,128)(2,1)}, bf16[192,2560]{1,0:T(8,128)(2,1)S(1)}, u32[]{:S(2)}, u32[]{:S(2)}) collective-permute-start(bf16[192,2560]{1,0:T(8,128)(2,1)} %bitcast.20.refs_4_), channel_id=1, source_target_pairs={{0,8},{8,0},{16,24},{24,16},{1,9},{9,1},{17,25},{25,17},{2,10},{10... | collective-permute-start | bytes 2949128 | tf_op jit(solution)/shard_map/ppermute | solution.py:349
  88.2 4.9 %collective-permute-start.15 = (bf16[192,2560]{1,0:T(8,128)(2,1)}, bf16[192,2560]{1,0:T(8,128)(2,1)S(1)}, u32[]{:S(2)}, u32[]{:S(2)}) collective-permute-start(bf16[192,2560]{1,0:T(8,128)(2,1)} %collective-permute-done.13.refs_5_), channel_id=1, source_target_pairs={{0,8},{8,0},{16,24},{24,16},{1,9},{9,1},{17,25},{25,17},{2,10},{10... | collective-permute-start | bytes 2949128 | tf_op jit(solution)/shard_map/ppermute | solution.py:349
  89.3 21.5 %collective-permute-start.16 = (bf16[16,2304]{1,0:T(8,128)(2,1)}, bf16[16,2304]{1,0:T(8,128)(2,1)S(1)}, u32[]{:S(2)}, u32[]{:S(2)}) collective-permute-start(bf16[16,2304]{1,0:T(8,128)(2,1)} %popular_middle.1), channel_id=1, source_target_pairs={{0,2},{1,3},{2,0},{3,1},{4,6},{5,7},{6,4},{7,5},{8,10},{9,11},{10,... | collective-permute-start | bytes 221192 | tf_op jit(solution)/shard_map/ppermute | solution.py:366
  91.3 4.4 %copy-start.14 = (bf16[192,2560]{1,0:T(8,128)(2,1)}, bf16[192,2560]{1,0:T(8,128)(2,1)S(1)}, u32[]{:S(2)}) copy-start(bf16[192,2560]{1,0:T(8,128)(2,1)S(1)} %collective-permute-done.14.refs_6_) | copy-start | bytes 2949124
  91.3 19.5 %collective-permute-start.17 = (bf16[16,2304]{1,0:T(8,128)(2,1)S(1)}, bf16[16,2304]{1,0:T(8,128)(2,1)S(1)}, u32[]{:S(2)}, u32[]{:S(2)}) collective-permute-start(bf16[16,2304]{1,0:T(8,128)(2,1)S(1)} %copy-done.18), channel_id=1, source_target_pairs={{0,4},{1,5},{2,6},{3,7},{4,0},{5,1},{6,2},{7,3},{8,12},{9,13},{10,... | collective-permute-start | bytes 221192 | tf_op jit(solution)/shard_map/ppermute | solution.py:366
  93.2 3.2 %copy-start.15 = (bf16[192,2560]{1,0:T(8,128)(2,1)}, bf16[192,2560]{1,0:T(8,128)(2,1)S(1)}, u32[]{:S(2)}) copy-start(bf16[192,2560]{1,0:T(8,128)(2,1)S(1)} %collective-permute-done.15.refs_7_) | copy-start | bytes 2949124
  93.2 17.7 %collective-permute-start.18 = (bf16[16,2304]{1,0:T(8,128)(2,1)S(1)}, bf16[16,2304]{1,0:T(8,128)(2,1)S(1)}, u32[]{:S(2)}, u32[]{:S(2)}) collective-permute-start(bf16[16,2304]{1,0:T(8,128)(2,1)S(1)} %copy-done.18), channel_id=1, source_target_pairs={{0,6},{1,7},{2,4},{3,5},{4,2},{5,3},{6,0},{7,1},{8,14},{9,15},{10,... | collective-permute-start | bytes 221192 | tf_op jit(solution)/shard_map/ppermute | solution.py:366
  95.7 1.3 copy-start.7
  95.7 24.7 %collective-permute-start.21 = (bf16[192,1280]{1,0:T(8,128)(2,1)S(1)}, bf16[192,1280]{1,0:T(8,128)(2,1)S(1)}, u32[]{:S(2)}, u32[]{:S(2)}) collective-permute-start(bf16[192,1280]{1,0:T(8,128)(2,1)S(1)} %pad_maximum_fusion.2), channel_id=1, source_target_pairs={{0,16},{8,24},{16,0},{24,8},{1,17},{9,25},{17,1},{25,9},{2,18},{10... | collective-permute-start | bytes 1474568 | tf_op jit(solution)/shard_map/ppermute | solution.py:345
  97.0 1.3 copy-start.8
  110.8 2.5 %copy-start.5 = (bf16[192,1536]{1,0:T(8,128)(2,1)S(1)}, bf16[192,1536]{1,0:T(8,128)(2,1)}, u32[]{:S(2)}) copy-start(bf16[192,1536]{1,0:T(8,128)(2,1)} %get-tuple-element.63.refs_2_) | copy-start | bytes 1769476
  110.9 9.6 %copy-start.16 = (bf16[64,2304]{1,0:T(8,128)(2,1)}, bf16[64,2304]{1,0:T(8,128)(2,1)S(1)}, u32[]{:S(2)}) copy-start(bf16[64,2304]{1,0:T(8,128)(2,1)S(1)} %constant_dynamic-update-slice_fusion.2.refs_0_) | copy-start | bytes 884740
  110.9 9.5 %collective-permute-start.19 = (bf16[64,2304]{1,0:T(8,128)(2,1)S(1)}, bf16[64,2304]{1,0:T(8,128)(2,1)S(1)}, u32[]{:S(2)}, u32[]{:S(2)}) collective-permute-start(bf16[64,2304]{1,0:T(8,128)(2,1)S(1)} %constant_dynamic-update-slice_fusion.2.refs_0_), channel_id=1, source_target_pairs={{0,1},{1,0},{2,3},{3,2},{4,5},{5,4},{6,7},{7,6},{8,9},{9,8},{10,11... | collective-permute-start | bytes 884744 | tf_op jit(solution)/shard_map/ppermute | solution.py:366
  113.3 14.8 %collective-permute-start.22 = (bf16[192,1536]{1,0:T(8,128)(2,1)S(1)}, bf16[192,1536]{1,0:T(8,128)(2,1)S(1)}, u32[]{:S(2)}, u32[]{:S(2)}) collective-permute-start(bf16[192,1536]{1,0:T(8,128)(2,1)S(1)} %copy-done.5), channel_id=1, source_target_pairs={{0,16},{8,24},{16,0},{24,8},{1,17},{9,25},{17,1},{25,9},{2,18},{10... | collective-permute-start | bytes 1769480 | tf_op jit(solution)/shard_map/ppermute | solution.py:345
  119.9 17.6 %collective-permute-start.27 = (bf16[192,2560]{1,0:T(8,128)(2,1)}, bf16[192,2560]{1,0:T(8,128)(2,1)}, u32[]{:S(2)}, u32[]{:S(2)}) collective-permute-start(bf16[192,2560]{1,0:T(8,128)(2,1)} %get-tuple-element.74), channel_id=1, source_target_pairs={{0,8},{8,0},{16,24},{24,16},{1,9},{9,1},{17,25},{25,17},{2,10},{10... | collective-permute-start | bytes 2949128 | tf_op jit(solution)/shard_map/ppermute | solution.py:349
  119.9 21.6 %collective-permute-start.30 = (bf16[192,2560]{1,0:T(8,128)(2,1)}, bf16[192,2560]{1,0:T(8,128)(2,1)}, u32[]{:S(2)}, u32[]{:S(2)}) collective-permute-start(bf16[192,2560]{1,0:T(8,128)(2,1)} %get-tuple-element.78), channel_id=1, source_target_pairs={{0,8},{8,0},{16,24},{24,16},{1,9},{9,1},{17,25},{25,17},{2,10},{10... | collective-permute-start | bytes 2949128 | tf_op jit(solution)/shard_map/ppermute | solution.py:349
  120.4 4.5 %copy-start.9 = (bf16[192,1280]{1,0:T(8,128)(2,1)}, bf16[192,1280]{1,0:T(8,128)(2,1)S(1)}, u32[]{:S(2)}) copy-start(bf16[192,1280]{1,0:T(8,128)(2,1)S(1)} %collective-permute-done.21.refs_1_) | copy-start | bytes 1474564
  120.5 0.8 copy-start.19
  125.0 1.7 copy-start.20
  126.6 11.0 %collective-permute-start.28 = (bf16[1152,320]{0,1:T(8,128)(2,1)S(1)}, bf16[1152,320]{0,1:T(8,128)(2,1)}, u32[]{:S(2)}, u32[]{:S(2)}) collective-permute-start(bf16[1152,320]{0,1:T(8,128)(2,1)S(1)} %copy.47), channel_id=1, source_target_pairs={{0,8},{8,0},{16,24},{24,16},{1,9},{9,1},{17,25},{25,17},{2,10},{10... | collective-permute-start | bytes 2211848 | tf_op jit(solution)/shard_map/ppermute | solution.py:349
  126.8 10.7 %collective-permute-start.20 = (bf16[4,4,2560]{2,1,0:T(4,128)(2,1)S(1)}, bf16[4,4,2560]{2,1,0:T(4,128)(2,1)S(1)}, u32[]{:S(2)}, u32[]{:S(2)}) collective-permute-start(bf16[4,4,2560]{2,1,0:T(4,128)(2,1)S(1)} %squeeze.68), channel_id=1, source_target_pairs={{0,1},{1,0},{2,3},{3,2},{4,5},{5,4},{6,7},{7,6},{8,9},{9,8},{10,11... | collective-permute-start | bytes 245768 | tf_op jit(solution)/shard_map/ppermute | solution.py:366
  128.1 0.8 copy-start.6
  133.4 22.0 %collective-permute-start.23 = (bf16[640,1536]{1,0:T(8,128)(2,1)}, bf16[640,1536]{1,0:T(8,128)(2,1)}, u32[]{:S(2)}, u32[]{:S(2)}) collective-permute-start(bf16[640,1536]{1,0:T(8,128)(2,1)} %gate_up_grads.2), channel_id=1, source_target_pairs={{0,8},{8,0},{16,24},{24,16},{1,9},{9,1},{17,25},{25,17},{2,10},{10... | collective-permute-start | bytes 5898248 | tf_op jit(solution)/shard_map/ppermute | solution.py:349
  133.6 53.9 %all-to-all-start.2 = ((bf16[8,24,5120]{2,1,0:T(8,128)(2,1)}), bf16[8,24,5120]{2,1,0:T(8,128)(2,1)S(1)}, u32[]{:S(2)}, u32[]{:S(2)}) async-start(bf16[8,24,5120]{2,1,0:T(8,128)(2,1)} %bitcast.81), calls=%async_computation.2 | async-start | bytes 3932160 | tf_op jit(solution)/shard_map/all_to_all | solution.py:322
  139.3 2.2 %copy-start.12 = (bf16[192,2560]{1,0:T(8,128)(2,1)S(1)}, bf16[192,2560]{1,0:T(8,128)(2,1)}, u32[]{:S(2)}) copy-start(bf16[192,2560]{1,0:T(8,128)(2,1)} %get-tuple-element.77) | copy-start | bytes 2949124
  140.9 13.0 %collective-permute-start.29 = (bf16[576,320]{1,0:T(8,128)(2,1)S(1)}, bf16[576,320]{1,0:T(8,128)(2,1)S(1)}, u32[]{:S(2)}, u32[]{:S(2)}) collective-permute-start(bf16[576,320]{1,0:T(8,128)(2,1)S(1)} %slice.166), channel_id=1, source_target_pairs={{0,16},{8,24},{16,0},{24,8},{1,17},{9,25},{17,1},{25,9},{2,18},{10... | collective-permute-start | bytes 1105928 | tf_op jit(solution)/shard_map/ppermute | solution.py:345
  143.0 31.6 %copy-start.13 = (bf16[192,2560]{1,0:T(8,128)(2,1)S(1)}, bf16[192,2560]{1,0:T(8,128)(2,1)}, u32[]{:S(2)}) copy-start(bf16[192,2560]{1,0:T(8,128)(2,1)} %get-tuple-element.85) | copy-start | bytes 2949124
  143.0 31.6 %collective-permute-start.31 = (bf16[192,2560]{1,0:T(8,128)(2,1)S(1)}, bf16[192,2560]{1,0:T(8,128)(2,1)S(1)}, u32[]{:S(2)}, u32[]{:S(2)}) collective-permute-start(bf16[192,2560]{1,0:T(8,128)(2,1)S(1)} %add_convert_fusion.2), channel_id=1, source_target_pairs={{0,16},{8,24},{16,0},{24,8},{1,17},{9,25},{17,1},{25,9},{2,18},{10... | collective-permute-start | bytes 2949128 | tf_op jit(solution)/shard_map/ppermute | solution.py:345
  155.5 26.8 %collective-permute-start.24 = (bf16[2,4,2560]{2,1,0:T(4,128)(2,1)S(1)}, bf16[2,4,2560]{2,1,0:T(4,128)(2,1)S(1)}, u32[]{:S(2)}, u32[]{:S(2)}) collective-permute-start(bf16[2,4,2560]{2,1,0:T(4,128)(2,1)S(1)} %get-tuple-element.109), channel_id=1, source_target_pairs={{0,2},{1,3},{2,0},{3,1},{4,6},{5,7},{6,4},{7,5},{8,10},{9,11},{10,... | collective-permute-start | bytes 122888 | tf_op jit(solution)/shard_map/ppermute | solution.py:366
  157.3 29.3 %collective-permute-start.25 = (bf16[2,4,2560]{2,1,0:T(4,128)(2,1)S(1)}, bf16[2,4,2560]{2,1,0:T(4,128)(2,1)S(1)}, u32[]{:S(2)}, u32[]{:S(2)}) collective-permute-start(bf16[2,4,2560]{2,1,0:T(4,128)(2,1)S(1)} %get-tuple-element.108), channel_id=1, source_target_pairs={{0,4},{1,5},{2,6},{3,7},{4,0},{5,1},{6,2},{7,3},{8,12},{9,13},{10,... | collective-permute-start | bytes 122888 | tf_op jit(solution)/shard_map/ppermute | solution.py:366
  159.7 26.8 %collective-permute-start.26 = (bf16[2,4,2560]{2,1,0:T(4,128)(2,1)S(1)}, bf16[2,4,2560]{2,1,0:T(4,128)(2,1)S(1)}, u32[]{:S(2)}, u32[]{:S(2)}) collective-permute-start(bf16[2,4,2560]{2,1,0:T(4,128)(2,1)S(1)} %slice_bitcast_fusion.9), channel_id=1, source_target_pairs={{0,6},{1,7},{2,4},{3,5},{4,2},{5,3},{6,0},{7,1},{8,14},{9,15},{10,... | collective-permute-start | bytes 122888 | tf_op jit(solution)/shard_map/ppermute | solution.py:366

commit v5 on v4

--- a/solution.py
+++ b/solution.py
@@ -505,8 +505,6 @@
     xs_last = list(after(tuple(xs_late), *hot_far, *dn_recv))
     grad_gu = gate_up_grads(xs_last, ds, 0, wide, inverse, gu_in)
 
-    if cores == 2:
-        hot_back = after(hot_back, gu_in)
     hot_back = [hot_back[0]] + [hop(hot_back[j], j * across) for j in range(1, depths)]
     hot_back = list(after(tuple(hot_back), grad_gu))
     hot_back = jnp.concatenate(hot_back).reshape(owners * few, PIECES * narrow)

time: 192 us -> 198 us (1.031)
  waiting for transfers between devices: 69.5 us -> 73.6 us
  other arithmetic: 12.6 us -> 15.6 us
    ppermute x7, waiting for transfers between devices: 27.3 us -> 29.6 us  [shift(): return lax.ppermute(value, 'dp', pairs)]
    unnamed x60 -> x58, local copies, waits for them, and re-layouts: 4.29 us -> 4.61 us
  transfers between devices with their start and end apart: 35 -> 35, of which waited for: 13 -> 11; matrix products, arithmetic and copies ran while one was open for 15% -> 16% of each run, Pallas kernels for 19% -> 19%
where the time goes in v5:
time: 198 us; the launch traced here: 197 us
  waiting for transfers between devices  73.6 us (37%)
  starting transfers between devices  43.8 us (22%)
  Pallas kernels  37.2 us (19%)
  local copies, waits for them, and re-layouts  18.7 us (9%)
  other arithmetic  15.6 us (8%)
  matrix products  6.89 us (3%)
    ppermute x7, waiting for transfers between devices, shift(): return lax.ppermute(value, 'dp', pairs)  29.6 us
    ppermute x16, waiting for transfers between devices, hop(): return lax.ppermute(value, 'expert', [(i, i ^ j) for i in range(owners)])  23.8 us
    ppermute x16, starting transfers between devices, hop(): return lax.ppermute(value, 'expert', [(i, i ^ j) for i in range(owners)])  21.5 us
    all_to_all x3, waiting for transfers between devices, exchange(): lax.all_to_all(blocks, 'expert', split_axis=0, concat_axis=0, tiled=True)  18.9 us
    all_to_all x3, starting transfers between devices, exchange(): lax.all_to_all(blocks, 'expert', split_axis=0, concat_axis=0, tiled=True)  13.5 us
    pallas_call x1, Pallas kernels, expert(): pl.pallas_call(body, in_specs=[SMEM, INSIDE, INSIDE] + [ANYWHERE] * (2 *...  12.5 us
    pallas_call x2, Pallas kernels, gate_up_grads(): pl.pallas_call(body, grid=(width // step,), in_specs=[pl.BlockSpec((rows,...  9.61 us
    ppermute x7, starting transfers between devices, shift(): return lax.ppermute(value, 'dp', pairs)  7.55 us
  transfers between devices with their start and end apart: 35, of which 11 were waited for; matrix products, arithmetic and copies ran while one was open for 16% of the time, Pallas kernels for 19%

profile of v5, /device:TPU:0, one launch (start us, length us, event | category | flops | bytes accessed | tf_op | source)
XLA Modules:
  0.0 197.1 jit_solution(12789342401880506467)
XLA Ops:
  0.7 1.2 pad_maximum_fusion.3
  1.8 3.0 %collective-permute-start.4 = (bf16[576,320]{1,0:T(8,128)(2,1)S(1)}, bf16[576,320]{1,0:T(8,128)(2,1)S(1)}, u32[]{:S(2)}, u32[]{:S(2)}) collective-permute-start(bf16[576,320]{1,0:T(8,128)(2,1)S(1)} %bitcast.89), channel_id=1, source_target_pairs={{0,16},{8,24},{16,0},{24,8},{1,17},{9,25},{17,1},{25,9},{2,18},{10... | collective-permute-start | bytes 1105928 | tf_op jit(solution)/shard_map/ppermute | solution.py:345
  4.9 0.7 fusion.14
  5.8 0.8 select_reduce_fusion
  6.8 1.4 convolution_convert_fusion
  8.1 5.9 %all-to-all-start.1 = ((bf16[8,24,2560]{2,1,0:T(8,128)(2,1)}), bf16[8,24,2560]{2,1,0:T(8,128)(2,1)S(1)}, u32[]{:S(2)}, u32[]{:S(2)}) async-start(bf16[8,24,2560]{2,1,0:T(8,128)(2,1)} %bitcast.91), calls=%async_computation.1 | async-start | bytes 1966080 | tf_op jit(solution)/shard_map/all_to_all | solution.py:322
  15.3 2.1 %collective-permute-start = (bf16[2,4,2560]{2,1,0:T(4,128)(2,1)S(1)}, bf16[2,4,2560]{2,1,0:T(4,128)(2,1)S(1)}, u32[]{:S(2)}, u32[]{:S(2)}) collective-permute-start(bf16[2,4,2560]{2,1,0:T(4,128)(2,1)S(1)} %squeeze.61), channel_id=1, source_target_pairs={{0,2},{1,3},{2,0},{3,1},{4,6},{5,7},{6,4},{7,5},{8,10},{9,11},{10,... | collective-permute-start | bytes 122888 | tf_op jit(solution)/shard_map/ppermute | solution.py:366
  17.4 2.4 %collective-permute-start.1 = (bf16[2,4,2560]{2,1,0:T(4,128)(2,1)S(1)}, bf16[2,4,2560]{2,1,0:T(4,128)(2,1)S(1)}, u32[]{:S(2)}, u32[]{:S(2)}) collective-permute-start(bf16[2,4,2560]{2,1,0:T(4,128)(2,1)S(1)} %squeeze.62), channel_id=1, source_target_pairs={{0,4},{1,5},{2,6},{3,7},{4,0},{5,1},{6,2},{7,3},{8,12},{9,13},{10,... | collective-permute-start | bytes 122888 | tf_op jit(solution)/shard_map/ppermute | solution.py:366
  20.0 1.4 convolution_convert_fusion.1
  21.5 0.6 collective-permute-start.7
  22.1 18.9 %all-to-all-done.1 = bf16[8,24,2560]{2,1,0:T(8,128)(2,1)S(1)} async-done(((bf16[8,24,2560]{2,1,0:T(8,128)(2,1)}), bf16[8,24,2560]{2,1,0:T(8,128)(2,1)S(1)}, u32[]{:S(2)}, u32[]{:S(2)}) %all-to-all-start.1) | async-done | bytes 983072 | tf_op jit(solution)/shard_map/all_to_all | solution.py:322
  41.0 3.7 %all-to-all-start = ((bf16[8,24,2560]{2,1,0:T(8,128)(2,1)}), bf16[8,24,2560]{2,1,0:T(8,128)(2,1)S(1)}, u32[]{:S(2)}, u32[]{:S(2)}) async-start(bf16[8,24,2560]{2,1,0:T(8,128)(2,1)} %bitcast.6), calls=%async_computation | async-start | bytes 1966080 | tf_op jit(solution)/shard_map/all_to_all | solution.py:322
  45.0 1.1 constant_dynamic-update-slice_fusion.refs_0_.refs_2_
  46.1 1.4 copy.41
  47.6 1.8 collective-permute-start.3
  49.5 0.7 convert_element_type.103.sel_ref
  50.2 6.0 %collective-permute-done.3 = bf16[4,4,2560]{2,1,0:T(4,128)(2,1)S(1)} collective-permute-done((bf16[4,4,2560]{2,1,0:T(4,128)(2,1)S(1)}, bf16[4,4,2560]{2,1,0:T(4,128)(2,1)S(1)}, u32[]{:S(2)}, u32[]{:S(2)}) %collective-permute-start.3) | collective-permute-done | bytes 81952 | tf_op jit(solution)/shard_map/ppermute | solution.py:366
  56.4 0.7 reshape.357.in_ref
  57.1 2.2 %copy.42.refs_1_.refs_3_ = bf16[1152,320]{1,0:T(8,128)(2,1)} copy(bf16[1152,320]{0,1:T(8,128)(2,1)} %collective-permute-done.5) | data formatting | bytes 1474560 | tf_op jit(solution)/shard_map/ppermute | solution.py:349
  59.3 3.7 %popular_partials.1 = (bf16[128,320]{1,0:T(8,128)(2,1)}, bf16[128,320]{1,0:T(8,128)(2,1)}, bf16[128,2304]{1,0:T(8,128)(2,1)}) custom-call(bf16[4,128,32]{2,1,0:T(8,128)(2,1)} %convert_element_type.103.sel_ref, bf16[32,2560]{1,0:T(8,128)(2,1)} %reshape.357.in_ref, bf16[1152,320]{1,0:T(8,128)(2,1)} %copy-done, bf16[1152,320]{1,0:T(8,128)(2,1)} %copy.42.refs_1_.refs_3_), custom_call_target="tpu_custom_call" | custom-call | flops 1 | bytes 1 | tf_op jit(solution)/shard_map/popular_partials/pallas_call | solution.py:221
  63.0 1.0 slice.125
  65.0 6.9 %collective-permute-done.6 = bf16[64,2304]{1,0:T(8,128)(2,1)S(1)} collective-permute-done((bf16[64,2304]{1,0:T(8,128)(2,1)S(1)}, bf16[64,2304]{1,0:T(8,128)(2,1)S(1)}, u32[]{:S(2)}, u32[]{:S(2)}) %collective-permute-start.6) | collective-permute-done | bytes 294944 | tf_op jit(solution)/shard_map/ppermute | solution.py:366
  71.9 1.2 add_convert_fusion.5
  73.2 0.7 fusion.40
  73.8 4.2 %collective-permute-start.10 = (bf16[16,2304]{1,0:T(8,128)(2,1)S(1)}, bf16[16,2304]{1,0:T(8,128)(2,1)S(1)}, u32[]{:S(2)}, u32[]{:S(2)}) collective-permute-start(bf16[16,2304]{1,0:T(8,128)(2,1)S(1)} %get-tuple-element.100), channel_id=1, source_target_pairs={{0,6},{1,7},{2,4},{3,5},{4,2},{5,3},{6,0},{7,1},{8,14},{9,15},{10,... | collective-permute-start | bytes 221192 | tf_op jit(solution)/shard_map/ppermute | solution.py:366
  78.6 1.9 collective-permute-done.10.refs_2_
  80.5 1.9 collective-permute-done.8.refs_0_
  82.4 0.9 collective-permute-done.9.refs_1_
  83.3 0.6 copy-done.22
  83.9 1.7 popular_middle.1
  85.7 2.5 %collective-permute-done.13.refs_5_ = bf16[192,2560]{1,0:T(8,128)(2,1)} collective-permute-done((bf16[192,2560]{1,0:T(8,128)(2,1)}, bf16[192,2560]{1,0:T(8,128)(2,1)}, u32[]{:S(2)}, u32[]{:S(2)}) %collective-permute-start.13) | collective-permute-done | bytes 983072 | tf_op jit(solution)/shard_map/ppermute | solution.py:345
  88.7 0.7 pad_add_fusion.1.order_ref
  89.4 0.6 collective-permute-start.16
  90.1 1.2 collective-permute-done.14.refs_6_
  91.3 2.0 collective-permute-start.17
  93.2 2.4 %collective-permute-start.18 = (bf16[16,2304]{1,0:T(8,128)(2,1)S(1)}, bf16[16,2304]{1,0:T(8,128)(2,1)S(1)}, u32[]{:S(2)}, u32[]{:S(2)}) collective-permute-start(bf16[16,2304]{1,0:T(8,128)(2,1)S(1)} %copy-done.18), channel_id=1, source_target_pairs={{0,6},{1,7},{2,4},{3,5},{4,2},{5,3},{6,0},{7,1},{8,14},{9,15},{10,... | collective-permute-start | bytes 221192 | tf_op jit(solution)/shard_map/ppermute | solution.py:366
  95.7 0.8 pad_maximum_fusion.2
  97.1 0.7 copy-done.8
  97.8 1.3 copy-done.9
  99.1 12.5 %expert.1 = (bf16[192,5120]{1,0:T(8,128)(2,1)}, bf16[192,768]{1,0:T(8,128)(2,1)}, bf16[192,1536]{1,0:T(8,128)(2,1)}) custom-call(s32[4]{0:T(128)} %pad_add_fusion.1.order_ref, bf16[192,2560]{1,0:T(8,128)(2,1)} %bitcast.81, bf16[192,2560]{1,0:T(8,128)(2,1)} %bitcast.80, bf16[640,1536]{1,0:T(8,128)(2,1)} %bitcast.86, ...), custom_call_target="tpu_custom_call" | custom-call | flops 1 | bytes 1 | tf_op jit(solution)/shard_map/expert/pallas_call | solution.py:115
  111.6 5.9 %down_grads.1 = (bf16[192,2560]{1,0:T(8,128)(2,1)}, bf16[192,2560]{1,0:T(8,128)(2,1)}, bf16[192,2560]{1,0:T(8,128)(2,1)}, bf16[192,2560]{1,0:T(8,128)(2,1)}) custom-call(s32[4]{0:T(128)} %pad_add_fusion.1.order_ref, bf16[192,768]{1,0:T(8,128)(2,1)} %get-tuple-element.71.h_ref, bf16[192,2560]{1,0:T(8,128)(2,1)} %bitcast.82), custom_call_target="tpu_custom_call" | custom-call | flops 1 | bytes 1 | tf_op jit(solution)/shard_map/down_grads/pallas_call | solution.py:180
  118.1 1.6 collective-permute-start.19
  119.7 0.8 pad_maximum_fusion.1.refs_0_
  120.5 0.8 collective-permute-start.30
  121.3 3.8 %all-to-all-start.2 = ((bf16[8,24,5120]{2,1,0:T(8,128)(2,1)}), bf16[8,24,5120]{2,1,0:T(8,128)(2,1)S(1)}, u32[]{:S(2)}, u32[]{:S(2)}) async-start(bf16[8,24,5120]{2,1,0:T(8,128)(2,1)} %bitcast.87), calls=%async_computation.2 | async-start | bytes 3932160 | tf_op jit(solution)/shard_map/all_to_all | solution.py:322
  125.1 6.2 %collective-permute-done.19.refs_1_ = bf16[64,2304]{1,0:T(8,128)(2,1)} collective-permute-done((bf16[64,2304]{1,0:T(8,128)(2,1)S(1)}, bf16[64,2304]{1,0:T(8,128)(2,1)}, u32[]{:S(2)}, u32[]{:S(2)}) %collective-permute-start.19) | collective-permute-done | bytes 294944 | tf_op jit(solution)/shard_map/ppermute | solution.py:366
  131.3 3.8 %popular_back.1 = (bf16[32,2560]{1,0:T(8,128)(2,1)}, bf16[1152,320]{1,0:T(8,128)(2,1)}, bf16[1152,320]{1,0:T(8,128)(2,1)}) custom-call(bf16[4,128,32]{2,1,0:T(8,128)(2,1)} %convert_element_type.103.sel_ref, bf16[128,320]{1,0:T(8,128)(2,1)} %get-tuple-element.60.x_ref, bf16[128,320]{1,0:T(8,128)(2,1)} %get-tuple-element.61.s_ref, ...), custom_call_target="tpu_custom_call" | custom-call | flops 1 | bytes 1 | tf_op jit(solution)/shard_map/popular_back/pallas_call | solution.py:301
  135.1 2.2 %copy.47 = bf16[1152,320]{0,1:T(8,128)(2,1)} copy(bf16[1152,320]{1,0:T(8,128)(2,1)} %get-tuple-element.74) | data formatting | bytes 1474560 | tf_op jit(solution)/shard_map/popular_back/pallas_call | solution.py:301
  137.4 3.3 %collective-permute-start.20 = (bf16[4,4,2560]{2,1,0:T(4,128)(2,1)S(1)}, bf16[4,4,2560]{2,1,0:T(4,128)(2,1)S(1)}, u32[]{:S(2)}, u32[]{:S(2)}) collective-permute-start(bf16[4,4,2560]{2,1,0:T(4,128)(2,1)S(1)} %squeeze.68), channel_id=1, source_target_pairs={{0,1},{1,0},{2,3},{3,2},{4,5},{5,4},{6,7},{7,6},{8,9},{9,8},{10,11... | collective-permute-start | bytes 245768 | tf_op jit(solution)/shard_map/ppermute | solution.py:366
  140.6 0.8 copy-done.7
  141.4 4.5 %gate_up_grads.2 = bf16[640,1536]{1,0:T(8,128)(2,1)} custom-call(bf16[192,1280]{1,0:T(8,128)(2,1)} %pad_maximum_fusion.1.refs_0_, bf16[192,1280]{1,0:T(8,128)(2,1)} %collective-permute-done.24.refs_1_, bf16[192,1536]{1,0:T(8,128)(2,1)} %get-tuple-element.62.refs_2_, bf16[192,1536]{1,0:T(8,128)(2,1)} %copy-done.7), custom_call_target="tpu_custom_call" | custom-call | flops 1 | bytes 1 | tf_op jit(solution)/shard_map/gate_up_grads/pallas_call | solution.py:152
  146.2 2.4 %add_convert_fusion.2 = bf16[192,2560]{1,0:T(8,128)(2,1)} fusion(bf16[192,2560]{1,0:T(8,128)(2,1)} %collective-permute-done.28, bf16[192,2560]{1,0:T(8,128)(2,1)S(1)} %copy-done.12), kind=kLoop, calls=%fused_computation.14 | loop fusion | flops 1966080 | bytes 2949120 | tf_op jit(solution)/shard_map/convert_element_type | solution.py:478
  148.6 1.7 copy.48
  150.3 1.4 add_convert_fusion.3
  151.7 1.0 copy-done.3
  152.7 2.1 %collective-permute-start.27 = (bf16[576,320]{1,0:T(8,128)(2,1)S(1)}, bf16[576,320]{1,0:T(8,128)(2,1)S(1)}, u32[]{:S(2)}, u32[]{:S(2)}) collective-permute-start(bf16[576,320]{1,0:T(8,128)(2,1)S(1)} %slice.169), channel_id=1, source_target_pairs={{0,16},{8,24},{16,0},{24,8},{1,17},{9,25},{17,1},{25,9},{2,18},{10... | collective-permute-start | bytes 1105928 | tf_op jit(solution)/shard_map/ppermute | solution.py:345
  155.3 26.9 %collective-permute-done.27 = bf16[576,320]{1,0:T(8,128)(2,1)S(1)} collective-permute-done((bf16[576,320]{1,0:T(8,128)(2,1)S(1)}, bf16[576,320]{1,0:T(8,128)(2,1)S(1)}, u32[]{:S(2)}, u32[]{:S(2)}) %collective-permute-start.27) | collective-permute-done | bytes 368672 | tf_op jit(solution)/shard_map/ppermute | solution.py:345
  182.2 1.1 add_convert_fusion.4
  183.3 0.7 slice.177
  184.1 0.7 slice.178
  184.7 2.9 %fusion.4 = bf16[1,192,2560]{2,1,0:T(8,128)(2,1)} fusion(bf16[192,2560]{1,0:T(8,128)(2,1)} %collective-permute-done.29, bf16[192,2560]{1,0:T(8,128)(2,1)} %collective-permute-done.25, bf16[192,2560]{1,0:T(8,128)(2,1)S(1)} %copy-done.13), kind=kLoop, calls=%fused_computation.19 | loop fusion | flops 3932160 | bytes 3932160 | tf_op jit(solution)/shard_map/broadcast_in_dim | solution.py:543
  187.6 5.1 %gate_up_grads.3 = bf16[640,1536]{1,0:T(8,128)(2,1)} custom-call(bf16[192,1280]{1,0:T(8,128)(2,1)} %pad_maximum_fusion.1.refs_0_, bf16[192,1280]{1,0:T(8,128)(2,1)} %collective-permute-done.24.refs_1_, bf16[192,1536]{1,0:T(8,128)(2,1)} %get-tuple-element.62.refs_2_, bf16[192,1536]{1,0:T(8,128)(2,1)} %copy-done.7, ...), custom_call_target="tpu_custom_call" | custom-call | flops 1 | bytes 1 | tf_op jit(solution)/shard_map/gate_up_grads/pallas_call | solution.py:152
  194.3 1.3 fusion.2
  195.8 1.3 fusion.1
  (142 shorter events, 8.1 us)
Async XLA Ops:
  0.6 6.0 %copy-start.24 = (s32[128,1]{0,1:T(1,128)S(1)}, s32[128,1]{0,1:T(1,128)}, u32[]{:S(2)}) copy-start(s32[128,1]{0,1:T(1,128)} %param.12) | copy-start | bytes 1540
  0.6 6.0 %copy-start.4 = (bf16[128,2560]{1,0:T(8,128)(2,1)S(1)}, bf16[128,2560]{1,0:T(8,128)(2,1)}, u32[]{:S(2)}) copy-start(bf16[128,2560]{1,0:T(8,128)(2,1)} %param.10) | copy-start | bytes 1966084
  1.8 6.3 %copy-start.10 = (bf16[3,192,320]{2,1,0:T(8,128)(2,1)}, bf16[3,192,320]{2,1,0:T(8,128)(2,1)S(1)}, u32[]{:S(2)}) copy-start(bf16[3,192,320]{2,1,0:T(8,128)(2,1)S(1)} %pad_maximum_fusion.3) | copy-start | bytes 1105924
  1.8 19.6 %collective-permute-start.4 = (bf16[576,320]{1,0:T(8,128)(2,1)S(1)}, bf16[576,320]{1,0:T(8,128)(2,1)S(1)}, u32[]{:S(2)}, u32[]{:S(2)}) collective-permute-start(bf16[576,320]{1,0:T(8,128)(2,1)S(1)} %bitcast.89), channel_id=1, source_target_pairs={{0,16},{8,24},{16,0},{24,8},{1,17},{9,25},{17,1},{25,9},{2,18},{10... | collective-permute-start | bytes 1105928 | tf_op jit(solution)/shard_map/ppermute | solution.py:345
  8.1 6.0 %copy-start.23 = (s32[16]{0:T(128)S(1)}, s32[16]{0:T(128)}, u32[]{:S(2)}) copy-start(s32[16]{0:T(128)} %param.14) | copy-start | bytes 196
  8.1 6.2 %copy-start.5 = (bf16[128,2560]{1,0:T(8,128)(2,1)S(1)}, bf16[128,2560]{1,0:T(8,128)(2,1)}, u32[]{:S(2)}) copy-start(bf16[128,2560]{1,0:T(8,128)(2,1)} %param.11) | copy-start | bytes 1966084
  8.1 6.2 %copy-start.26 = (f32[16]{0:T(128)S(1)}, f32[16]{0:T(128)}, u32[]{:S(2)}) copy-start(f32[16]{0:T(128)} %param.15) | copy-start | bytes 196
  8.1 32.9 %all-to-all-start.1 = ((bf16[8,24,2560]{2,1,0:T(8,128)(2,1)}), bf16[8,24,2560]{2,1,0:T(8,128)(2,1)S(1)}, u32[]{:S(2)}, u32[]{:S(2)}) async-start(bf16[8,24,2560]{2,1,0:T(8,128)(2,1)} %bitcast.91), calls=%async_computation.1 | async-start | bytes 1966080 | tf_op jit(solution)/shard_map/all_to_all | solution.py:322
  14.6 5.4 %copy-start.25 = (f32[128,1]{0,1:T(1,128)S(1)}, f32[128,1]{0,1:T(1,128)}, u32[]{:S(2)}) copy-start(f32[128,1]{0,1:T(1,128)} %param.13) | copy-start | bytes 1540
  15.3 29.4 %collective-permute-start = (bf16[2,4,2560]{2,1,0:T(4,128)(2,1)S(1)}, bf16[2,4,2560]{2,1,0:T(4,128)(2,1)S(1)}, u32[]{:S(2)}, u32[]{:S(2)}) collective-permute-start(bf16[2,4,2560]{2,1,0:T(4,128)(2,1)S(1)} %squeeze.61), channel_id=1, source_target_pairs={{0,2},{1,3},{2,0},{3,1},{4,6},{5,7},{6,4},{7,5},{8,10},{9,11},{10,... | collective-permute-start | bytes 122888 | tf_op jit(solution)/shard_map/ppermute | solution.py:366
  17.4 27.3 %collective-permute-start.1 = (bf16[2,4,2560]{2,1,0:T(4,128)(2,1)S(1)}, bf16[2,4,2560]{2,1,0:T(4,128)(2,1)S(1)}, u32[]{:S(2)}, u32[]{:S(2)}) collective-permute-start(bf16[2,4,2560]{2,1,0:T(4,128)(2,1)S(1)} %squeeze.62), channel_id=1, source_target_pairs={{0,4},{1,5},{2,6},{3,7},{4,0},{5,1},{6,2},{7,3},{8,12},{9,13},{10,... | collective-permute-start | bytes 122888 | tf_op jit(solution)/shard_map/ppermute | solution.py:366
  19.9 24.9 %collective-permute-start.2 = (bf16[2,4,2560]{2,1,0:T(4,128)(2,1)S(1)}, bf16[2,4,2560]{2,1,0:T(4,128)(2,1)S(1)}, u32[]{:S(2)}, u32[]{:S(2)}) collective-permute-start(bf16[2,4,2560]{2,1,0:T(4,128)(2,1)S(1)} %squeeze.63), channel_id=1, source_target_pairs={{0,6},{1,7},{2,4},{3,5},{4,2},{5,3},{6,0},{7,1},{8,14},{9,15},{10,... | collective-permute-start | bytes 122888 | tf_op jit(solution)/shard_map/ppermute | solution.py:366
  21.4 23.5 %copy-start.11 = (bf16[3,192,320]{2,1,0:T(8,128)(2,1)S(1)}, bf16[3,192,320]{2,1,0:T(8,128)(2,1)}, u32[]{:S(2)}) copy-start(bf16[3,192,320]{2,1,0:T(8,128)(2,1)} %copy-done.10) | copy-start | bytes 1105924
  21.5 23.3 %copy-start.17 = (bf16[576,320]{1,0:T(8,128)(2,1)}, bf16[576,320]{1,0:T(8,128)(2,1)S(1)}, u32[]{:S(2)}) copy-start(bf16[576,320]{1,0:T(8,128)(2,1)S(1)} %collective-permute-done.4) | copy-start | bytes 1105924
  21.5 43.5 %collective-permute-start.7 = (bf16[640,1536]{1,0:T(8,128)(2,1)}, bf16[640,1536]{1,0:T(8,128)(2,1)}, u32[]{:S(2)}, u32[]{:S(2)}) collective-permute-start(bf16[640,1536]{1,0:T(8,128)(2,1)} %bitcast.84), channel_id=1, source_target_pairs={{0,16},{8,24},{16,0},{24,8},{1,17},{9,25},{17,1},{25,9},{2,18},{10... | collective-permute-start | bytes 5898248 | tf_op jit(solution)/shard_map/ppermute | solution.py:345
  41.0 49.0 %copy-start.1 = (bf16[8,24,2560]{2,1,0:T(8,128)(2,1)}, bf16[8,24,2560]{2,1,0:T(8,128)(2,1)S(1)}, u32[]{:S(2)}) copy-start(bf16[8,24,2560]{2,1,0:T(8,128)(2,1)S(1)} %all-to-all-done.1) | copy-start | bytes 2949124
  41.0 31.0 %all-to-all-start = ((bf16[8,24,2560]{2,1,0:T(8,128)(2,1)}), bf16[8,24,2560]{2,1,0:T(8,128)(2,1)S(1)}, u32[]{:S(2)}, u32[]{:S(2)}) async-start(bf16[8,24,2560]{2,1,0:T(8,128)(2,1)} %bitcast.6), calls=%async_computation | async-start | bytes 1966080 | tf_op jit(solution)/shard_map/all_to_all | solution.py:322
  46.1 11.0 %copy-start = (bf16[1152,320]{1,0:T(8,128)(2,1)}, bf16[1152,320]{1,0:T(8,128)(2,1)S(1)}, u32[]{:S(2)}) copy-start(bf16[1152,320]{1,0:T(8,128)(2,1)S(1)} %constant_dynamic-update-slice_fusion.refs_0_.refs_2_) | copy-start | bytes 2211844
  47.5 9.6 %collective-permute-start.5 = (bf16[1152,320]{0,1:T(8,128)(2,1)}, bf16[1152,320]{0,1:T(8,128)(2,1)}, u32[]{:S(2)}, u32[]{:S(2)}) collective-permute-start(bf16[1152,320]{0,1:T(8,128)(2,1)} %copy.41), channel_id=1, source_target_pairs={{0,8},{8,0},{16,24},{24,16},{1,9},{9,1},{17,25},{25,17},{2,10},{10... | collective-permute-start | bytes 2211848 | tf_op jit(solution)/shard_map/ppermute | solution.py:349
  47.6 8.7 %collective-permute-start.3 = (bf16[4,4,2560]{2,1,0:T(4,128)(2,1)S(1)}, bf16[4,4,2560]{2,1,0:T(4,128)(2,1)S(1)}, u32[]{:S(2)}, u32[]{:S(2)}) collective-permute-start(bf16[4,4,2560]{2,1,0:T(4,128)(2,1)S(1)} %get-tuple-element.113), channel_id=1, source_target_pairs={{0,1},{1,0},{2,3},{3,2},{4,5},{5,4},{6,7},{7,6},{8,9},{9,8},{10,11... | collective-permute-start | bytes 245768 | tf_op jit(solution)/shard_map/ppermute | solution.py:366
  64.0 7.9 %collective-permute-start.6 = (bf16[64,2304]{1,0:T(8,128)(2,1)S(1)}, bf16[64,2304]{1,0:T(8,128)(2,1)S(1)}, u32[]{:S(2)}, u32[]{:S(2)}) collective-permute-start(bf16[64,2304]{1,0:T(8,128)(2,1)S(1)} %slice.125), channel_id=1, source_target_pairs={{0,1},{1,0},{2,3},{3,2},{4,5},{5,4},{6,7},{7,6},{8,9},{9,8},{10,11... | collective-permute-start | bytes 884744 | tf_op jit(solution)/shard_map/ppermute | solution.py:366
  64.3 23.9 %collective-permute-start.13 = (bf16[192,2560]{1,0:T(8,128)(2,1)}, bf16[192,2560]{1,0:T(8,128)(2,1)}, u32[]{:S(2)}, u32[]{:S(2)}) collective-permute-start(bf16[192,2560]{1,0:T(8,128)(2,1)} %bitcast.20.refs_4_), channel_id=1, source_target_pairs={{0,16},{8,24},{16,0},{24,8},{1,17},{9,25},{17,1},{25,9},{2,18},{10... | collective-permute-start | bytes 2949128 | tf_op jit(solution)/shard_map/ppermute | solution.py:345
  71.9 18.1 %copy-start.2 = (bf16[8,24,2560]{2,1,0:T(8,128)(2,1)}, bf16[8,24,2560]{2,1,0:T(8,128)(2,1)S(1)}, u32[]{:S(2)}) copy-start(bf16[8,24,2560]{2,1,0:T(8,128)(2,1)S(1)} %all-to-all-done) | copy-start | bytes 2949124
  73.8 6.7 %collective-permute-start.10 = (bf16[16,2304]{1,0:T(8,128)(2,1)S(1)}, bf16[16,2304]{1,0:T(8,128)(2,1)S(1)}, u32[]{:S(2)}, u32[]{:S(2)}) collective-permute-start(bf16[16,2304]{1,0:T(8,128)(2,1)S(1)} %get-tuple-element.100), channel_id=1, source_target_pairs={{0,6},{1,7},{2,4},{3,5},{4,2},{5,3},{6,0},{7,1},{8,14},{9,15},{10,... | collective-permute-start | bytes 221192 | tf_op jit(solution)/shard_map/ppermute | solution.py:366
  78.1 4.4 %collective-permute-start.8 = (bf16[16,2304]{1,0:T(8,128)(2,1)S(1)}, bf16[16,2304]{1,0:T(8,128)(2,1)S(1)}, u32[]{:S(2)}, u32[]{:S(2)}) collective-permute-start(bf16[16,2304]{1,0:T(8,128)(2,1)S(1)} %get-tuple-element.103), channel_id=1, source_target_pairs={{0,2},{1,3},{2,0},{3,1},{4,6},{5,7},{6,4},{7,5},{8,10},{9,11},{10,... | collective-permute-start | bytes 221192 | tf_op jit(solution)/shard_map/ppermute | solution.py:366
  78.1 5.3 %collective-permute-start.9 = (bf16[16,2304]{1,0:T(8,128)(2,1)S(1)}, bf16[16,2304]{1,0:T(8,128)(2,1)S(1)}, u32[]{:S(2)}, u32[]{:S(2)}) collective-permute-start(bf16[16,2304]{1,0:T(8,128)(2,1)S(1)} %get-tuple-element.102), channel_id=1, source_target_pairs={{0,4},{1,5},{2,6},{3,7},{4,0},{5,1},{6,2},{7,3},{8,12},{9,13},{10,... | collective-permute-start | bytes 221192 | tf_op jit(solution)/shard_map/ppermute | solution.py:366
  78.6 17.9 %collective-permute-start.12 = (bf16[640,1536]{1,0:T(8,128)(2,1)}, bf16[640,1536]{1,0:T(8,128)(2,1)S(1)}, u32[]{:S(2)}, u32[]{:S(2)}) collective-permute-start(bf16[640,1536]{1,0:T(8,128)(2,1)} %collective-permute-done.7.refs_1_), channel_id=1, source_target_pairs={{0,8},{8,0},{16,24},{24,16},{1,9},{9,1},{17,25},{25,17},{2,10},{10... | collective-permute-start | bytes 5898248 | tf_op jit(solution)/shard_map/ppermute | solution.py:349
  80.5 2.8 %copy-start.20 = (bf16[16,2304]{1,0:T(8,128)(2,1)}, bf16[16,2304]{1,0:T(8,128)(2,1)S(1)}, u32[]{:S(2)}) copy-start(bf16[16,2304]{1,0:T(8,128)(2,1)S(1)} %collective-permute-done.10.refs_2_) | copy-start | bytes 221188
  82.4 0.9 copy-start.21
  83.3 0.6 copy-start.22
  85.7 5.6 %copy-start.18 = (bf16[16,2304]{1,0:T(8,128)(2,1)S(1)}, bf16[16,2304]{1,0:T(8,128)(2,1)}, u32[]{:S(2)}) copy-start(bf16[16,2304]{1,0:T(8,128)(2,1)} %popular_middle.1) | copy-start | bytes 221188
  85.7 11.4 %collective-permute-start.11 = (bf16[640,1536]{1,0:T(8,128)(2,1)}, bf16[640,1536]{1,0:T(8,128)(2,1)S(1)}, u32[]{:S(2)}, u32[]{:S(2)}) collective-permute-start(bf16[640,1536]{1,0:T(8,128)(2,1)} %bitcast.85), channel_id=1, source_target_pairs={{0,8},{8,0},{16,24},{24,16},{1,9},{9,1},{17,25},{25,17},{2,10},{10... | collective-permute-start | bytes 5898248 | tf_op jit(solution)/shard_map/ppermute | solution.py:349
  88.2 3.1 %collective-permute-start.14 = (bf16[192,2560]{1,0:T(8,128)(2,1)}, bf16[192,2560]{1,0:T(8,128)(2,1)S(1)}, u32[]{:S(2)}, u32[]{:S(2)}) collective-permute-start(bf16[192,2560]{1,0:T(8,128)(2,1)} %bitcast.20.refs_4_), channel_id=1, source_target_pairs={{0,8},{8,0},{16,24},{24,16},{1,9},{9,1},{17,25},{25,17},{2,10},{10... | collective-permute-start | bytes 2949128 | tf_op jit(solution)/shard_map/ppermute | solution.py:349
  88.2 5.0 %collective-permute-start.15 = (bf16[192,2560]{1,0:T(8,128)(2,1)}, bf16[192,2560]{1,0:T(8,128)(2,1)S(1)}, u32[]{:S(2)}, u32[]{:S(2)}) collective-permute-start(bf16[192,2560]{1,0:T(8,128)(2,1)} %collective-permute-done.13.refs_5_), channel_id=1, source_target_pairs={{0,8},{8,0},{16,24},{24,16},{1,9},{9,1},{17,25},{25,17},{2,10},{10... | collective-permute-start | bytes 2949128 | tf_op jit(solution)/shard_map/ppermute | solution.py:349
  89.4 28.1 %collective-permute-start.16 = (bf16[16,2304]{1,0:T(8,128)(2,1)}, bf16[16,2304]{1,0:T(8,128)(2,1)S(1)}, u32[]{:S(2)}, u32[]{:S(2)}) collective-permute-start(bf16[16,2304]{1,0:T(8,128)(2,1)} %popular_middle.1), channel_id=1, source_target_pairs={{0,2},{1,3},{2,0},{3,1},{4,6},{5,7},{6,4},{7,5},{8,10},{9,11},{10,... | collective-permute-start | bytes 221192 | tf_op jit(solution)/shard_map/ppermute | solution.py:366
  91.3 5.2 %copy-start.14 = (bf16[192,2560]{1,0:T(8,128)(2,1)}, bf16[192,2560]{1,0:T(8,128)(2,1)S(1)}, u32[]{:S(2)}) copy-start(bf16[192,2560]{1,0:T(8,128)(2,1)S(1)} %collective-permute-done.14.refs_6_) | copy-start | bytes 2949124
  91.3 26.2 %collective-permute-start.17 = (bf16[16,2304]{1,0:T(8,128)(2,1)S(1)}, bf16[16,2304]{1,0:T(8,128)(2,1)S(1)}, u32[]{:S(2)}, u32[]{:S(2)}) collective-permute-start(bf16[16,2304]{1,0:T(8,128)(2,1)S(1)} %copy-done.18), channel_id=1, source_target_pairs={{0,4},{1,5},{2,6},{3,7},{4,0},{5,1},{6,2},{7,3},{8,12},{9,13},{10,... | collective-permute-start | bytes 221192 | tf_op jit(solution)/shard_map/ppermute | solution.py:366
  93.2 3.8 %copy-start.15 = (bf16[192,2560]{1,0:T(8,128)(2,1)}, bf16[192,2560]{1,0:T(8,128)(2,1)S(1)}, u32[]{:S(2)}) copy-start(bf16[192,2560]{1,0:T(8,128)(2,1)S(1)} %collective-permute-done.15.refs_7_) | copy-start | bytes 2949124
  93.2 24.3 %collective-permute-start.18 = (bf16[16,2304]{1,0:T(8,128)(2,1)S(1)}, bf16[16,2304]{1,0:T(8,128)(2,1)S(1)}, u32[]{:S(2)}, u32[]{:S(2)}) collective-permute-start(bf16[16,2304]{1,0:T(8,128)(2,1)S(1)} %copy-done.18), channel_id=1, source_target_pairs={{0,6},{1,7},{2,4},{3,5},{4,2},{5,3},{6,0},{7,1},{8,14},{9,15},{10,... | collective-permute-start | bytes 221192 | tf_op jit(solution)/shard_map/ppermute | solution.py:366
  96.5 1.3 copy-start.8
  96.5 28.6 %collective-permute-start.24 = (bf16[192,1280]{1,0:T(8,128)(2,1)}, bf16[192,1280]{1,0:T(8,128)(2,1)}, u32[]{:S(2)}, u32[]{:S(2)}) collective-permute-start(bf16[192,1280]{1,0:T(8,128)(2,1)} %pad_maximum_fusion.2), channel_id=1, source_target_pairs={{0,16},{8,24},{16,0},{24,8},{1,17},{9,25},{17,1},{25,9},{2,18},{10... | collective-permute-start | bytes 1474568 | tf_op jit(solution)/shard_map/ppermute | solution.py:345
  97.8 1.3 copy-start.9
  111.6 8.9 %copy-start.6 = (bf16[192,1536]{1,0:T(8,128)(2,1)S(1)}, bf16[192,1536]{1,0:T(8,128)(2,1)}, u32[]{:S(2)}) copy-start(bf16[192,1536]{1,0:T(8,128)(2,1)} %get-tuple-element.62.refs_2_) | copy-start | bytes 1769476
  117.5 28.7 %collective-permute-start.25 = (bf16[192,2560]{1,0:T(8,128)(2,1)}, bf16[192,2560]{1,0:T(8,128)(2,1)}, u32[]{:S(2)}, u32[]{:S(2)}) collective-permute-start(bf16[192,2560]{1,0:T(8,128)(2,1)} %get-tuple-element.72), channel_id=1, source_target_pairs={{0,8},{8,0},{16,24},{24,16},{1,9},{9,1},{17,25},{25,17},{2,10},{10... | collective-permute-start | bytes 2949128 | tf_op jit(solution)/shard_map/ppermute | solution.py:349
  117.5 28.7 %collective-permute-start.28 = (bf16[192,2560]{1,0:T(8,128)(2,1)}, bf16[192,2560]{1,0:T(8,128)(2,1)}, u32[]{:S(2)}, u32[]{:S(2)}) collective-permute-start(bf16[192,2560]{1,0:T(8,128)(2,1)} %get-tuple-element.76), channel_id=1, source_target_pairs={{0,8},{8,0},{16,24},{24,16},{1,9},{9,1},{17,25},{25,17},{2,10},{10... | collective-permute-start | bytes 2949128 | tf_op jit(solution)/shard_map/ppermute | solution.py:349
  118.1 3.2 %copy-start.16 = (bf16[64,2304]{1,0:T(8,128)(2,1)}, bf16[64,2304]{1,0:T(8,128)(2,1)S(1)}, u32[]{:S(2)}) copy-start(bf16[64,2304]{1,0:T(8,128)(2,1)S(1)} %constant_dynamic-update-slice_fusion.2.refs_0_) | copy-start | bytes 884740
  118.1 13.2 %collective-permute-start.19 = (bf16[64,2304]{1,0:T(8,128)(2,1)S(1)}, bf16[64,2304]{1,0:T(8,128)(2,1)}, u32[]{:S(2)}, u32[]{:S(2)}) collective-permute-start(bf16[64,2304]{1,0:T(8,128)(2,1)S(1)} %constant_dynamic-update-slice_fusion.2.refs_0_), channel_id=1, source_target_pairs={{0,1},{1,0},{2,3},{3,2},{4,5},{5,4},{6,7},{7,6},{8,9},{9,8},{10,11... | collective-permute-start | bytes 884744 | tf_op jit(solution)/shard_map/ppermute | solution.py:366
  120.5 20.1 %collective-permute-start.30 = (bf16[192,1536]{1,0:T(8,128)(2,1)S(1)}, bf16[192,1536]{1,0:T(8,128)(2,1)S(1)}, u32[]{:S(2)}, u32[]{:S(2)}) collective-permute-start(bf16[192,1536]{1,0:T(8,128)(2,1)S(1)} %copy-done.6), channel_id=1, source_target_pairs={{0,16},{8,24},{16,0},{24,8},{1,17},{9,25},{17,1},{25,9},{2,18},{10... | collective-permute-start | bytes 1769480 | tf_op jit(solution)/shard_map/ppermute | solution.py:345
  121.3 72.4 %all-to-all-start.2 = ((bf16[8,24,5120]{2,1,0:T(8,128)(2,1)}), bf16[8,24,5120]{2,1,0:T(8,128)(2,1)S(1)}, u32[]{:S(2)}, u32[]{:S(2)}) async-start(bf16[8,24,5120]{2,1,0:T(8,128)(2,1)} %bitcast.87), calls=%async_computation.2 | async-start | bytes 3932160 | tf_op jit(solution)/shard_map/all_to_all | solution.py:322
  135.1 2.2 %copy-start.19 = (bf16[32,2560]{1,0:T(8,128)(2,1)S(1)}, bf16[32,2560]{1,0:T(8,128)(2,1)}, u32[]{:S(2)}) copy-start(bf16[32,2560]{1,0:T(8,128)(2,1)} %get-tuple-element.67) | copy-start | bytes 491524
  137.3 11.3 %collective-permute-start.26 = (bf16[1152,320]{0,1:T(8,128)(2,1)}, bf16[1152,320]{0,1:T(8,128)(2,1)}, u32[]{:S(2)}, u32[]{:S(2)}) collective-permute-start(bf16[1152,320]{0,1:T(8,128)(2,1)} %copy.47), channel_id=1, source_target_pairs={{0,8},{8,0},{16,24},{24,16},{1,9},{9,1},{17,25},{25,17},{2,10},{10... | collective-permute-start | bytes 2211848 | tf_op jit(solution)/shard_map/ppermute | solution.py:349
  137.4 8.8 %copy-start.12 = (bf16[192,2560]{1,0:T(8,128)(2,1)S(1)}, bf16[192,2560]{1,0:T(8,128)(2,1)}, u32[]{:S(2)}) copy-start(bf16[192,2560]{1,0:T(8,128)(2,1)} %get-tuple-element.75) | copy-start | bytes 2949124
  137.4 17.6 %collective-permute-start.20 = (bf16[4,4,2560]{2,1,0:T(4,128)(2,1)S(1)}, bf16[4,4,2560]{2,1,0:T(4,128)(2,1)S(1)}, u32[]{:S(2)}, u32[]{:S(2)}) collective-permute-start(bf16[4,4,2560]{2,1,0:T(4,128)(2,1)S(1)} %squeeze.68), channel_id=1, source_target_pairs={{0,1},{1,0},{2,3},{3,2},{4,5},{5,4},{6,7},{7,6},{8,9},{9,8},{10,11... | collective-permute-start | bytes 245768 | tf_op jit(solution)/shard_map/ppermute | solution.py:366
  140.6 0.8 copy-start.7
  145.9 41.7 %collective-permute-start.31 = (bf16[640,1536]{1,0:T(8,128)(2,1)}, bf16[640,1536]{1,0:T(8,128)(2,1)}, u32[]{:S(2)}, u32[]{:S(2)}) collective-permute-start(bf16[640,1536]{1,0:T(8,128)(2,1)} %gate_up_grads.2), channel_id=1, source_target_pairs={{0,8},{8,0},{16,24},{24,16},{1,9},{9,1},{17,25},{25,17},{2,10},{10... | collective-permute-start | bytes 5898248 | tf_op jit(solution)/shard_map/ppermute | solution.py:349
  148.5 36.2 %collective-permute-start.29 = (bf16[192,2560]{1,0:T(8,128)(2,1)}, bf16[192,2560]{1,0:T(8,128)(2,1)}, u32[]{:S(2)}, u32[]{:S(2)}) collective-permute-start(bf16[192,2560]{1,0:T(8,128)(2,1)} %add_convert_fusion.2), channel_id=1, source_target_pairs={{0,16},{8,24},{16,0},{24,8},{1,17},{9,25},{17,1},{25,9},{2,18},{10... | collective-permute-start | bytes 2949128 | tf_op jit(solution)/shard_map/ppermute | solution.py:345
  151.7 1.0 copy-start.3
  152.7 29.5 %collective-permute-start.27 = (bf16[576,320]{1,0:T(8,128)(2,1)S(1)}, bf16[576,320]{1,0:T(8,128)(2,1)S(1)}, u32[]{:S(2)}, u32[]{:S(2)}) collective-permute-start(bf16[576,320]{1,0:T(8,128)(2,1)S(1)} %slice.169), channel_id=1, source_target_pairs={{0,16},{8,24},{16,0},{24,8},{1,17},{9,25},{17,1},{25,9},{2,18},{10... | collective-permute-start | bytes 1105928 | tf_op jit(solution)/shard_map/ppermute | solution.py:345
  155.0 29.8 %copy-start.13 = (bf16[192,2560]{1,0:T(8,128)(2,1)S(1)}, bf16[192,2560]{1,0:T(8,128)(2,1)}, u32[]{:S(2)}) copy-start(bf16[192,2560]{1,0:T(8,128)(2,1)} %get-tuple-element.83) | copy-start | bytes 2949124
  155.1 37.6 %collective-permute-start.21 = (bf16[2,4,2560]{2,1,0:T(4,128)(2,1)S(1)}, bf16[2,4,2560]{2,1,0:T(4,128)(2,1)S(1)}, u32[]{:S(2)}, u32[]{:S(2)}) collective-permute-start(bf16[2,4,2560]{2,1,0:T(4,128)(2,1)S(1)} %get-tuple-element.108), channel_id=1, source_target_pairs={{0,2},{1,3},{2,0},{3,1},{4,6},{5,7},{6,4},{7,5},{8,10},{9,11},{10,... | collective-permute-start | bytes 122888 | tf_op jit(solution)/shard_map/ppermute | solution.py:366
  155.2 37.5 %collective-permute-start.22 = (bf16[2,4,2560]{2,1,0:T(4,128)(2,1)S(1)}, bf16[2,4,2560]{2,1,0:T(4,128)(2,1)S(1)}, u32[]{:S(2)}, u32[]{:S(2)}) collective-permute-start(bf16[2,4,2560]{2,1,0:T(4,128)(2,1)S(1)} %get-tuple-element.109), channel_id=1, source_target_pairs={{0,4},{1,5},{2,6},{3,7},{4,0},{5,1},{6,2},{7,3},{8,12},{9,13},{10,... | collective-permute-start | bytes 122888 | tf_op jit(solution)/shard_map/ppermute | solution.py:366
  182.2 10.6 %collective-permute-start.23 = (bf16[2,4,2560]{2,1,0:T(4,128)(2,1)S(1)}, bf16[2,4,2560]{2,1,0:T(4,128)(2,1)S(1)}, u32[]{:S(2)}, u32[]{:S(2)}) collective-permute-start(bf16[2,4,2560]{2,1,0:T(4,128)(2,1)S(1)} %get-tuple-element.106), channel_id=1, source_target_pairs={{0,6},{1,7},{2,4},{3,5},{4,2},{5,3},{6,0},{7,1},{8,14},{9,15},{10,... | collective-permute-start | bytes 122888 | tf_op jit(solution)/shard_map/ppermute | solution.py:366
